TPU v7x, 32 devices: a whole 2x2x4 slice. The times are simulated.
32 devices in a mesh: dp: 8 (over z, x), mp: 4 (over y, core).
Axes of the slice: x: 2, y: 2, z: 4, core: 2. Of those that a mesh axis runs over, the one named last changes fastest.
Arguments:
- image: bfloat16 [16, 16, 64, 2048], P(None, 'mp', 'dp'), may hold values from -6 to 6
- text: bfloat16 [16, 1024, 768], P('dp'), may hold values from -6 to 6
- cotangent: bfloat16 [16, 1024, 768], P('dp'), may hold values from -6 to 6
- segments: int32 [16, 1024], P('dp'), may hold values from 0 to 3, never falling along the last dimension, each value on 1 to 512 neighbouring positions
- boxes: int32 [16, 2, 1024], P('dp'), may hold values from 0 to 31
- reduce_weight: float32 [2048, 512], P(('dp', 'mp')), may hold values from -0.125 to 0.125
- reduce_weight_rows: float32 [2048], P(('dp', 'mp')), may hold values from 163.84 to 1228.8
- reduce_weight_cols: float32 [512], replicated, may hold values from 163.84 to 1228.8
- spatial_weight: float32 [4608, 512], P(('dp', 'mp')), may hold values from -0.09375 to 0.09375
- spatial_weight_rows: float32 [4608], P(('dp', 'mp')), may hold values from 163.84 to 1228.8
- spatial_weight_cols: float32 [512], replicated, may hold values from 163.84 to 1228.8
- expand_weight: float32 [512, 2048], P(('dp', 'mp')), may hold values from -0.25 to 0.25
- expand_weight_rows: float32 [512], P(('dp', 'mp')), may hold values from 163.84 to 1228.8
- expand_weight_cols: float32 [2048], replicated, may hold values from 163.84 to 1228.8
- visual_proj: float32 [2048, 768], P(('dp', 'mp')), may hold values from -0.125 to 0.125
- visual_proj_rows: float32 [2048], P(('dp', 'mp')), may hold values from 1638.4 to 12288
- visual_proj_cols: float32 [768], replicated, may hold values from 1638.4 to 12288
- attn_in: float32 [2, 3, 768, 768], P(None, None, 'dp', 'mp'), may hold values from -0.21875 to 0.21875
- attn_in_rows: float32 [2, 3, 768], P(None, None, 'dp'), may hold values from 491.52 to 3686.4
- attn_in_cols: float32 [2, 3, 768], P(None, None, 'mp'), may hold values from 491.52 to 3686.4
- attn_out: float32 [2, 768, 768], P(None, 'mp', 'dp'), may hold values from -1.25 to 1.25
- attn_out_rows: float32 [2, 768], P(None, 'mp'), may hold values from 32.768 to 245.76
- attn_out_cols: float32 [2, 768], P(None, 'dp'), may hold values from 32.768 to 245.76
- ffn_up: float32 [768, 3072], P('dp', 'mp'), may hold values from -0.21875 to 0.21875
- ffn_up_rows: float32 [768], P('dp'), may hold values from 819.2 to 6144
- ffn_up_cols: float32 [3072], P('mp'), may hold values from 819.2 to 6144
- ffn_down: float32 [3072, 768], P('mp', 'dp'), may hold values from -0.109375 to 0.109375
- ffn_down_rows: float32 [3072], P('mp'), may hold values from 1310.72 to 9830.4
- ffn_down_cols: float32 [768], P('dp'), may hold values from 1310.72 to 9830.4
- norm_params: float32 [5, 768], replicated, may hold values from 0.1 to 1.9
- norm_moment: float32 [5, 768], replicated, may hold values from 3276.8 to 24576
- up_bias: float32 [3072], replicated, may hold values from -1.8 to 1.8
- up_moment: float32 [3072], replicated, may hold values from 819.2 to 6144
- tables: float32 [2, 33, 12], replicated, may hold values from -4 to 4
- table_moment: float32 [2, 33, 12], replicated, may hold values from 327.68 to 2457.6
Outputs:
- out: bfloat16 [16, 1024, 768], P('dp')
- grad_text: float32 [16, 1024, 768], P('dp', 'mp')
- grad_image: float32 [16, 16, 64, 2048], P(None, 'mp', 'dp')
- reduce_weight_grad: float32 [2048, 512], P(('dp', 'mp'))
- reduce_weight_next: float32 [2048, 512], P(('dp', 'mp'))
- reduce_weight_rows_next: float32 [2048], P(('dp', 'mp'))
- reduce_weight_cols_next: float32 [512], replicated
- reduce_weight_low: bfloat16 [2048, 512], P(('dp', 'mp'))
- spatial_weight_grad: float32 [4608, 512], P(('dp', 'mp'))
- spatial_weight_next: float32 [4608, 512], P(('dp', 'mp'))
- spatial_weight_rows_next: float32 [4608], P(('dp', 'mp'))
- spatial_weight_cols_next: float32 [512], replicated
- spatial_weight_low: bfloat16 [4608, 512], P(('dp', 'mp'))
- expand_weight_grad: float32 [512, 2048], P(('dp', 'mp'))
- expand_weight_next: float32 [512, 2048], P(('dp', 'mp'))
- expand_weight_rows_next: float32 [512], P(('dp', 'mp'))
- expand_weight_cols_next: float32 [2048], replicated
- expand_weight_low: bfloat16 [512, 2048], P(('dp', 'mp'))
- visual_proj_grad: float32 [2048, 768], P(('dp', 'mp'))
- visual_proj_next: float32 [2048, 768], P(('dp', 'mp'))
- visual_proj_rows_next: float32 [2048], P(('dp', 'mp'))
- visual_proj_cols_next: float32 [768], replicated
- visual_proj_low: bfloat16 [2048, 768], P(('dp', 'mp'))
- attn_in_grad: float32 [2, 3, 768, 768], P(None, None, 'dp', 'mp')
- attn_in_next: float32 [2, 3, 768, 768], P(None, None, 'dp', 'mp')
- attn_in_rows_next: float32 [2, 3, 768], P(None, None, 'dp')
- attn_in_cols_next: float32 [2, 3, 768], P(None, None, 'mp')
- attn_in_low: bfloat16 [2, 3, 768, 768], P(None, None, 'dp', 'mp')
- attn_out_grad: float32 [2, 768, 768], P(None, 'mp', 'dp')
- attn_out_next: float32 [2, 768, 768], P(None, 'mp', 'dp')
- attn_out_rows_next: float32 [2, 768], P(None, 'mp')
- attn_out_cols_next: float32 [2, 768], P(None, 'dp')
- attn_out_low: bfloat16 [2, 768, 768], P(None, 'mp', 'dp')
- ffn_up_grad: float32 [768, 3072], P('dp', 'mp')
- ffn_up_next: float32 [768, 3072], P('dp', 'mp')
- ffn_up_rows_next: float32 [768], P('dp')
- ffn_up_cols_next: float32 [3072], P('mp')
- ffn_up_low: bfloat16 [768, 3072], P('dp', 'mp')
- ffn_down_grad: float32 [3072, 768], P('mp', 'dp')
- ffn_down_next: float32 [3072, 768], P('mp', 'dp')
- ffn_down_rows_next: float32 [3072], P('mp')
- ffn_down_cols_next: float32 [768], P('dp')
- ffn_down_low: bfloat16 [3072, 768], P('mp', 'dp')
- norm_grad: float32 [5, 768], replicated
- norm_moment_next: float32 [5, 768], replicated
- norm_next: float32 [5, 768], replicated
- up_grad: float32 [3072], replicated
- up_moment_next: float32 [3072], replicated
- up_next: float32 [3072], replicated
- table_grad: float32 [2, 33, 12], replicated
- table_moment_next: float32 [2, 33, 12], replicated
- table_next: float32 [2, 33, 12], replicated
Inputs may be any that keep to these rules, and one draw needn't show every extreme that they name: `segments`: within a page the segment id never falls.
All inputs are finite; a program needn't handle non-finite values.
Results may differ from a plain program's by a relative error of at most 0.025.
Values may be sent and summed in bfloat16 or wider, within the bound.
No kernel may reach another device: no remote copies, remote signals or barrier semaphores. Data moves between devices by JAX's collectives and lax.ppermute only.
A program may use at most 256 MiB of HBM per device.

v0:
```python
import math

import jax
import jax.numpy as jnp
from jax import lax
from jax.sharding import PartitionSpec as P

MICRO = 2
NB = 32
STEP = 5


NEGATIVE = -1000000000.0
NORM_EPS = 1e-05
RELATIVE = 0.5
RATE_FLOOR = 0.001
PRECISE = lax.Precision.HIGHEST
FORWARD_TAPS = tuple(((shift_col, shift_row) for shift_col in range(3) for shift_row in range(3)))
BACKWARD_TAPS = tuple(
    ((2 - shift_col, 2 - shift_row) for shift_col in range(3) for shift_row in range(3))
)


def extended(cells, sides, width):
    for axis, dim in sides:
        count = lax.axis_size(axis)
        ends = count - 1
        head = lax.slice_in_dim(cells, 0, width, axis=dim)
        tail = lax.slice_in_dim(cells, cells.shape[dim] - width, cells.shape[dim], axis=dim)
        cells = jnp.concatenate(
            [
                lax.ppermute(tail, axis, [(i, (i + 1) % count) for i in range(ends)]),
                cells,
                lax.ppermute(head, axis, [((i + 1) % count, i) for i in range(ends)]),
            ],
            axis=dim,
        )
    return cells


def smooth(values):
    return jax.nn.gelu(values, approximate=True)


def smooth_back(values, upstream):
    return jax.vjp(smooth, values)[1](upstream)[0]


def layer_norm(values, norm_gain, norm_shift):
    centre = values - jnp.mean(values, axis=-1, keepdims=True)
    spread = jnp.mean(centre * centre, axis=-1, keepdims=True)
    return centre * lax.rsqrt(spread + NORM_EPS) * norm_gain + norm_shift


def relative_select(buckets, reach_max):
    offsets = (
        jnp.arange(buckets, dtype=jnp.int32)[None, :]
        - jnp.arange(buckets, dtype=jnp.int32)[:, None]
    )
    clipped = jnp.clip(offsets, -reach_max, reach_max) + reach_max
    return (
        clipped[:, :, None] == jnp.arange(2 * reach_max + 1, dtype=jnp.int32)[None, None, :]
    ).astype(jnp.float32)


def box_onehot(boxes_page, buckets):
    levels = jnp.arange(buckets, dtype=jnp.int32)[None, :]
    across_hot = (boxes_page[0][:, None] == levels).astype(jnp.float32)
    down_hot = (boxes_page[1][:, None] == levels).astype(jnp.float32)
    return jnp.concatenate([across_hot, down_hot], axis=1)


def bias_block(rows_hot, keys_low, span_tables, buckets):
    first_part = jnp.einsum("qa,hab->hqb", rows_hot[:, :buckets], span_tables[0], precision=PRECISE)
    second_part = jnp.einsum(
        "qa,hab->hqb", rows_hot[:, buckets:], span_tables[1], precision=PRECISE
    )
    joined = jnp.concatenate([first_part, second_part], axis=-1)
    upper = joined.astype(jnp.bfloat16)
    lower = (joined - upper.astype(jnp.float32)).astype(jnp.bfloat16)
    high_sum = jnp.einsum("hqc,kc->hqk", upper, keys_low, preferred_element_type=jnp.float32)
    return high_sum + jnp.einsum("hqc,kc->hqk", lower, keys_low, preferred_element_type=jnp.float32)


def stacked_taps(padded, across, downward, anchors):
    return jnp.concatenate(
        [
            padded[:, from_col : from_col + across, from_row : from_row + downward, :]
            for from_col, from_row in anchors
        ],
        axis=-1,
    )


def block_scores(query_block, key_rows, bias_rows, same_page):
    scaling = query_block.shape[-1] ** (-0.5)
    scores = (
        jnp.einsum("qhd,khd->hqk", query_block, key_rows, preferred_element_type=jnp.float32)
        * scaling
        + bias_rows
    )
    return jnp.where(same_page[None], scores, NEGATIVE)


def forward_page(projected, segment_row, onehot, span_tables):
    length = segment_row.shape[0]
    block_rows = min(512, length)
    buckets = onehot.shape[1] // 2
    onehot_low = onehot.astype(jnp.bfloat16)

    def forward_one_block(block_index):
        block_start = block_index * block_rows
        rows_hot = lax.dynamic_slice_in_dim(onehot, block_start, block_rows, 0)
        bias_rows = bias_block(rows_hot, onehot_low, span_tables, buckets)
        same_page = (
            lax.dynamic_slice_in_dim(segment_row, block_start, block_rows, 0)[:, None]
            == segment_row[None, :]
        )
        results = []
        log_parts = []
        for stream in range(2):
            query_block = lax.dynamic_slice_in_dim(projected[stream, 0], block_start, block_rows, 0)
            scores = block_scores(query_block, projected[stream, 1], bias_rows, same_page)
            row_max = jnp.max(scores, axis=-1, keepdims=True)
            exponent = jnp.exp(scores - row_max)
            totals = jnp.sum(exponent, axis=-1, keepdims=True)
            weights = (exponent / totals).astype(jnp.bfloat16)
            results.append(
                jnp.einsum(
                    "hqk,khd->qhd",
                    weights,
                    projected[stream, 2],
                    preferred_element_type=jnp.float32,
                ).astype(jnp.bfloat16)
            )
            log_parts.append(row_max[..., 0] + jnp.log(totals[..., 0]))
        return (jnp.stack(results), jnp.stack(log_parts))

    return lax.map(forward_one_block, jnp.arange(length // block_rows, dtype=jnp.int32))


def backward_page(projected, log_sums, grad_heads, segment_row, onehot, span_tables):
    length = segment_row.shape[0]
    block_rows = min(512, length)
    buckets = onehot.shape[1] // 2
    scaling = projected.shape[-1] ** (-0.5)
    onehot_low = onehot.astype(jnp.bfloat16)

    def backward_one_block(running, block_index):
        key_grads, span_grads = running
        block_start = block_index * block_rows
        rows_hot = lax.dynamic_slice_in_dim(onehot, block_start, block_rows, 0)
        bias_rows = bias_block(rows_hot, onehot_low, span_tables, buckets)
        same_page = (
            lax.dynamic_slice_in_dim(segment_row, block_start, block_rows, 0)[:, None]
            == segment_row[None, :]
        )
        query_grads = []
        for stream in range(2):
            query_block = lax.dynamic_slice_in_dim(projected[stream, 0], block_start, block_rows, 0)
            scores = block_scores(query_block, projected[stream, 1], bias_rows, same_page)
            probs = jnp.exp(scores - log_sums[block_index, stream][..., None])
            out_block = lax.dynamic_slice_in_dim(grad_heads[stream], block_start, block_rows, 0)
            prob_grad = jnp.einsum(
                "qhd,khd->hqk", out_block, projected[stream, 2], preferred_element_type=jnp.float32
            )
            score_grad = probs * (prob_grad - jnp.sum(probs * prob_grad, axis=-1, keepdims=True))
            score_low = score_grad.astype(jnp.bfloat16)
            query_grads.append(
                (
                    jnp.einsum(
                        "hqk,khd->qhd",
                        score_low,
                        projected[stream, 1],
                        preferred_element_type=jnp.float32,
                    )
                    * scaling
                ).astype(jnp.bfloat16)
            )
            key_add = (
                jnp.einsum(
                    "hqk,qhd->khd", score_low, query_block, preferred_element_type=jnp.float32
                )
                * scaling
            )
            value_add = jnp.einsum(
                "hqk,qhd->khd",
                probs.astype(jnp.bfloat16),
                out_block,
                preferred_element_type=jnp.float32,
            )
            key_grads = key_grads.at[stream].add(jnp.stack([key_add, value_add]))
            through = jnp.einsum(
                "hqk,kc->hqc", score_low, onehot_low, preferred_element_type=jnp.float32
            )
            span_first = jnp.einsum(
                "qa,hqb->hab", rows_hot[:, :buckets], through[..., :buckets], precision=PRECISE
            )
            span_second = jnp.einsum(
                "qa,hqb->hab", rows_hot[:, buckets:], through[..., buckets:], precision=PRECISE
            )
            span_grads = span_grads + jnp.stack([span_first, span_second])
        return ((key_grads, span_grads), jnp.stack(query_grads))

    start_keys = jnp.zeros((2, 2) + projected.shape[2:], jnp.float32)
    start_spans = jnp.zeros(span_tables.shape, jnp.float32)
    (key_grads, span_grads), query_parts = lax.scan(
        backward_one_block,
        (start_keys, start_spans),
        jnp.arange(length // block_rows, dtype=jnp.int32),
    )
    query_full = query_parts.transpose(1, 0, 2, 3, 4).reshape((2,) + projected.shape[2:])
    joined = jnp.concatenate([query_full[:, None], key_grads.astype(jnp.bfloat16)], axis=1)
    return (joined, span_grads)


def fetch_image(reduce_part, spatial_part, expand_part, proj_part):
    return (
        lax.all_gather(reduce_part, ("dp", "mp"), axis=0, tiled=True),
        lax.all_gather(spatial_part, ("dp", "mp"), axis=0, tiled=True),
        lax.all_gather(expand_part, ("dp", "mp"), axis=0, tiled=True),
        lax.all_gather(proj_part, ("dp", "mp"), axis=0, tiled=True),
    )


def fetch_layer(in_part, out_part, up_part, down_part):
    return (
        lax.all_gather(in_part, "dp", axis=2, tiled=True),
        lax.all_gather(out_part, "dp", axis=2, tiled=True),
        lax.all_gather(up_part, "dp", axis=0, tiled=True),
        lax.all_gather(down_part, "dp", axis=1, tiled=True),
    )


def reduce_image(reduce_part, spatial_part, expand_part, proj_part):
    return (
        lax.psum_scatter(reduce_part, ("dp", "mp"), scatter_dimension=0, tiled=True),
        lax.psum_scatter(spatial_part, ("dp", "mp"), scatter_dimension=0, tiled=True),
        lax.psum_scatter(expand_part, ("dp", "mp"), scatter_dimension=0, tiled=True),
        lax.psum_scatter(proj_part, ("dp", "mp"), scatter_dimension=0, tiled=True),
    )


def reduce_layer(in_part, out_part, up_part, down_part):
    return (
        lax.psum_scatter(in_part, "dp", scatter_dimension=2, tiled=True),
        lax.psum_scatter(out_part, "dp", scatter_dimension=2, tiled=True),
        lax.psum_scatter(up_part, "dp", scatter_dimension=0, tiled=True),
        lax.psum_scatter(down_part, "dp", scatter_dimension=1, tiled=True),
    )


def embed_last(values_in, offset, total_len):
    full_shape = values_in.shape[:-1] + (total_len,)
    return lax.dynamic_update_slice_in_dim(
        jnp.zeros(full_shape, jnp.float32), values_in, offset, values_in.ndim - 1
    )


def stat_terms(
    gradient, weight, rows_old, row_offset, row_total, col_offset, col_total, row_weight
):
    squares = gradient * gradient
    row_sums = embed_last(jnp.sum(squares, axis=-1), row_offset, row_total)
    col_sums = embed_last(jnp.sum(squares, axis=-2), col_offset, col_total)
    return (
        row_sums,
        col_sums,
        jnp.sum(rows_old, axis=-1) * row_weight,
        jnp.sum(weight * weight, axis=(-2, -1)),
    )


def factored_step(
    weight,
    gradient,
    rows_old,
    cols_old,
    row_sums,
    col_sums,
    old_total,
    weight_squares,
    row_offset,
    col_offset,
):
    decay_rate = 1.0 - STEP ** (-0.8)
    row_total = row_sums.shape[-1]
    col_total = col_sums.shape[-1]
    row_piece = lax.dynamic_slice_in_dim(row_sums, row_offset, weight.shape[-2], row_sums.ndim - 1)
    col_piece = lax.dynamic_slice_in_dim(col_sums, col_offset, weight.shape[-1], col_sums.ndim - 1)
    rows_next = decay_rate * rows_old + (1.0 - decay_rate) * row_piece / col_total
    cols_next = decay_rate * cols_old + (1.0 - decay_rate) * col_piece / row_total
    row_mean = (
        decay_rate * old_total + (1.0 - decay_rate) * jnp.sum(row_sums, axis=-1) / col_total
    ) / row_total
    second = rows_next[..., :, None] * cols_next[..., None, :] / row_mean[..., None, None]
    step_rate = RELATIVE * jnp.maximum(
        RATE_FLOOR, jnp.sqrt(weight_squares / (row_total * col_total))
    )
    weight_next = weight - step_rate[..., None, None] * (gradient * lax.rsqrt(second))
    return (gradient, weight_next, rows_next, cols_next, weight_next.astype(jnp.bfloat16))


def moment_step(parameter, gradient, moment, reduce_axes):
    decay_rate = 1.0 - STEP ** (-0.8)
    moment_next = decay_rate * moment + (1.0 - decay_rate) * gradient * gradient
    rms_value = jnp.sqrt(jnp.mean(parameter * parameter, axis=reduce_axes, keepdims=True))
    return (
        gradient,
        moment_next,
        parameter
        - RELATIVE * jnp.maximum(RATE_FLOOR, rms_value) * gradient * lax.rsqrt(moment_next),
    )


def on_device(
    image,
    text,
    cotangent,
    segments,
    boxes,
    reduce_weight,
    reduce_weight_rows,
    reduce_weight_cols,
    spatial_weight,
    spatial_weight_rows,
    spatial_weight_cols,
    expand_weight,
    expand_weight_rows,
    expand_weight_cols,
    visual_proj,
    visual_proj_rows,
    visual_proj_cols,
    attn_in,
    attn_in_rows,
    attn_in_cols,
    attn_out,
    attn_out_rows,
    attn_out_cols,
    ffn_up,
    ffn_up_rows,
    ffn_up_cols,
    ffn_down,
    ffn_down_rows,
    ffn_down_cols,
    norm_params,
    norm_moment,
    up_bias,
    up_moment,
    tables,
    table_moment,
):
    dp_count = lax.axis_size("dp")
    mp_count = lax.axis_size("mp")
    dp_index = lax.axis_index("dp")
    mp_index = lax.axis_index("mp")
    flat_index = lax.axis_index(("dp", "mp"))
    pages_dev, length, model_width = text.shape
    per_micro = pages_dev // MICRO
    token_count = per_micro * length
    head_count = tables.shape[2]
    local_heads = head_count // mp_count
    head_size = model_width // head_count
    local_width = attn_in.shape[3]
    local_hidden = ffn_up.shape[1]
    hidden_total = local_hidden * mp_count
    across_local = image.shape[1]
    down_local = image.shape[2]
    grid_cols = across_local * mp_count
    grid_rows = down_local * dp_count
    channels_mid = spatial_weight.shape[1]
    bucket_select = relative_select(NB, (tables.shape[1] - 1) // 2)
    local_tables = lax.dynamic_slice_in_dim(tables, mp_index * local_heads, local_heads, 2)
    span_tables = jnp.einsum("abr,trh->thab", bucket_select, local_tables, precision=PRECISE)
    local_up = lax.dynamic_slice_in_dim(up_bias, mp_index * local_hidden, local_hidden, 0)
    image_low = (
        reduce_weight.astype(jnp.bfloat16),
        spatial_weight.astype(jnp.bfloat16),
        expand_weight.astype(jnp.bfloat16),
        visual_proj.astype(jnp.bfloat16),
    )
    layer_low = (
        attn_in.astype(jnp.bfloat16),
        attn_out.astype(jnp.bfloat16),
        ffn_up.astype(jnp.bfloat16),
        ffn_down.astype(jnp.bfloat16),
    )
    image_total = tuple(
        (
            jnp.zeros(matrix.shape, jnp.float32)
            for matrix in (reduce_weight, spatial_weight, expand_weight, visual_proj)
        )
    )
    layer_total = tuple(
        (jnp.zeros(matrix.shape, jnp.float32) for matrix in (attn_in, attn_out, ffn_up, ffn_down))
    )
    norm_total = jnp.zeros(norm_params.shape, jnp.float32)
    up_total = jnp.zeros((local_hidden,), jnp.float32)
    span_total = jnp.zeros(span_tables.shape, jnp.float32)
    out_pieces = []
    text_pieces = []
    image_pieces = []
    for micro_step in range(MICRO):
        weight_reduce, weight_spatial, weight_expand, weight_proj = fetch_image(
            image_low[0], image_low[1], image_low[2], image_low[3]
        )
        weight_in, weight_out, weight_up, weight_down = fetch_layer(
            layer_low[0], layer_low[1], layer_low[2], layer_low[3]
        )
        page_first = micro_step * per_micro
        page_last = page_first + per_micro
        pictures = image.reshape((dp_count, pages_dev) + image.shape[1:])[
            :, page_first:page_last
        ].reshape((dp_count * per_micro,) + image.shape[1:])
        reduced = jnp.einsum(
            "pwhc,cd->pwhd", pictures, weight_reduce, preferred_element_type=jnp.float32
        )
        hidden_one = smooth(reduced).astype(jnp.bfloat16)
        padded = extended(hidden_one, (("dp", 2), ("mp", 1)), 1)
        tap_stack = stacked_taps(padded, across_local, down_local, FORWARD_TAPS)
        convolved = jnp.einsum(
            "pwhk,kd->pwhd", tap_stack, weight_spatial, preferred_element_type=jnp.float32
        )
        hidden_two = smooth(convolved).astype(jnp.bfloat16)
        expanded = jnp.einsum(
            "pwhc,cd->pwhd", hidden_two, weight_expand, preferred_element_type=jnp.float32
        )
        summed_pre = pictures.astype(jnp.float32) + expanded
        feature_low = smooth(summed_pre).astype(jnp.bfloat16)
        visual_rows = jnp.einsum(
            "pwhc,cd->pwhd", feature_low, weight_proj, preferred_element_type=jnp.float32
        ).astype(jnp.bfloat16)
        visual_part = lax.all_to_all(visual_rows, "dp", split_axis=0, concat_axis=2, tiled=True)
        visual_grid = lax.all_gather(visual_part, "mp", axis=1, tiled=True)
        visual_tokens = visual_grid.reshape(token_count, model_width)
        text_tokens = text[page_first:page_last].reshape(token_count, model_width)
        page_segments = segments[page_first:page_last]
        onehots = jax.vmap(box_onehot, in_axes=(0, None))(boxes[page_first:page_last], NB)
        sources = jnp.stack([text_tokens, visual_tokens])
        projected = jnp.einsum(
            "std,skdc->sktc", sources, weight_in, preferred_element_type=jnp.float32
        ).astype(jnp.bfloat16)
        projected = projected.reshape(2, 3, per_micro, length, local_heads, head_size).transpose(
            2, 0, 1, 3, 4, 5
        )

        def page_forward(page_items):
            return forward_page(page_items[0], page_items[1], page_items[2], span_tables)

        head_outputs, log_sums = lax.map(page_forward, (projected, page_segments, onehots))
        attended = head_outputs.transpose(2, 0, 1, 3, 4, 5).reshape(2, token_count, local_width)
        partial_heads = jnp.einsum(
            "stc,scd->td", attended, weight_out, preferred_element_type=jnp.float32
        )
        attention = lax.psum(partial_heads.astype(jnp.bfloat16), "mp").astype(jnp.float32)
        first_sum = text_tokens.astype(jnp.float32) + visual_tokens.astype(jnp.float32) + attention
        normed, first_pull = jax.vjp(layer_norm, first_sum, norm_params[0], norm_params[1])
        normed_low = normed.astype(jnp.bfloat16)
        hidden_pre = jnp.dot(normed_low, weight_up, preferred_element_type=jnp.float32) + local_up
        hidden_low = smooth(hidden_pre).astype(jnp.bfloat16)
        down_part = jnp.dot(hidden_low, weight_down, preferred_element_type=jnp.float32)
        second_sum = normed + (
            lax.psum(down_part.astype(jnp.bfloat16), "mp").astype(jnp.float32) + norm_params[4]
        )
        final_out, second_pull = jax.vjp(layer_norm, second_sum, norm_params[2], norm_params[3])
        out_pieces.append(final_out.astype(jnp.bfloat16).reshape(per_micro, length, model_width))
        upstream = (
            cotangent[page_first:page_last].reshape(token_count, model_width).astype(jnp.float32)
        )
        second_grad, gain_two, shift_two = second_pull(upstream)
        down_low = second_grad.astype(jnp.bfloat16)
        down_bias_grad = jnp.sum(down_low.astype(jnp.float32), axis=0)
        grad_down = jnp.einsum(
            "tf,td->fd", hidden_low, down_low, preferred_element_type=jnp.float32
        )
        hidden_grad = smooth_back(
            hidden_pre,
            jnp.einsum("td,fd->tf", down_low, weight_down, preferred_element_type=jnp.float32),
        )
        hidden_grad_low = hidden_grad.astype(jnp.bfloat16)
        up_total = up_total + jnp.sum(hidden_grad_low.astype(jnp.float32), axis=0)
        grad_up = jnp.einsum(
            "td,tf->df", normed_low, hidden_grad_low, preferred_element_type=jnp.float32
        )
        normed_part = jnp.einsum(
            "tf,df->td", hidden_grad_low, weight_up, preferred_element_type=jnp.float32
        )
        normed_grad = second_grad + lax.psum(normed_part.astype(jnp.bfloat16), "mp").astype(
            jnp.float32
        )
        first_grad, gain_one, shift_one = first_pull(normed_grad)
        norm_total = norm_total + jnp.stack(
            [gain_one, shift_one, gain_two, shift_two, down_bias_grad]
        )
        attention_low = first_grad.astype(jnp.bfloat16)
        grad_out = jnp.einsum(
            "stc,td->scd", attended, attention_low, preferred_element_type=jnp.float32
        )
        head_grads = jnp.einsum(
            "td,scd->stc", attention_low, weight_out, preferred_element_type=jnp.float32
        ).astype(jnp.bfloat16)
        head_grads = head_grads.reshape(2, per_micro, length, local_heads, head_size).transpose(
            1, 0, 2, 3, 4
        )

        def page_backward(page_items):
            return backward_page(
                page_items[0],
                page_items[1],
                page_items[2],
                page_items[3],
                page_items[4],
                span_tables,
            )

        projected_grads, span_grads = lax.map(
            page_backward, (projected, log_sums, head_grads, page_segments, onehots)
        )
        span_total = span_total + jnp.sum(span_grads, axis=0)
        projected_grads = projected_grads.transpose(1, 2, 0, 3, 4, 5).reshape(
            2, 3, token_count, local_width
        )
        grad_in = jnp.einsum(
            "std,sktc->skdc", sources, projected_grads, preferred_element_type=jnp.float32
        )
        source_grads = jnp.einsum(
            "sktc,skdc->std", projected_grads, weight_in, preferred_element_type=jnp.float32
        )
        text_grid = source_grads[0].reshape(per_micro, grid_cols, grid_rows, model_width)
        visual_grid_grad = source_grads[1].reshape(per_micro, grid_cols, grid_rows, model_width)
        text_back, visual_back = (
            lax.psum_scatter(
                text_grid.astype(jnp.bfloat16), "mp", scatter_dimension=1, tiled=True
            ).astype(jnp.float32),
            lax.psum_scatter(
                visual_grid_grad.astype(jnp.bfloat16), "mp", scatter_dimension=1, tiled=True
            ).astype(jnp.float32),
        )
        residual_part = lax.dynamic_slice_in_dim(
            first_grad.reshape(per_micro, grid_cols, grid_rows, model_width),
            mp_index * across_local,
            across_local,
            1,
        )
        text_pieces.append(
            (text_back + residual_part).reshape(per_micro, across_local * grid_rows, model_width)
        )
        visual_low = (visual_back + residual_part).astype(jnp.bfloat16)
        visual_rows_grad = lax.all_to_all(visual_low, "dp", split_axis=2, concat_axis=0, tiled=True)
        grad_proj = jnp.einsum(
            "pwhc,pwhd->cd", feature_low, visual_rows_grad, preferred_element_type=jnp.float32
        )
        feature_grad = jnp.einsum(
            "pwhd,cd->pwhc", visual_rows_grad, weight_proj, preferred_element_type=jnp.float32
        )
        pre_grad = smooth_back(summed_pre, feature_grad)
        expanded_low = pre_grad.astype(jnp.bfloat16)
        grad_expand = jnp.einsum(
            "pwhc,pwhd->cd", hidden_two, expanded_low, preferred_element_type=jnp.float32
        )
        conv_grad = smooth_back(
            convolved,
            jnp.einsum(
                "pwhd,cd->pwhc", expanded_low, weight_expand, preferred_element_type=jnp.float32
            ),
        ).astype(jnp.bfloat16)
        grad_spatial = jnp.einsum(
            "pwhk,pwhd->kd", tap_stack, conv_grad, preferred_element_type=jnp.float32
        )
        back_padded = extended(conv_grad, (("dp", 2), ("mp", 1)), 1)
        back_taps = stacked_taps(back_padded, across_local, down_local, BACKWARD_TAPS).reshape(
            conv_grad.shape[:3] + (9, channels_mid)
        )
        spatial_taps = weight_spatial.reshape(9, channels_mid, channels_mid)
        reduced_grad = smooth_back(
            reduced,
            jnp.einsum(
                "pwhko,kio->pwhi", back_taps, spatial_taps, preferred_element_type=jnp.float32
            ),
        ).astype(jnp.bfloat16)
        grad_reduce = jnp.einsum(
            "pwhc,pwhd->cd", pictures, reduced_grad, preferred_element_type=jnp.float32
        )
        image_grad = pre_grad + jnp.einsum(
            "pwhd,cd->pwhc", reduced_grad, weight_reduce, preferred_element_type=jnp.float32
        )
        image_pieces.append(image_grad.reshape((dp_count, per_micro) + image.shape[1:]))
        image_sums = reduce_image(grad_reduce, grad_spatial, grad_expand, grad_proj)
        layer_sums = reduce_layer(grad_in, grad_out, grad_up, grad_down)
        image_total = tuple((held + added for held, added in zip(image_total, image_sums)))
        layer_total = tuple((held + added for held, added in zip(layer_total, layer_sums)))
    dp_first = (dp_index == 0).astype(jnp.float32)
    mp_first = (mp_index == 0).astype(jnp.float32)
    image_sets = (
        (reduce_weight, reduce_weight_rows, reduce_weight_cols),
        (spatial_weight, spatial_weight_rows, spatial_weight_cols),
        (expand_weight, expand_weight_rows, expand_weight_cols),
        (visual_proj, visual_proj_rows, visual_proj_cols),
    )
    specs = []
    for position, (weight, rows_old, cols_old) in enumerate(image_sets):
        specs.append(
            (
                image_total[position],
                weight,
                rows_old,
                cols_old,
                flat_index * weight.shape[0],
                weight.shape[0] * dp_count * mp_count,
                0,
                weight.shape[1],
                1.0,
            )
        )
    specs.append(
        (
            layer_total[0],
            attn_in,
            attn_in_rows,
            attn_in_cols,
            dp_index * attn_in.shape[2],
            attn_in.shape[2] * dp_count,
            mp_index * attn_in.shape[3],
            attn_in.shape[3] * mp_count,
            mp_first,
        )
    )
    specs.append(
        (
            layer_total[1],
            attn_out,
            attn_out_rows,
            attn_out_cols,
            mp_index * attn_out.shape[1],
            attn_out.shape[1] * mp_count,
            dp_index * attn_out.shape[2],
            attn_out.shape[2] * dp_count,
            dp_first,
        )
    )
    specs.append(
        (
            layer_total[2],
            ffn_up,
            ffn_up_rows,
            ffn_up_cols,
            dp_index * ffn_up.shape[0],
            ffn_up.shape[0] * dp_count,
            mp_index * ffn_up.shape[1],
            ffn_up.shape[1] * mp_count,
            mp_first,
        )
    )
    specs.append(
        (
            layer_total[3],
            ffn_down,
            ffn_down_rows,
            ffn_down_cols,
            mp_index * ffn_down.shape[0],
            ffn_down.shape[0] * mp_count,
            dp_index * ffn_down.shape[1],
            ffn_down.shape[1] * dp_count,
            dp_first,
        )
    )
    flat_parts = []
    part_shapes = []
    for spec in specs:
        for term in stat_terms(
            spec[0], spec[1], spec[2], spec[4], spec[5], spec[6], spec[7], spec[8]
        ):
            flat_parts.append(term.reshape(-1))
            part_shapes.append(term.shape)
    flat_stats = jnp.concatenate(flat_parts)
    norm_term = norm_total * mp_first
    up_term = embed_last(up_total, mp_index * local_hidden, hidden_total)
    table_local = jnp.einsum("abr,thab->trh", bucket_select, span_total, precision=PRECISE)
    table_term = embed_last(table_local, mp_index * local_heads, head_count)
    summed_stats, norm_gradient, up_gradient, table_gradient = lax.psum(
        (flat_stats, norm_term, up_term, table_term), ("dp", "mp")
    )
    unpacked = []
    cursor = 0
    for part_shape in part_shapes:
        count_here = math.prod(part_shape)
        unpacked.append(summed_stats[cursor : cursor + count_here].reshape(part_shape))
        cursor = cursor + count_here
    results = []
    for spec_index, spec in enumerate(specs):
        found = unpacked[4 * spec_index : 4 * spec_index + 4]
        results.append(
            factored_step(
                spec[1],
                spec[0],
                spec[2],
                spec[3],
                found[0],
                found[1],
                found[2],
                found[3],
                spec[4],
                spec[6],
            )
        )
    norm_parts = moment_step(norm_params, norm_gradient, norm_moment, (1,))
    bias_parts = moment_step(up_bias, up_gradient, up_moment, (0,))
    table_parts = moment_step(tables, table_gradient, table_moment, (1, 2))
    out_local = jnp.concatenate(out_pieces, axis=0)
    text_grad_local = jnp.concatenate(text_pieces, axis=0)
    image_grad_local = jnp.concatenate(image_pieces, axis=1).reshape(image.shape)
    return (
        out_local,
        text_grad_local,
        image_grad_local,
        results[0][0],
        results[0][1],
        results[0][2],
        results[0][3],
        results[0][4],
        results[1][0],
        results[1][1],
        results[1][2],
        results[1][3],
        results[1][4],
        results[2][0],
        results[2][1],
        results[2][2],
        results[2][3],
        results[2][4],
        results[3][0],
        results[3][1],
        results[3][2],
        results[3][3],
        results[3][4],
        results[4][0],
        results[4][1],
        results[4][2],
        results[4][3],
        results[4][4],
        results[5][0],
        results[5][1],
        results[5][2],
        results[5][3],
        results[5][4],
        results[6][0],
        results[6][1],
        results[6][2],
        results[6][3],
        results[6][4],
        results[7][0],
        results[7][1],
        results[7][2],
        results[7][3],
        results[7][4],
        norm_parts[0],
        norm_parts[1],
        norm_parts[2],
        bias_parts[0],
        bias_parts[1],
        bias_parts[2],
        table_parts[0],
        table_parts[1],
        table_parts[2],
    )


def solution(mesh):
    placed = (
        P(None, "mp", "dp", None),
        P("dp", None, None),
        P("dp", None, None),
        P("dp", None),
        P("dp", None, None),
        P(("dp", "mp"), None),
        P(("dp", "mp")),
        P(),
        P(("dp", "mp"), None),
        P(("dp", "mp")),
        P(),
        P(("dp", "mp"), None),
        P(("dp", "mp")),
        P(),
        P(("dp", "mp"), None),
        P(("dp", "mp")),
        P(),
        P(None, None, "dp", "mp"),
        P(None, None, "dp"),
        P(None, None, "mp"),
        P(None, "mp", "dp"),
        P(None, "mp"),
        P(None, "dp"),
        P("dp", "mp"),
        P("dp"),
        P("mp"),
        P("mp", "dp"),
        P("mp"),
        P("dp"),
        P(),
        P(),
        P(),
        P(),
        P(),
        P(),
    )
    return jax.shard_map(
        on_device,
        mesh=mesh,
        in_specs=placed,
        out_specs=(
            P("dp", None, None),
            P("dp", "mp", None),
            P(None, "mp", "dp", None),
            P(("dp", "mp"), None),
            P(("dp", "mp"), None),
            P(("dp", "mp")),
            P(),
            P(("dp", "mp"), None),
            P(("dp", "mp"), None),
            P(("dp", "mp"), None),
            P(("dp", "mp")),
            P(),
            P(("dp", "mp"), None),
            P(("dp", "mp"), None),
            P(("dp", "mp"), None),
            P(("dp", "mp")),
            P(),
            P(("dp", "mp"), None),
            P(("dp", "mp"), None),
            P(("dp", "mp"), None),
            P(("dp", "mp")),
            P(),
            P(("dp", "mp"), None),
            P(None, None, "dp", "mp"),
            P(None, None, "dp", "mp"),
            P(None, None, "dp"),
            P(None, None, "mp"),
            P(None, None, "dp", "mp"),
            P(None, "mp", "dp"),
            P(None, "mp", "dp"),
            P(None, "mp"),
            P(None, "dp"),
            P(None, "mp", "dp"),
            P("dp", "mp"),
            P("dp", "mp"),
            P("dp"),
            P("mp"),
            P("dp", "mp"),
            P("mp", "dp"),
            P("mp", "dp"),
            P("mp"),
            P("dp"),
            P("mp", "dp"),
            P(),
            P(),
            P(),
            P(),
            P(),
            P(),
            P(),
            P(),
            P(),
        ),
        check_vma=False,
    )
```

profile of v0, /device:TPU:0, one launch (start us, length us, event | category | flops | bytes accessed | tf_op | source)
XLA Modules:
  0.0 2144.5 jit_solution(3450691591620435286)
XLA Ops:
  22.8 34.8 %all_gather.44 = bf16[2,192,768]{1,0,2:T(2,128)(2,1)S(1)} all-gather(bf16[2,192,96]{1,0,2:T(2,128)(2,1)S(1)} %copy.233), channel_id=1, replica_groups=mesh['dp'=8,'mp'=4] {'dp'}, dimensions={2}, use_global_device_ids=true | all-gather | bytes 663552 | tf_op jit(solution)/shard_map/all_gather | solution.py:229
  60.2 12.3 all-gather.10.cloned.1.call-done
  107.2 31.3 %all-gather.12.cloned.1.call-done = bf16[4608,512]{1,0:T(8,128)(2,1)} async-done(((bf16[144,512]{1,0:T(8,128)(2,1)}), bf16[4608,512]{1,0:T(8,128)(2,1)}) %all-gather.12.cloned.1.call-update) | async-done | bytes 4718608 | tf_op jit(solution)/shard_map/all_gather | solution.py:220
  142.9 54.2 %all-gather.14.cloned.1.call-done = bf16[512,2048]{1,0:T(8,128)(2,1)} async-done(((bf16[16,2048]{1,0:T(8,128)(2,1)}), bf16[512,2048]{1,0:T(8,128)(2,1)}) %all-gather.14.cloned.1.call-update) | async-done | bytes 2097168 | tf_op jit(solution)/shard_map/all_gather | solution.py:221
  201.1 57.3 %all-gather.16.cloned.1.call-done = bf16[2048,768]{1,0:T(8,128)(2,1)} async-done(((bf16[64,768]{1,0:T(8,128)(2,1)}), bf16[2048,768]{1,0:T(8,128)(2,1)}) %all-gather.16.cloned.1.call-update) | async-done | bytes 3145744 | tf_op jit(solution)/shard_map/all_gather | solution.py:222
  270.7 17.4 all-to-all-done
  308.1 16.1 all-gather.20.cloned.1.call-done
  330.8 13.5 all-gather.18.cloned.1.call-done
  349.6 35.2 %while.100 = (s32[]{:T(128)}, bf16[2,2,512,3,64]{2,4,3,1,0:T(8,128)(2,1)}, f32[2,2,3,512]{3,2,1,0:T(4,128)S(1)}, s32[2]{0:T(128)S(1)}, s32[1024]{0:T(1024)S(1)},...) while((s32[]{:T(128)}, ...), condition=%wide.region_5.6_spmd, body=%wide.region_0.5_spmd.sunk | while | flops 1279557632 | bytes 89876776 | solution.py:139
  394.7 35.8 %while.101 = (s32[]{:T(128)}, bf16[2,2,512,3,64]{2,4,3,1,0:T(8,128)(2,1)}, f32[2,2,3,512]{3,2,1,0:T(4,128)S(1)}, s32[2]{0:T(128)S(1)}, s32[1024]{0:T(1024)S(1)},...) while((s32[]{:T(128)}, ...), condition=%wide.region_17.18_spmd, body=%wide.region_12.17_spmd.sunk | while | flops 1279557632 | bytes 89876776 | solution.py:139
  446.4 65.2 %all-reduce.15.cloned.1.call-done = (bf16[1024,768]{1,0:T(8,128)(2,1)}, bf16[1024,768]{1,0:T(8,128)(2,1)}) async-done(((bf16[1024,768]{1,0:T(8,128)(2,1)}, bf16[1024,768]{1,0:T(8,128)(2,1)}), (bf16[1024,768]{1,0:T(8,128)(2,1)}, bf16[1024,768]{1,0:T(8,128)(2,1)})) %all-reduce.15.cloned.1.call-update) | async-done | bytes 3145744 | tf_op jit(solution)/shard_map/psum | solution.py:455
  520.6 34.9 %all-gather.22.cloned.1.call-done = bf16[768,768]{1,0:T(8,128)(2,1)} async-done(((bf16[96,768]{1,0:T(8,128)(2,1)}), bf16[768,768]{1,0:T(8,128)(2,1)}) %all-gather.22.cloned.1.call-update) | async-done | bytes 1179664 | tf_op jit(solution)/shard_map/all_gather | solution.py:230
  563.6 34.4 %all-gather.24.cloned.1.call-done = bf16[768,768]{0,1:T(8,128)(2,1)} async-done(((bf16[768,96]{0,1:T(8,128)(2,1)}), bf16[768,768]{0,1:T(8,128)(2,1)}) %all-gather.24.cloned.1.call-update) | async-done | bytes 1179664 | tf_op jit(solution)/shard_map/all_gather | solution.py:231
  607.0 67.5 %all-reduce.13.cloned.1.call-done = (bf16[1024,768]{1,0:T(8,128)(2,1)}, bf16[1024,768]{1,0:T(8,128)(2,1)}) async-done(((bf16[1024,768]{1,0:T(8,128)(2,1)}, bf16[1024,768]{1,0:T(8,128)(2,1)}), (bf16[1024,768]{1,0:T(8,128)(2,1)}, bf16[1024,768]{1,0:T(8,128)(2,1)})) %all-reduce.13.cloned.1.call-update) | async-done | bytes 3145744 | tf_op jit(solution)/shard_map/psum | solution.py:463
  695.0 6.9 convert_reduce_fusion.3
  707.1 68.8 %all-reduce.11.cloned.1.call-done = (bf16[1024,768]{1,0:T(8,128)(2,1)}, bf16[1024,768]{1,0:T(8,128)(2,1)}) async-done(((bf16[1024,768]{1,0:T(8,128)(2,1)}, bf16[1024,768]{1,0:T(8,128)(2,1)}), (bf16[1024,768]{1,0:T(8,128)(2,1)}, bf16[1024,768]{1,0:T(8,128)(2,1)})) %all-reduce.11.cloned.1.call-update) | async-done | bytes 3145744 | tf_op jit(solution)/shard_map/psum | solution.py:488
  776.0 8.1 multiply_reduce_fusion.5
  795.0 117.4 %while.102 = (s32[]{:T(128)}, f32[2,2,1024,3,64]{2,4,3,1,0:T(8,128)}, f32[2,3,32,32]{2,3,1,0:T(8,128)S(1)}, bf16[2,2,512,3,64]{2,4,3,1,0:T(8,128)(2,1)}, bf16[2,...) while((s32[]{:T(128)}, ...), condition=%wide.region_32.33_spmd.clone, body=%wide.region_29.32_spmd.clone.sunk | while | flops 2971003904 | bytes 218270400 | solution.py:207
  933.5 117.4 %while.103 = (s32[]{:T(128)}, f32[2,2,1024,3,64]{2,4,3,1,0:T(8,128)}, f32[2,3,32,32]{2,3,1,0:T(8,128)S(1)}, bf16[2,2,512,3,64]{2,4,3,1,0:T(8,128)(2,1)}, bf16[2,...) while((s32[]{:T(128)}, ...), condition=%wide.region_42.43_spmd.clone, body=%wide.region_39.42_spmd.clone.sunk | while | flops 2971003904 | bytes 218270400 | solution.py:207
  1100.1 7.0 copy.299
  1107.1 8.2 reshape.1328
  1127.4 8.2 all-to-all-done.2
  1145.4 11.1 all-to-all-done.3
  1246.5 43.9 %all-reduce = (f32[5,768]{1,0:T(8,128)S(1)}, f32[3072]{0:T(1024)S(1)}, f32[2,33,12]{1,0,2:T(2,128)S(1)}) all-reduce(f32[5,768]{1,0:T(8,128)S(1)} %add_multiply_fusion, f32[3072]{0:T(1024)S(1)} %add_dynamic-update-slice_fusion, f32[2,33,12]{1,0,2:T(2,128)S(1)} %copy_dynamic-update-slice_fusion), channel_id=1, replica_groups=mesh['dp'=8,'mp'=4] {'dp','mp'}, use_global_device_ids=true, to_apply=%region_113.114 | all-reduce | flops 7704 | bytes 61632 | tf_op jit(solution)/shard_map/psum | solution.py:680
  1295.9 42.2 %reduce-scatter.33.cloned.1.call-done = f32[96,768]{1,0:T(8,128)} async-done(((f32[768,768]{1,0:T(8,128)}), f32[96,768]{1,0:T(8,128)}) %reduce-scatter.33.cloned.1.call-update) | async-done | bytes 294928 | tf_op jit(solution)/shard_map/reduce_scatter | solution.py:248
  1347.9 72.0 %reduce-scatter.39.cloned.1.call-done = f32[96,1152]{1,0:T(8,128)} async-done(((f32[768,1152]{1,0:T(8,128)}), f32[96,1152]{1,0:T(8,128)}) %reduce-scatter.39.cloned.1.call-update) | async-done | bytes 442384
  1422.5 141.0 %reduce-scatter.29.cloned.1.call-done = f32[16,2048]{1,0:T(8,128)} async-done(((f32[512,2048]{1,0:T(8,128)}), f32[16,2048]{1,0:T(8,128)}) %reduce-scatter.29.cloned.1.call-update) | async-done | bytes 131088 | tf_op jit(solution)/shard_map/reduce_scatter | solution.py:239
  1564.8 115.4 %reduce-scatter.31.cloned.1.call-done = f32[64,768]{1,0:T(8,128)} async-done(((f32[2048,768]{1,0:T(8,128)}), f32[64,768]{1,0:T(8,128)}) %reduce-scatter.31.cloned.1.call-update) | async-done | bytes 196624 | tf_op jit(solution)/shard_map/reduce_scatter | solution.py:240
  1681.5 141.7 %reduce-scatter.37.cloned.1.call-done = f32[64,512]{1,0:T(8,128)} async-done(((f32[2048,512]{1,0:T(8,128)}), f32[64,512]{1,0:T(8,128)}) %reduce-scatter.37.cloned.1.call-update) | async-done | bytes 131088
  1824.7 137.2 %reduce-scatter.27.cloned.1.call-done = f32[144,512]{1,0:T(8,128)} async-done(((f32[4608,512]{1,0:T(8,128)}), f32[144,512]{1,0:T(8,128)}) %reduce-scatter.27.cloned.1.call-update) | async-done | bytes 294928 | tf_op jit(solution)/shard_map/reduce_scatter | solution.py:238
  1963.3 7.4 concatenate.195
  1976.7 113.6 %all-reduce.9.cloned.1.call-done = f32[33052]{0:T(1024)} async-done(((f32[33052]{0:T(1024)}), f32[33052]{0:T(1024)}) %all-reduce.9.cloned.1.call-update) | async-done | bytes 132224 | tf_op jit(solution)/shard_map/psum | solution.py:680
  (1064 shorter events, 725.7 us)
Async XLA Ops:
  7.2 65.3 %all-gather.10.cloned.1.call-start = ((), (), s32[]{:S(2)}) async-start(), calls=%async_computation.16 | async-start | bytes 2162688 | tf_op jit(solution)/shard_map/all_gather | solution.py:219
  9.5 128.9 %all-gather.12.cloned.1.call-start = ((), (), s32[]{:S(2)}) async-start(), calls=%async_computation.17 | async-start | bytes 4866048 | tf_op jit(solution)/shard_map/all_gather | solution.py:220
  11.9 185.2 %all-gather.14.cloned.1.call-start = ((), (), s32[]{:S(2)}) async-start(), calls=%async_computation.18 | async-start | bytes 2162688 | tf_op jit(solution)/shard_map/all_gather | solution.py:221
  14.2 244.2 %all-gather.16.cloned.1.call-start = ((), (), s32[]{:S(2)}) async-start(), calls=%async_computation.19 | async-start | bytes 3244032 | tf_op jit(solution)/shard_map/all_gather | solution.py:222
  16.6 307.7 %all-gather.20.cloned.1.call-start = ((), (), s32[]{:S(2)}) async-start(), calls=%async_computation.21 | async-start | bytes 2654208 | tf_op jit(solution)/shard_map/all_gather | solution.py:228
  76.2 12.2 collective-permute-start.4
  263.0 25.1 %all-to-all-start = ((bf16[8,4,8,768]{3,2,1,0:T(8,128)(2,1)}), bf16[8,4,8,768]{3,2,1,0:T(8,128)(2,1)S(1)}, u32[]{:S(2)}, u32[]{:S(2)}) async-start(bf16[8,4,8,768]{3,2,1,0:T(8,128)(2,1)} %fusion.354), calls=%async_computation | async-start | bytes 786432 | tf_op jit(solution)/shard_map/all_to_all | solution.py:433
  267.3 77.0 %all-gather.18.cloned.1.call-start = ((), (), s32[]{:S(2)}) async-start(), calls=%async_computation.20 | async-start | bytes 1966080 | tf_op jit(solution)/shard_map/all_gather | solution.py:434
  299.3 30.6 %all-to-all-start.1 = ((bf16[8,4,8,768]{3,2,1,0:T(8,128)(2,1)}), bf16[8,4,8,768]{3,2,1,0:T(8,128)(2,1)S(1)}, u32[]{:S(2)}, u32[]{:S(2)}) async-start(bf16[8,4,8,768]{3,2,1,0:T(8,128)(2,1)} %fusion.357), calls=%async_computation.1 | async-start | bytes 786432 | tf_op jit(solution)/shard_map/all_to_all | solution.py:433
  302.9 85.9 %all-gather.26.cloned.1.call-start = ((), (), s32[]{:S(2)}) async-start(), calls=%async_computation.24 | async-start | bytes 1966080 | tf_op jit(solution)/shard_map/all_gather | solution.py:434
  330.8 180.8 %all-reduce.15.cloned.1.call-start = ((), (), s32[]{:S(2)}) async-start(), calls=%async_computation.40 | async-start | bytes 6291456 | tf_op jit(solution)/shard_map/psum | solution.py:455
  442.8 112.7 %all-gather.22.cloned.1.call-start = ((), (), s32[]{:S(2)}) async-start(), calls=%async_computation.22 | async-start | bytes 1327104 | tf_op jit(solution)/shard_map/all_gather | solution.py:230
  444.2 153.8 %all-gather.24.cloned.1.call-start = ((), (), s32[]{:S(2)}) async-start(), calls=%async_computation.23 | async-start | bytes 1327104 | tf_op jit(solution)/shard_map/all_gather | solution.py:231
  445.5 229.0 %all-reduce.13.cloned.1.call-start = ((), (), s32[]{:S(2)}) async-start(), calls=%async_computation.39 | async-start | bytes 6291456 | tf_op jit(solution)/shard_map/psum | solution.py:463
  607.0 169.0 %all-reduce.11.cloned.1.call-start = ((), (), s32[]{:S(2)}) async-start(), calls=%async_computation.38 | async-start | bytes 6291456 | tf_op jit(solution)/shard_map/psum | solution.py:488
  707.1 408.2 %reduce-scatter.19.cloned.1.call-start = ((), (), s32[]{:S(2)}) async-start(), calls=%async_computation.25 | async-start | bytes 1966080 | tf_op jit(solution)/shard_map/reduce_scatter | solution.py:532
  925.6 189.7 %reduce-scatter.23.cloned.1.call-start = ((), (), s32[]{:S(2)}) async-start(), calls=%async_computation.27 | async-start | bytes 1966080 | tf_op jit(solution)/shard_map/reduce_scatter | solution.py:535
  930.5 193.5 %reduce-scatter.21.cloned.1.call-start = ((), (), s32[]{:S(2)}) async-start(), calls=%async_computation.26 | async-start | bytes 1966080 | tf_op jit(solution)/shard_map/reduce_scatter | solution.py:532
  1064.3 59.7 %reduce-scatter.25.cloned.1.call-start = ((), (), s32[]{:S(2)}) async-start(), calls=%async_computation.28 | async-start | bytes 1966080 | tf_op jit(solution)/shard_map/reduce_scatter | solution.py:535
  1064.8 227.6 %reduce-scatter.41.cloned.1.call-start = ((), (), s32[]{:S(2)}) async-start(), calls=%async_computation.37 | async-start | bytes 1327104
  1076.8 217.4 %reduce-scatter.35.cloned.1.call-start = ((), (), s32[]{:S(2)}) async-start(), calls=%async_computation.34 | async-start | bytes 2654208 | tf_op jit(solution)/shard_map/reduce_scatter | solution.py:249
  1084.8 253.3 %reduce-scatter.33.cloned.1.call-start = ((), (), s32[]{:S(2)}) async-start(), calls=%async_computation.33 | async-start | bytes 2654208 | tf_op jit(solution)/shard_map/reduce_scatter | solution.py:248
  1091.5 328.3 %reduce-scatter.39.cloned.1.call-start = ((), (), s32[]{:S(2)}) async-start(), calls=%async_computation.36 | async-start | bytes 3981312
  1118.5 17.1 all-to-all-start.2
  1135.6 20.9 all-to-all-start.3
  1139.2 424.3 %reduce-scatter.29.cloned.1.call-start = ((), (), s32[]{:S(2)}) async-start(), calls=%async_computation.31 | async-start | bytes 4325376 | tf_op jit(solution)/shard_map/reduce_scatter | solution.py:239
  1165.5 514.7 %reduce-scatter.31.cloned.1.call-start = ((), (), s32[]{:S(2)}) async-start(), calls=%async_computation.32 | async-start | bytes 6488064 | tf_op jit(solution)/shard_map/reduce_scatter | solution.py:240
  1169.0 20.0 collective-permute-start.8
  1172.0 17.0 collective-permute-start.9
  1186.2 637.0 %reduce-scatter.37.cloned.1.call-start = ((), (), s32[]{:S(2)}) async-start(), calls=%async_computation.35 | async-start | bytes 4325376
  1215.7 746.2 %reduce-scatter.27.cloned.1.call-start = ((), (), s32[]{:S(2)}) async-start(), calls=%async_computation.30 | async-start | bytes 9732096 | tf_op jit(solution)/shard_map/reduce_scatter | solution.py:238
  1224.3 865.9 %all-reduce.9.cloned.1.call-start = ((), (), s32[]{:S(2)}) async-start(), calls=%async_computation.29 | async-start | bytes 270336 | tf_op jit(solution)/shard_map/psum | solution.py:680
  (235 other events, 5722.2 us)
Sparse Core Ops, SparseCore 0:
  11.5 60.9 all-gather.9
  76.0 62.4 all-gather.11
  141.9 55.1 all-gather.13
  200.5 57.8 all-gather.15
  261.0 63.2 all-gather.19
  325.7 18.5 all-gather.17
  346.4 19.6 all-gather.25
  442.9 68.6 all-reduce.14
  514.4 41.1 all-gather.21
  558.1 39.8 all-gather.23
  607.1 67.4 all-reduce.12
  707.2 68.7 all-reduce.10
  925.7 28.2 reduce-scatter.18
  956.6 28.1 reduce-scatter.22
  1064.4 28.4 reduce-scatter.20
  1095.4 28.1 reduce-scatter.24
  1126.8 67.2 reduce-scatter.40
  1198.0 67.8 reduce-scatter.34
  1270.0 68.0 reduce-scatter.32
  1341.6 78.1 reduce-scatter.38
  1422.7 140.7 reduce-scatter.28
  1569.7 110.3 reduce-scatter.30
  1683.1 140.0 reduce-scatter.36
  1830.6 131.3 reduce-scatter.26
  1970.9 119.3 all-reduce.8
where the time goes:
time: 2160 us; the launch traced here: 2140 us
  waiting for transfers between devices  1260 us (58%)
  matrix products  373 us (17%)
  local copies, waits for them, and re-layouts  168 us (8%)
  other arithmetic  162 us (8%)
  blocking collectives  78.7 us (4%)
  starting transfers between devices  57.1 us (3%)
  between operations  31.1 us (1%)
    unnamed x28, waiting for transfers between devices  215 us
    reduce_scatter x1, waiting for transfers between devices, reduce_image(): lax.psum_scatter(expand_part, ('dp', 'mp'), scatter_dimension=0, tiled=True)  141 us
    reduce_scatter x1, waiting for transfers between devices, reduce_image(): lax.psum_scatter(spatial_part, ('dp', 'mp'), scatter_dimension=0, tiled=T...  137 us
    reduce_scatter x1, waiting for transfers between devices, reduce_image(): lax.psum_scatter(proj_part, ('dp', 'mp'), scatter_dimension=0, tiled=True)  115 us
    psum x1, waiting for transfers between devices, on_device(): lax.psum((flat_stats, norm_term, up_term, table_term), ('dp', 'mp'))  114 us
    dot_general x16, matrix products, block_scores(): jnp.einsum('qhd,khd->hqk', query_block, key_rows, preferred_element_type=...  72.8 us
    unnamed x369, local copies, waits for them, and re-layouts  69.4 us
    psum x1, waiting for transfers between devices, on_device(): lax.psum(normed_part.astype(jnp.bfloat16), 'mp').astype(jnp.float32)  68.8 us
  transfers between devices with their start and end apart: 45, of which 24 were waited for; matrix products, arithmetic and copies ran while one was open for 19% of the time, Pallas kernels for 0%

commit v1 on v0

v1 whole, which is shorter than its diff:
```python
import functools

import jax
import jax.numpy as jnp
from jax import lax
from jax.experimental import pallas as pl
from jax.experimental.pallas import tpu as pltpu
from jax.sharding import Mesh
from jax.sharding import PartitionSpec as P

NB = 32
STEP = 5
NEGATIVE = -1000000000.0
SAFE = 2.0e8
NT = (((1,), (1,)), ((), ()))
NN = (((1,), (0,)), ((), ()))


def mm(a, b, dims=NN):
    return lax.dot_general(a, b, dims, preferred_element_type=jnp.float32)


def column(head, kind, group, size):
    return ((head // group * 3 + kind) * group + head % group) * size


def stage_heads(p_ref, kx_ref, tab_ref, q_scr, k_scr, heads, group, size):
    kx = kx_ref[...]
    for h in range(heads):
        first, second = column(h, 0, group, size), column(h, 1, group, size)
        mixed = mm(kx, tab_ref[h]).astype(jnp.bfloat16)
        q_scr[h, :, : 256 - size] = mixed[:, : 256 - size]
        q_scr[h, :, 256 - size :] = p_ref[:, first : first + size] * jnp.bfloat16(size**-0.5)
        k_scr[h, :, :128] = kx
        k_scr[h, :, 128 : 256 - size] = kx[:, : 128 - size]
        k_scr[h, :, 256 - size :] = p_ref[:, second : second + size]


def bound_ok(q_scr, k_scr, heads, size):
    big_q, big_k = 0.0, 0.0
    for h in range(heads):
        big_q = jnp.maximum(big_q, jnp.max(jnp.abs(q_scr[h, :, 256 - size :].astype(jnp.float32))))
        big_k = jnp.maximum(big_k, jnp.max(jnp.abs(k_scr[h, :, 256 - size :].astype(jnp.float32))))
    return big_q * big_k * size < SAFE


def window(win_ref, chunk, safe, length, tile):
    start = jnp.where(safe, win_ref[0, chunk], 0)
    count = jnp.where(safe, win_ref[1, chunk], length // tile)
    return pl.multiple_of(start, 128), count


def masked(safe, scores_scr, row, tile, seg_col, seg_row):
    @pl.when(jnp.logical_not(safe))
    def _():
        scores_scr[pl.ds(row, tile), :] = jnp.where(
            seg_col == seg_row, scores_scr[pl.ds(row, tile), :], NEGATIVE
        )


def forward_kernel(
    win_ref, p_ref, kx_ref, tab_ref, segc_ref, segr_ref, o_ref, lse_ref,
    q_scr, k_scr, vt_scr, s_scr, ot_scr, *, heads, group, size, chunk_rows, tile,
):
    length = kx_ref.shape[0]
    stage_heads(p_ref, kx_ref, tab_ref, q_scr, k_scr, heads, group, size)
    for h in range(heads):
        third = column(h, 2, group, size)
        vt_scr[h] = p_ref[:, third : third + size].astype(jnp.float32).T.astype(jnp.bfloat16)
    safe = bound_ok(q_scr, k_scr, heads, size)
    lse_ref[...] = jnp.zeros_like(lse_ref)

    def one_chunk(item, _):
        h, c = item // (length // chunk_rows), item % (length // chunk_rows)
        start, count = window(win_ref, c, safe, length, tile)
        first = pl.multiple_of(c * chunk_rows, chunk_rows)
        q = q_scr[h, pl.ds(first, chunk_rows), :]
        seg_row = segr_ref[:, pl.ds(first, chunk_rows)]

        def score(t, top):
            row = pl.multiple_of(t * tile, tile)
            src = pl.multiple_of(start + t * tile, 128)
            s_scr[pl.ds(row, tile), :] = mm(k_scr[h, pl.ds(src, tile), :], q, NT)
            masked(safe, s_scr, row, tile, segc_ref[pl.ds(src, tile), :1], seg_row)
            s = s_scr[pl.ds(row, tile), :]
            return jnp.maximum(top, jnp.max(s.reshape(tile // 8, 8, chunk_rows), axis=0))

        top = lax.fori_loop(0, count, score, jnp.full((8, chunk_rows), -3.0e38, jnp.float32))
        top = jnp.max(top, axis=0, keepdims=True)

        def mix(t, carry):
            total, out = carry
            row = pl.multiple_of(t * tile, tile)
            src = pl.multiple_of(start + t * tile, 128)
            p = jnp.exp(s_scr[pl.ds(row, tile), :] - top)
            total = total + jnp.sum(p.reshape(tile // 8, 8, chunk_rows), axis=0)
            out = out + mm(vt_scr[h, :, pl.ds(src, tile)], p.astype(jnp.bfloat16))
            return total, out

        total, out = lax.fori_loop(
            0, count, mix,
            (jnp.zeros((8, chunk_rows), jnp.float32), jnp.zeros((size, chunk_rows), jnp.float32)),
        )
        total = jnp.sum(total, axis=0, keepdims=True)
        lse_ref[pl.ds(h, 1), pl.ds(first, chunk_rows)] = top + jnp.log(total)
        ot_scr[h, :, pl.ds(first, chunk_rows)] = out / total
        return 0

    lax.fori_loop(0, heads * (length // chunk_rows), one_chunk, 0)
    for h in range(heads):
        o_ref[:, h * size : (h + 1) * size] = ot_scr[h].T.astype(jnp.bfloat16)


def backward_kernel(
    win_ref, p_ref, kx_ref, tab_ref, segc_ref, segr_ref, o_ref, lse_ref, g_ref, d_ref, span_ref,
    q_scr, k_scr, kt_scr, v_scr, g_scr, dk_scr, dv_scr, dq_scr, dl_scr, s_scr,
    *, heads, group, size, chunk_rows, tile, offset,
):
    length = kx_ref.shape[0]
    stage_heads(p_ref, kx_ref, tab_ref, q_scr, k_scr, heads, group, size)
    safe = bound_ok(q_scr, k_scr, heads, size)
    for h in range(heads):
        third = column(h, 2, group, size)
        kt_scr[h] = k_scr[h, :, 128:].astype(jnp.float32).T.astype(jnp.bfloat16)
        v_scr[h] = p_ref[:, third : third + size]
        g = g_ref[:, offset + h * size : offset + (h + 1) * size]
        g_scr[h] = g
        o = o_ref[:, h * size : (h + 1) * size]
        mixed = g.astype(jnp.float32) * o.astype(jnp.float32)
        dl_scr[pl.ds(h, 1), :] = jnp.sum(mixed.T, axis=0, keepdims=True)
    dk_scr[...] = jnp.zeros_like(dk_scr)
    dv_scr[...] = jnp.zeros_like(dv_scr)

    def one_chunk(item, _):
        h, c = item // (length // chunk_rows), item % (length // chunk_rows)
        start, count = window(win_ref, c, safe, length, tile)
        first = pl.multiple_of(c * chunk_rows, chunk_rows)
        q = q_scr[h, pl.ds(first, chunk_rows), :]
        q_own = q_scr[h, pl.ds(first, chunk_rows), 256 - size :]
        g = g_scr[h, pl.ds(first, chunk_rows), :]
        seg_row = segr_ref[:, pl.ds(first, chunk_rows)]
        lse = lse_ref[pl.ds(h, 1), pl.ds(first, chunk_rows)]
        delta = dl_scr[pl.ds(h, 1), pl.ds(first, chunk_rows)]

        def step(t, acc):
            src = pl.multiple_of(start + t * tile, 128)
            s_scr[...] = mm(k_scr[h, pl.ds(src, tile), :], q, NT)
            masked(safe, s_scr, 0, tile, segc_ref[pl.ds(src, tile), :1], seg_row)
            p = jnp.exp(s_scr[...] - lse)
            dp = mm(v_scr[h, pl.ds(src, tile), :], g, NT)
            ds = (p * (dp - delta)).astype(jnp.bfloat16)
            dv_scr[h, pl.ds(src, tile), :] += mm(p.astype(jnp.bfloat16), g)
            dk_scr[h, pl.ds(src, tile), :] += mm(ds, q_own)
            return acc + mm(kt_scr[h, :, pl.ds(src, tile)], ds)

        acc = lax.fori_loop(0, count, step, jnp.zeros((128, chunk_rows), jnp.float32))
        dq_scr[h, :, pl.ds(first, chunk_rows)] = acc
        return 0

    lax.fori_loop(0, heads * (length // chunk_rows), one_chunk, 0)
    for h in range(heads):
        first, second, third = (column(h, kind, group, size) for kind in range(3))
        d_ref[:, first : first + size] = (
            (dq_scr[h, 128 - size :, :] * size**-0.5).T.astype(jnp.bfloat16)
        )
        d_ref[:, second : second + size] = dk_scr[h].astype(jnp.bfloat16)
        d_ref[:, third : third + size] = dv_scr[h].astype(jnp.bfloat16)
        thr = dq_scr[h, : 128 - size, :]
        upper = thr.astype(jnp.bfloat16)
        lower = (thr - upper.astype(jnp.float32)).astype(jnp.bfloat16)
        span_ref[h] = mm(upper, kx_ref[...]) + mm(lower, kx_ref[...])


CHUNK = 256
TILE = 256
VMEM = pltpu.VMEM


def attend_forward(proj, around, size, group):
    length, total = proj.shape
    heads = total // (3 * size)
    full = pl.BlockSpec(memory_space=pltpu.VMEM)
    return pl.pallas_call(
        functools.partial(
            forward_kernel, heads=heads, group=group, size=size, chunk_rows=CHUNK, tile=TILE
        ),
        in_specs=[pl.BlockSpec(memory_space=pltpu.SMEM)] + [full] * 5,
        out_specs=[full, full],
        out_shape=[
            jax.ShapeDtypeStruct((length, heads * size), jnp.bfloat16),
            jax.ShapeDtypeStruct((8, length), jnp.float32),
        ],
        scratch_shapes=[
            VMEM((heads, length, 256), jnp.bfloat16),
            VMEM((heads, length, 256), jnp.bfloat16),
            VMEM((heads, size, length), jnp.bfloat16),
            VMEM((length, CHUNK), jnp.float32),
            VMEM((heads, size, length), jnp.float32),
        ],
        compiler_params=pltpu.CompilerParams(vmem_limit_bytes=48 * 1024 * 1024),
        cost_estimate=pl.CostEstimate(
            flops=heads * length * length * 512,
            bytes_accessed=length * total * 4,
            transcendentals=heads * length * length,
        ),
    )(around[0], proj, *around[1:])


def attend_backward(proj, around, out, lse, grads, stream, size, group):
    length, total = proj.shape
    heads = total // (3 * size)
    full = pl.BlockSpec(memory_space=pltpu.VMEM)
    return pl.pallas_call(
        functools.partial(
            backward_kernel, heads=heads, group=group, size=size, chunk_rows=CHUNK, tile=TILE,
            offset=stream * heads * size,
        ),
        in_specs=[pl.BlockSpec(memory_space=pltpu.SMEM)] + [full] * 8,
        out_specs=[full, full],
        out_shape=[
            jax.ShapeDtypeStruct((length, total), jnp.bfloat16),
            jax.ShapeDtypeStruct((heads, 128 - size, 128), jnp.float32),
        ],
        scratch_shapes=[
            VMEM((heads, length, 256), jnp.bfloat16),
            VMEM((heads, length, 256), jnp.bfloat16),
            VMEM((heads, 128, length), jnp.bfloat16),
            VMEM((heads, length, size), jnp.bfloat16),
            VMEM((heads, length, size), jnp.bfloat16),
            VMEM((heads, length, size), jnp.float32),
            VMEM((heads, length, size), jnp.float32),
            VMEM((heads, 128, length), jnp.float32),
            VMEM((8, length), jnp.float32),
            VMEM((TILE, CHUNK), jnp.float32),
        ],
        compiler_params=pltpu.CompilerParams(vmem_limit_bytes=56 * 1024 * 1024),
        cost_estimate=pl.CostEstimate(
            flops=heads * length * length * 1280,
            bytes_accessed=length * total * 8,
            transcendentals=heads * length * length,
        ),
    )(around[0], proj, *around[1:], out, lse, grads)


def attention_windows(segment_row, chunk_rows, tile):
    length = segment_row.shape[0]
    heads_of = segment_row[::chunk_rows]
    tails_of = segment_row[chunk_rows - 1 :: chunk_rows]
    low = jnp.sum((segment_row[None, :] < heads_of[:, None]).astype(jnp.int32), axis=1)
    high = jnp.sum((segment_row[None, :] <= tails_of[:, None]).astype(jnp.int32), axis=1)
    start = low // 128 * 128
    count = (high - start + tile - 1) // tile
    start = jnp.minimum(start, length - count * tile)
    return jnp.stack([start, count]).astype(jnp.int32)


def attention_tables(span_tables):
    _, heads, buckets, _ = span_tables.shape
    upper = lax.reduce_precision(span_tables, 8, 7)
    lower = (span_tables - upper).astype(jnp.bfloat16)
    def diag(t):
        z = jnp.zeros_like(t[0])
        return jnp.concatenate([jnp.concatenate([t[0], z], 2), jnp.concatenate([z, t[1]], 2)], 1)
    hi, lo = diag(upper.astype(jnp.bfloat16)), diag(lower)
    level = jnp.arange(64)
    away = jnp.where((level[:, None] != level[None, :]), NEGATIVE, 0.0)
    segs = jnp.where((level[:, None] < 4) & (level[None, :] < 4), away, 0.0).astype(jnp.bfloat16)
    segs = jnp.broadcast_to(segs[None], (heads, 64, 64))
    zero = jnp.zeros((heads, 64, 64), jnp.bfloat16)
    top = jnp.concatenate([hi, zero, lo, zero], 2)
    bottom = jnp.concatenate([zero, segs, zero, zero], 2)
    return jnp.concatenate([top, bottom], 1)


def token_marks(boxes_page, segment_row, buckets):
    levels = jnp.arange(buckets, dtype=jnp.int32)[None, :]
    kinds = jnp.arange(64, dtype=jnp.int32)[None, :]
    return jnp.concatenate(
        [boxes_page[0][:, None] == levels, boxes_page[1][:, None] == levels, segment_row[:, None] == kinds],
        axis=1,
    ).astype(jnp.bfloat16)


NORM_EPS = 1e-05
RELATIVE = 0.5
RATE_FLOOR = 0.001
PRECISE = lax.Precision.HIGHEST
LOW = jnp.bfloat16
WIDE = jnp.float32
AXES = ("dz", "dx", "my", "core")
DP = ("dz", "dx")
MP = ("my", "core")
CHIPS = ("dz", "dx", "my")
OWNERS = ("my", "dz", "dx")
FORWARD_TAPS = tuple((col, row) for col in range(3) for row in range(3))
BACKWARD_TAPS = tuple((2 - col, 2 - row) for col in range(3) for row in range(3))


def swap(values, axis, reach):
    count = lax.axis_size(axis)
    return lax.ppermute(values, axis, [(i, i ^ reach) for i in range(count)])


def bits_of(axis):
    reach, found = lax.axis_size(axis) // 2, []
    while reach:
        found.append((axis, reach))
        reach //= 2
    return found


def bits(axes):
    return [bit for axis in axes for bit in bits_of(axis)]


def side(bit):
    return lax.axis_index(bit[0]) // bit[1] % 2


def gather_tree(shard, order, owners):
    places = bits(owners)
    steps = [bit for axis in order for bit in reversed(bits_of(axis))]
    sides = [side(place) for place in places]
    rest = [0] * shard.ndim

    def corner(done, other=None):
        return [
            0 if place in done else (1 - mine if place == other else mine)
            for place, mine in zip(places, sides)
        ] + rest

    held = shard.reshape((1,) * len(places) + shard.shape)
    whole = jnp.zeros((2,) * len(places) + shard.shape, shard.dtype)
    whole = lax.dynamic_update_slice(whole, held, corner(()))
    done = []
    for bit in steps:
        whole = lax.dynamic_update_slice(whole, swap(held, *bit), corner(done, bit))
        done.append(bit)
        sizes = [2 if place in done else 1 for place in places] + list(shard.shape)
        held = lax.dynamic_slice(whole, corner(done), sizes)
    return whole.reshape((2 ** len(places) * shard.shape[0],) + shard.shape[1:])


def scatter_tree(blocks, order, live, wide=True):
    live = list(live)
    steps = [bit for axis in order for bit in bits_of(axis)]
    for number, bit in enumerate(steps):
        place = live.index(bit)
        half = blocks.shape[place] // 2
        mine = side(bit)
        sent = lax.dynamic_slice_in_dim(blocks, (1 - mine) * half, half, place)
        kept = lax.dynamic_slice_in_dim(blocks, mine * half, half, place)
        blocks = kept.astype(WIDE) + swap(sent, *bit).astype(WIDE)
        if number < len(steps) - 1:
            blocks = blocks.astype(LOW)
    return blocks


def scatter_rows(blocks, order, owners):
    live = bits(owners)
    split = blocks.reshape((2,) * len(live) + (-1,) + blocks.shape[1:])
    summed = scatter_tree(split, order, live + [None] * blocks.ndim)
    return summed.reshape(summed.shape[len(live) :])


def total_over(values, axes):
    for bit in bits(axes):
        values = values + swap(values, *bit)
    return values


def by_side(bit, own, other, axis):
    return jnp.where(
        side(bit) == 0, jnp.stack([own, other], axis), jnp.stack([other, own], axis)
    )


def from_both(own):
    both = by_side(("core", 1), own, swap(own, "core", 1), 1)
    return both.reshape((-1,) + own.shape[2:])


def add_both(partial, quarter):
    parts = partial.reshape((-1, 2, quarter) + partial.shape[1:])
    core = lax.axis_index("core")
    sent = lax.dynamic_index_in_dim(parts, 1 - core, 1, keepdims=False)
    kept = lax.dynamic_index_in_dim(parts, core, 1, keepdims=False)
    return (kept + swap(sent.astype(LOW), "core", 1).astype(WIDE)).reshape(
        (-1,) + partial.shape[1:]
    )


def extended(cells, sides, width):
    for axis, dim in sides:
        count = lax.axis_size(axis)
        ends = count - 1
        head = lax.slice_in_dim(cells, 0, width, axis=dim)
        tail = lax.slice_in_dim(cells, cells.shape[dim] - width, cells.shape[dim], axis=dim)
        cells = jnp.concatenate(
            [
                lax.ppermute(tail, axis, [(i, i + 1) for i in range(ends)]),
                cells,
                lax.ppermute(head, axis, [(i + 1, i) for i in range(ends)]),
            ],
            axis=dim,
        )
    return cells


def smooth(values):
    return jax.nn.gelu(values, approximate=True)


def smooth_back(values, upstream):
    return jax.vjp(smooth, values)[1](upstream)[0]


def layer_norm(values, norm_gain, norm_shift):
    centre = values - jnp.mean(values, axis=-1, keepdims=True)
    spread = jnp.mean(centre * centre, axis=-1, keepdims=True)
    return centre * lax.rsqrt(spread + NORM_EPS) * norm_gain + norm_shift


def relative_select(buckets, reach_max):
    offsets = (
        jnp.arange(buckets, dtype=jnp.int32)[None, :]
        - jnp.arange(buckets, dtype=jnp.int32)[:, None]
    )
    clipped = jnp.clip(offsets, -reach_max, reach_max) + reach_max
    return (
        clipped[:, :, None] == jnp.arange(2 * reach_max + 1, dtype=jnp.int32)[None, None, :]
    ).astype(WIDE)


def stacked_taps(padded, across, downward, anchors):
    return jnp.concatenate(
        [
            padded[:, from_col : from_col + across, from_row : from_row + downward, :]
            for from_col, from_row in anchors
        ],
        axis=-1,
    )


def dot(left, right, dims="nn"):
    first = 0 if dims[0] == "t" else 1
    second = 1 if dims[1] == "t" else 0
    return lax.dot_general(
        left, right, (((first,), (second,)), ((), ())), preferred_element_type=WIDE
    )


def factored_step(weight, gradient, rows_old, cols_old, row_piece, col_piece, row_mean, weight_mean, sizes):
    decay_rate = 1.0 - STEP ** (-0.8)
    rows_next = decay_rate * rows_old + (1.0 - decay_rate) * row_piece / sizes[1]
    cols_next = decay_rate * cols_old + (1.0 - decay_rate) * col_piece / sizes[0]
    second = rows_next[..., :, None] * cols_next[..., None, :] / row_mean[..., None, None]
    step_rate = RELATIVE * jnp.maximum(RATE_FLOOR, jnp.sqrt(weight_mean))
    weight_next = weight - step_rate[..., None, None] * (gradient * lax.rsqrt(second))
    return (gradient, weight_next, rows_next, cols_next, weight_next.astype(LOW))


def moment_step(parameter, gradient, moment, reduce_axes):
    decay_rate = 1.0 - STEP ** (-0.8)
    moment_next = decay_rate * moment + (1.0 - decay_rate) * gradient * gradient
    rms_value = jnp.sqrt(jnp.mean(parameter * parameter, axis=reduce_axes, keepdims=True))
    return (
        gradient,
        moment_next,
        parameter
        - RELATIVE * jnp.maximum(RATE_FLOOR, rms_value) * gradient * lax.rsqrt(moment_next),
    )


def pack(parts):
    return jnp.concatenate([part.reshape(-1) for part in parts])


def unpack(flat, like):
    found, cursor = [], 0
    for part in like:
        found.append(flat[cursor : cursor + part.size].reshape(part.shape))
        cursor += part.size
    return found


def on_device(
    image, text, cotangent, segments, boxes,
    reduce_weight, reduce_weight_rows, reduce_weight_cols,
    spatial_weight, spatial_weight_rows, spatial_weight_cols,
    expand_weight, expand_weight_rows, expand_weight_cols,
    visual_proj, visual_proj_rows, visual_proj_cols,
    attn_in, attn_in_rows, attn_in_cols,
    attn_out, attn_out_rows, attn_out_cols,
    ffn_up, ffn_up_rows, ffn_up_cols,
    ffn_down, ffn_down_rows, ffn_down_cols,
    norm_params, norm_moment, up_bias, up_moment, tables, table_moment,
):
    dp_count = lax.axis_size(DP)
    pair = lax.axis_size("my")
    mp_count = 2 * pair
    my, core = lax.axis_index("my"), lax.axis_index("core")
    mp_index = lax.axis_index(MP)
    length, width = text.shape[1:]
    quarter = length // mp_count
    heads = tables.shape[2]
    size = width // heads
    group = heads // mp_count
    part = group * size
    units = ffn_up.shape[1]
    pages, across, down, channels = image.shape
    middle = spatial_weight.shape[1]

    layer_in = jnp.concatenate(
        [
            attn_in.astype(LOW).transpose(2, 0, 1, 3).reshape(attn_in.shape[2], -1),
            attn_out.astype(LOW).transpose(2, 0, 1).reshape(attn_out.shape[2], -1),
        ],
        axis=1,
    )
    layer_ffn = jnp.concatenate([ffn_up.astype(LOW), ffn_down.astype(LOW).T], axis=1)
    attn_whole = lax.all_gather(layer_in, OWNERS, axis=0, tiled=True).reshape(pair, width, -1)
    ffn_whole = lax.all_gather(layer_ffn, OWNERS, axis=0, tiled=True).reshape(pair, width, -1)
    reduce_low = reduce_weight.astype(LOW)
    reduce_half = reduce_low.shape[0] // 2
    middle_cut = spatial_weight.shape[0] // 2
    side_low = jnp.concatenate(
        [expand_weight.astype(LOW).reshape(-1, middle), visual_proj.astype(LOW)], axis=1
    )
    weight_reduce = gather_tree(reduce_low, ("dz", "dx", "my", "core"), AXES)
    weight_spatial = gather_tree(spatial_weight.astype(LOW), ("dz", "my", "dx", "core"), AXES)
    side_whole = gather_tree(side_low, ("dz", "dx", "my", "core"), AXES)
    weight_expand = side_whole[:, :middle].reshape(middle, channels)
    weight_proj = side_whole[:, middle:]

    bucket_select = relative_select(NB, (tables.shape[1] - 1) // 2)
    own_tables = tables.reshape(tables.shape[:2] + (pair, 2, group))
    own_tables = lax.dynamic_index_in_dim(own_tables, core, 3, keepdims=False).reshape(
        tables.shape[:2] + (pair * group,)
    )
    span_tables = jnp.einsum("abr,trh->thab", bucket_select, own_tables, precision=PRECISE)
    head_tables = attention_tables(span_tables)
    page_segments = lax.dynamic_index_in_dim(segments, my, 0, keepdims=False)
    page_boxes = lax.dynamic_index_in_dim(boxes, my, 0, keepdims=False)
    marks = token_marks(page_boxes, page_segments, NB)
    windows = attention_windows(page_segments, CHUNK, TILE)
    segment_cols = jnp.broadcast_to(page_segments[:, None], (length, 128))
    around = (windows, marks, head_tables, segment_cols, page_segments[None])
    text_page = lax.dynamic_index_in_dim(text, my, 0, keepdims=False)
    upstream_page = lax.dynamic_index_in_dim(cotangent, my, 0, keepdims=False)

    def own_tokens(page):
        split = page.reshape(pair, 2, quarter, width)
        return lax.dynamic_index_in_dim(split, core, 1, keepdims=False).reshape(-1, width)

    weight_in = [
        attn_whole[:, :, stream * 3 * part : (stream + 1) * 3 * part]
        .transpose(1, 0, 2)
        .reshape(width, pair * 3 * part)
        for stream in range(2)
    ]
    weight_out = (
        attn_whole[:, :, 6 * part :]
        .reshape(pair, width, 2, part)
        .transpose(1, 2, 0, 3)
        .reshape(width, 2 * pair * part)
    )
    weight_up = [ffn_whole[y, :, :units] for y in range(pair)]
    weight_down = [ffn_whole[y, :, units:] for y in range(pair)]

    reduced = jnp.einsum("pwhc,cd->pwhd", image, weight_reduce, preferred_element_type=WIDE)
    hidden_one = smooth(reduced).astype(LOW)
    padded = extended(hidden_one, ((DP, 2), (MP, 1)), 1)
    tap_stack = stacked_taps(padded, across, down, FORWARD_TAPS)
    convolved = jnp.einsum("pwhk,kd->pwhd", tap_stack, weight_spatial, preferred_element_type=WIDE)
    hidden_two = smooth(convolved).astype(LOW)
    expanded = jnp.einsum("pwhc,cd->pwhd", hidden_two, weight_expand, preferred_element_type=WIDE)
    summed_pre = image.astype(WIDE) + expanded
    feature_low = smooth(summed_pre).astype(LOW)
    visual_rows = jnp.einsum(
        "pwhc,cd->pwhd", feature_low, weight_proj, preferred_element_type=WIDE
    ).astype(LOW)
    visual_own = lax.all_to_all(visual_rows, CHIPS, split_axis=0, concat_axis=0, tiled=True)
    visual_own = (
        visual_own.reshape(dp_count, pair, across, down, width)
        .transpose(1, 2, 0, 3, 4)
        .reshape(pair, quarter, width)
    )
    visual_page = from_both(visual_own)

    sources = (text_page, visual_page)
    projected, attended, logs = [], [], []
    for stream in range(2):
        projected.append(dot(sources[stream], weight_in[stream]).astype(LOW))
        mixed, log_sum = attend_forward(projected[stream], around, size, group)
        attended.append(mixed)
        logs.append(log_sum)
    attended_both = jnp.concatenate(attended, axis=1)
    attention = add_both(dot(attended_both, weight_out, "nt"), quarter)
    first_sum = (
        own_tokens(text_page).astype(WIDE) + visual_own.reshape(-1, width).astype(WIDE) + attention
    )
    normed, first_pull = jax.vjp(layer_norm, first_sum, norm_params[0], norm_params[1])
    normed_low = from_both(normed.astype(LOW).reshape(pair, quarter, width))
    own_bias = lax.dynamic_index_in_dim(up_bias.reshape(pair, 2, units), core, 1, keepdims=False)
    hidden_pre = [dot(normed_low, weight_up[y]) + own_bias[y] for y in range(pair)]
    hidden_low = [smooth(pre).astype(LOW) for pre in hidden_pre]
    down_part = sum(dot(hidden_low[y], weight_down[y], "nt") for y in range(pair))
    second_sum = normed + (add_both(down_part, quarter) + norm_params[4])
    final_out, second_pull = jax.vjp(layer_norm, second_sum, norm_params[2], norm_params[3])
    out_low = final_out.astype(LOW)
    out_pages = by_side(("my", 1), out_low, swap(out_low, "my", 1), 0)
    out_pages = out_pages.reshape(pair, pair, quarter, width)
    out_pages = by_side(("core", 1), out_pages, swap(out_pages, "core", 1), 2)
    out_local = out_pages.reshape(text.shape)

    second_grad, gain_two, shift_two = second_pull(own_tokens(upstream_page).astype(WIDE))
    down_own = second_grad.astype(LOW)
    down_bias_grad = jnp.sum(down_own.astype(WIDE), axis=0)
    down_low = from_both(down_own.reshape(pair, quarter, width))
    hidden_grad_low = [
        smooth_back(hidden_pre[y], dot(down_low, weight_down[y])).astype(LOW) for y in range(pair)
    ]
    normed_part = sum(dot(hidden_grad_low[y], weight_up[y], "nt") for y in range(pair))
    up_part = jnp.stack([jnp.sum(part_low.astype(WIDE), axis=0) for part_low in hidden_grad_low])
    grad_down = jnp.concatenate([dot(down_low, hidden_low[y], "tn").astype(LOW) for y in range(pair)])
    grad_up = jnp.concatenate(
        [dot(normed_low, hidden_grad_low[y], "tn").astype(LOW) for y in range(pair)]
    )
    down_shard = scatter_rows(grad_down, ("my", "dx", "dz"), OWNERS)
    up_shard = scatter_rows(grad_up, ("dx", "my", "dz"), OWNERS)
    normed_grad = second_grad + add_both(normed_part, quarter)
    first_grad, gain_one, shift_one = first_pull(normed_grad)
    norm_part = jnp.stack([gain_one, shift_one, gain_two, shift_two, down_bias_grad])
    attention_low = from_both(first_grad.astype(LOW).reshape(pair, quarter, width))
    head_grads = dot(attention_low, weight_out).astype(LOW)
    grad_out = dot(attention_low, attended_both, "tn").astype(LOW)
    projected_grads, span_grads = [], []
    for stream in range(2):
        own_grads, span_part = attend_backward(
            projected[stream], around, attended[stream], logs[stream], head_grads, stream, size, group
        )
        projected_grads.append(own_grads)
        span_grads.append(span_part)
    source_own = [
        add_both(dot(projected_grads[stream], weight_in[stream], "nt"), quarter)
        for stream in range(2)
    ]
    visual_low = (first_grad + source_own[1]).astype(LOW)
    text_back = (first_grad + source_own[0]).reshape(pair, quarter, width)
    text_sent = lax.dynamic_index_in_dim(text_back, 1 - my, 0, keepdims=False)
    text_kept = lax.dynamic_index_in_dim(text_back, my, 0, keepdims=False)
    text_grad_local = by_side(
        ("my", 1), text_kept, swap(text_sent.astype(LOW), "my", 1).astype(WIDE), 0
    )
    visual_sent = (
        visual_low.reshape(pair, across, dp_count, down, width)
        .transpose(2, 0, 1, 3, 4)
        .reshape(pages, across, down, width)
    )
    visual_grad = lax.all_to_all(visual_sent, CHIPS, split_axis=0, concat_axis=0, tiled=True)
    grad_in = [
        dot(sources[stream], projected_grads[stream], "tn").astype(LOW).reshape(width, pair, 3 * part)
        for stream in range(2)
    ]
    grad_attn = jnp.concatenate(
        grad_in + [grad_out.reshape(width, 2, pair, part)[:, s] for s in range(2)], axis=2
    ).transpose(1, 0, 2)
    attn_cut = grad_attn.shape[2] // 2
    attn_shard = jnp.concatenate(
        [
            scatter_rows(
                grad_attn[:, :, :attn_cut].reshape(-1, attn_cut), ("my", "dx", "dz"), OWNERS
            ),
            scatter_rows(
                grad_attn[:, :, attn_cut:].reshape(-1, attn_cut), ("dx", "my", "dz"), OWNERS
            ),
        ],
        axis=1,
    )

    grad_proj = jnp.einsum("pwhc,pwhd->cd", feature_low, visual_grad, preferred_element_type=WIDE)
    feature_grad = jnp.einsum("pwhd,cd->pwhc", visual_grad, weight_proj, preferred_element_type=WIDE)
    pre_grad = smooth_back(summed_pre, feature_grad)
    expanded_low = pre_grad.astype(LOW)
    grad_expand = jnp.einsum("pwhc,pwhd->cd", hidden_two, expanded_low, preferred_element_type=WIDE)
    conv_grad = smooth_back(
        convolved,
        jnp.einsum("pwhd,cd->pwhc", expanded_low, weight_expand, preferred_element_type=WIDE),
    ).astype(LOW)
    back_padded = extended(conv_grad, ((DP, 2), (MP, 1)), 1)
    back_taps = stacked_taps(back_padded, across, down, BACKWARD_TAPS).reshape(
        conv_grad.shape[:3] + (9, middle)
    )
    reduced_grad = smooth_back(
        reduced,
        jnp.einsum(
            "pwhko,kio->pwhi",
            back_taps,
            weight_spatial.reshape(9, middle, middle),
            preferred_element_type=WIDE,
        ),
    ).astype(LOW)
    grad_spatial = jnp.einsum("pwhk,pwhd->kd", tap_stack, conv_grad, preferred_element_type=WIDE)
    grad_reduce = jnp.einsum("pwhc,pwhd->cd", image, reduced_grad, preferred_element_type=WIDE)
    image_grad_local = pre_grad + jnp.einsum(
        "pwhd,cd->pwhc", reduced_grad, weight_reduce, preferred_element_type=WIDE
    )
    grad_side = jnp.concatenate(
        [grad_expand.astype(LOW).reshape(-1, middle), grad_proj.astype(LOW)], axis=1
    )
    side_shard = scatter_rows(grad_side, ("core", "my", "dx", "dz"), AXES)
    spatial_shard = scatter_rows(grad_spatial.astype(LOW), ("core", "dx", "my", "dz"), AXES)
    reduce_shard = scatter_rows(grad_reduce.astype(LOW), ("core", "my", "dx", "dz"), AXES)
    expand_shard = side_shard[:, :middle].reshape(expand_weight.shape)
    proj_shard = side_shard[:, middle:]

    in_shard = attn_shard[:, : 6 * part].reshape(-1, 2, 3, part).transpose(1, 2, 0, 3)
    out_shard = attn_shard[:, 6 * part :].reshape(-1, 2, part).transpose(1, 2, 0)
    down_shard = down_shard.T
    image_sets = (
        (reduce_weight, reduce_shard, reduce_weight_rows, reduce_weight_cols),
        (spatial_weight, spatial_shard, spatial_weight_rows, spatial_weight_cols),
        (expand_weight, expand_shard, expand_weight_rows, expand_weight_cols),
        (visual_proj, proj_shard, visual_proj_rows, visual_proj_cols),
    )
    layer_sets = (
        (attn_in, in_shard, attn_in_rows, attn_in_cols, dp_count, mp_count, True),
        (attn_out, out_shard, attn_out_rows, attn_out_cols, mp_count, dp_count, False),
        (ffn_up, up_shard, ffn_up_rows, ffn_up_cols, dp_count, mp_count, True),
        (ffn_down, down_shard, ffn_down_rows, ffn_down_cols, mp_count, dp_count, False),
    )
    weight_squares = [jnp.sum(entry[0] * entry[0], axis=(-2, -1)) for entry in image_sets + layer_sets]
    rows_before = [jnp.sum(entry[2], axis=-1) for entry in image_sets] + [
        jnp.sum(entry[2], axis=-1) / (entry[5]) for entry in layer_sets
    ]
    early = weight_squares + rows_before
    early_sums = unpack(total_over(pack(early), AXES), early)
    weight_squares, rows_before = early_sums[:8], early_sums[8:]

    row_parts = [jnp.sum(entry[1] * entry[1], axis=-1) for entry in layer_sets]
    col_parts = [jnp.sum(entry[1] * entry[1], axis=-2) for entry in layer_sets]
    over_dp = [(cols if entry[6] else rows) for rows, cols, entry in zip(row_parts, col_parts, layer_sets)]
    over_mp = [(rows if entry[6] else cols) for rows, cols, entry in zip(row_parts, col_parts, layer_sets)]
    dp_sums = unpack(total_over(pack(over_dp), DP), over_dp)
    mp_sums = unpack(total_over(pack(over_mp), MP), over_mp)
    squares_total = [jnp.sum(rows, axis=-1) for rows in row_parts]
    span_sum = span_grads[0] + span_grads[1]
    span_sum = jnp.stack([span_sum[:, :NB, :NB], span_sum[:, NB : 2 * NB, NB : 2 * NB]])
    table_part = jnp.einsum("abr,thba->trh", bucket_select, span_sum, precision=PRECISE)
    table_term = jnp.zeros(tables.shape[:2] + (pair, 2, group), WIDE)
    table_term = lax.dynamic_update_slice(
        table_term, table_part.reshape(tables.shape[:2] + (pair, 1, group)), (0, 0, 0, core, 0)
    ).reshape(tables.shape)
    up_term = lax.dynamic_update_slice(
        jnp.zeros((pair, 2, units), WIDE), up_part[:, None], (0, core, 0)
    ).reshape(up_bias.shape)
    middle_terms = [norm_part, up_term, table_term] + squares_total
    middle_sums = unpack(total_over(pack(middle_terms), AXES), middle_terms)
    norm_gradient, up_gradient, table_gradient = middle_sums[:3]
    squares_total = middle_sums[3:]
    late = [jnp.sum(entry[1] * entry[1], axis=-2) for entry in image_sets]
    image_cols = unpack(total_over(pack(late), AXES), late)

    decay_rate = 1.0 - STEP ** (-0.8)
    results = []
    for number, (weight, gradient, rows_old, cols_old) in enumerate(image_sets):
        sizes = (weight.shape[0] * dp_count * mp_count, weight.shape[1])
        rows_sum = jnp.sum(gradient * gradient, axis=-1)
        mean = (
            decay_rate * rows_before[number]
            + (1.0 - decay_rate) * jnp.sum(image_cols[number], axis=-1) / sizes[1]
        ) / sizes[0]
        results.append(
            factored_step(
                weight, gradient, rows_old, cols_old, rows_sum, image_cols[number], mean,
                weight_squares[number] / (sizes[0] * sizes[1]), sizes,
            )
        )
    for number, (weight, gradient, rows_old, cols_old, row_split, col_split, flag) in enumerate(layer_sets):
        sizes = (weight.shape[-2] * row_split, weight.shape[-1] * col_split)
        rows_sum = mp_sums[number] if flag else dp_sums[number]
        cols_sum = dp_sums[number] if flag else mp_sums[number]
        mean = (
            decay_rate * rows_before[4 + number]
            + (1.0 - decay_rate) * squares_total[number] / sizes[1]
        ) / sizes[0]
        results.append(
            factored_step(
                weight, gradient, rows_old, cols_old, rows_sum, cols_sum, mean,
                weight_squares[4 + number] / (sizes[0] * sizes[1]), sizes,
            )
        )
    norm_parts = moment_step(norm_params, norm_gradient, norm_moment, (1,))
    bias_parts = moment_step(up_bias, up_gradient, up_moment, (0,))
    table_parts = moment_step(tables, table_gradient, table_moment, (1, 2))
    flat = [value for result in results for value in result]
    return (
        (out_local, text_grad_local, image_grad_local)
        + tuple(flat)
        + norm_parts
        + bias_parts
        + table_parts
    )


def solution(mesh):
    whole = mesh.shape["dp"], mesh.shape["mp"]
    devices = mesh.devices.reshape(whole[0] // 2, 2, whole[1] // 2, 2)
    flat, rows, none = P(AXES, None), P(AXES), P()
    image_weight_in = (flat, rows, none)
    image_weight_out = (flat, flat, rows, none, flat)
    in_spec, in_rows, in_cols = P(None, None, DP, MP), P(None, None, DP), P(None, None, MP)
    out_spec, out_rows, out_cols = P(None, MP, DP), P(None, MP), P(None, DP)
    up_spec, up_rows, up_cols = P(DP, MP), P(DP), P(MP)
    down_spec, down_rows, down_cols = P(MP, DP), P(MP), P(DP)
    placed = (
        (P(None, MP, DP, None), P(DP, None, None), P(DP, None, None), P(DP, None), P(DP, None, None))
        + image_weight_in * 4
        + (in_spec, in_rows, in_cols, out_spec, out_rows, out_cols)
        + (up_spec, up_rows, up_cols, down_spec, down_rows, down_cols)
        + (none,) * 6
    )
    given = (
        (P(DP, None, None), P(DP, MP, None), P(None, MP, DP, None))
        + image_weight_out * 4
        + (in_spec, in_spec, in_rows, in_cols, in_spec)
        + (out_spec, out_spec, out_rows, out_cols, out_spec)
        + (up_spec, up_spec, up_rows, up_cols, up_spec)
        + (down_spec, down_spec, down_rows, down_cols, down_spec)
        + (none,) * 9
    )
    return jax.shard_map(
        on_device, mesh=Mesh(devices, AXES), in_specs=placed, out_specs=given, check_vma=False
    )
```

time: 2160 us -> 1030 us (0.48)
  waiting for transfers between devices: 1260 us -> 256 us
  matrix products: 373 us -> 125 us
  Pallas kernels: 0 us -> 173 us
  starting transfers between devices: 57.1 us -> 136 us
  blocking collectives: 78.7 us -> 0 us
  other arithmetic: 162 us -> 125 us
    reduce_scatter x9 -> x0, waiting for transfers between devices: 436 us -> none  [the longest x1 141 us: reduce_image(): lax.psum_scatter(expand_part, ('dp', 'mp'), scatter_dimension=0, tiled=True)]
    psum x4 -> x0, waiting for transfers between devices: 315 us -> none  [the longest x1 114 us: on_device(): lax.psum((flat_stats, norm_term, up_term, table_term), ('dp', 'mp'))]
    all_gather x9 -> x2, waiting for transfers between devices: 254 us -> 0.01 us  [the longest x1 0.01 us: on_device(): lax.all_gather(layer_in, OWNERS, axis=0, tiled=True)]
    ppermute x16 -> x86, waiting for transfers between devices: 2.17 us -> 239 us  [the longest x78 225 us: swap(): return lax.ppermute(values, axis, [(i, i ^ reach) for i in range(count)])]
    unnamed x28 -> x2, waiting for transfers between devices: 215 us -> 0.03 us
    dot_general x130 -> x28, matrix products: 303 us -> 92 us  [the longest x21 62.7 us: dot(): lax.dot_general(left, right, (((first,), (second,)), ((), ())), preferred...]
    pallas_call x0 -> x4, Pallas kernels: none -> 173 us  [the longest x2 107 us: attend_backward(): pl.pallas_call(functools.partial(backward_kernel, heads=heads, group=grou...]
    ppermute x16 -> x86, starting transfers between devices: 38.4 us -> 127 us  [the longest x78 111 us: swap(): return lax.ppermute(values, axis, [(i, i ^ reach) for i in range(count)])]
  transfers between devices with their start and end apart: 45 -> 90, of which waited for: 24 -> 41; matrix products, arithmetic and copies ran while one was open for 19% -> 35% of each run, Pallas kernels for 0% -> 17%
where the time goes in v1:
time: 1030 us; the launch traced here: 1020 us
  waiting for transfers between devices  256 us (25%)
  local copies, waits for them, and re-layouts  173 us (17%)
  Pallas kernels  173 us (17%)
  starting transfers between devices  136 us (13%)
  other arithmetic  125 us (12%)
  matrix products  125 us (12%)
  between operations  31.7 us (3%)
    ppermute x78, waiting for transfers between devices, swap(): return lax.ppermute(values, axis, [(i, i ^ reach) for i in range(count)])  225 us
    ppermute x78, starting transfers between devices, swap(): return lax.ppermute(values, axis, [(i, i ^ reach) for i in range(count)])  111 us
    pallas_call x2, Pallas kernels, attend_backward(): pl.pallas_call(functools.partial(backward_kernel, heads=heads, group=grou...  107 us
    pallas_call x2, Pallas kernels, attend_forward(): pl.pallas_call(functools.partial(forward_kernel, heads=heads, group=group...  66.3 us
    dot_general x21, matrix products, dot(): lax.dot_general(left, right, (((first,), (second,)), ((), ())), preferred...  62.7 us
    unnamed x388, local copies, waits for them, and re-layouts  34 us
  transfers between devices with their start and end apart: 90, of which 41 were waited for; matrix products, arithmetic and copies ran while one was open for 35% of the time, Pallas kernels for 17%

profile of v1, /device:TPU:0, one launch (start us, length us, event | category | flops | bytes accessed | tf_op | source)
XLA Modules:
  0.0 1019.9 jit_solution(4177069314636624477)
XLA Ops:
  44.0 12.4 %collective-permute-done.1 = bf16[1,2,1,1,1,64,512]{6,5,4,3,2,1,0:T(8,128)(2,1)S(1)} collective-permute-done((bf16[1,2,1,1,1,64,512]{6,5,4,3,2,1,0:T(8,128)(2,1)S(1)}, bf16[1,2,1,1,1,64,512]{6,5,4,3,2,1,0:T(8,128)(2,1)S(1)}, u32[]{:S(2)}, u32[]{:S(2)}) %collective-permute-start.1) | collective-permute-done | bytes 131104 | tf_op jit(solution)/shard_map/ppermute | solution.py:301
  60.9 17.3 %collective-permute-done.10 = bf16[1,2,1,1,1,144,512]{6,5,4,3,2,1,0:T(8,128)(2,1)S(1)} collective-permute-done((bf16[1,2,1,1,1,144,512]{6,5,4,3,2,1,0:T(8,128)(2,1)S(1)}, bf16[1,2,1,1,1,144,512]{6,5,4,3,2,1,0:T(8,128)(2,1)S(1)}, u32[]{:S(2)}, u32[]{:S(2)}) %collective-permute-start.10) | collective-permute-done | bytes 294944 | tf_op jit(solution)/shard_map/ppermute | solution.py:301
  89.2 17.5 %collective-permute-done.3 = bf16[2,2,2,1,1,64,512]{6,5,4,3,2,1,0:T(8,128)(2,1)S(1)} collective-permute-done((bf16[2,2,2,1,1,64,512]{6,5,4,3,2,1,0:T(8,128)(2,1)S(1)}, bf16[2,2,2,1,1,64,512]{6,5,4,3,2,1,0:T(8,128)(2,1)S(1)}, u32[]{:S(2)}, u32[]{:S(2)}) %collective-permute-start.3) | collective-permute-done | bytes 524320 | tf_op jit(solution)/shard_map/ppermute | solution.py:301
  110.1 13.7 %collective-permute-done.11 = bf16[2,2,1,1,1,144,512]{6,5,4,3,2,1,0:T(8,128)(2,1)} collective-permute-done((bf16[2,2,1,1,1,144,512]{6,5,4,3,2,1,0:T(8,128)(2,1)}, bf16[2,2,1,1,1,144,512]{6,5,4,3,2,1,0:T(8,128)(2,1)}, u32[]{:S(2)}, u32[]{:S(2)}) %collective-permute-start.11) | collective-permute-done | bytes 589856 | tf_op jit(solution)/shard_map/ppermute | solution.py:301
  144.1 13.8 %collective-permute-done.5 = bf16[16,4,1,512]{3,0,2,1:T(8,128)(2,1)S(1)} collective-permute-done((bf16[16,4,1,512]{3,0,2,1:T(8,128)(2,1)S(1)}, bf16[16,4,1,512]{3,0,2,1:T(8,128)(2,1)S(1)}, u32[]{:S(2)}, u32[]{:S(2)}) %collective-permute-start.5) | collective-permute-done | bytes 65568 | tf_op jit(solution)/shard_map/ppermute | solution.py:401
  176.9 6.3 multiply_convert_fusion.3
  198.0 5.3 fusion.67
  213.0 16.9 %all-to-all-done = bf16[16,4,8,768]{3,2,1,0:T(8,128)(2,1)} async-done(((bf16[16,4,8,768]{3,2,1,0:T(8,128)(2,1)}), bf16[16,4,8,768]{3,2,1,0:T(8,128)(2,1)}, u32[]{:S(2)}, u32[]{:S(2)}) %all-to-all-start) | async-done | bytes 786464 | tf_op jit(solution)/shard_map/all_to_all | solution.py:583
  256.1 33.2 %shard_map.738 = (bf16[1024,384]{1,0:T(8,128)(2,1)S(1)}, f32[8,1024]{1,0:T(8,128)S(1)}) custom-call(s32[2,4]{1,0:T(2,128)S(1)} %pad_add_fusion.win_ref, bf16[1024,1152]{1,0:T(8,128)(2,1)S(1)} %convolution_convert_fusion.1.p_ref, bf16[1024,128]{1,0:T(8,128)(2,1)S(1)} %add_convert_fusion.26.kx_ref, bf16[6,128,256]{2,1,0:T(8,128)(2,1)S(1)} %fusion.134.tab_ref, ...), custom_call_target="tpu_custom_call" | custom-call | flops 3221225472 | bytes 4718592 | tf_op jit(solution)/shard_map/pallas_call | solution.py:183
  291.8 33.0 %shard_map.739 = (bf16[1024,384]{1,0:T(8,128)(2,1)S(1)}, f32[8,1024]{1,0:T(8,128)S(1)}) custom-call(s32[2,4]{1,0:T(2,128)S(1)} %pad_add_fusion.win_ref, bf16[1024,1152]{1,0:T(8,128)(2,1)S(1)} %convolution_convert_fusion.p_ref, bf16[1024,128]{1,0:T(8,128)(2,1)S(1)} %add_convert_fusion.26.kx_ref, bf16[6,128,256]{2,1,0:T(8,128)(2,1)S(1)} %fusion.134.tab_ref, ...), custom_call_target="tpu_custom_call" | custom-call | flops 3221225472 | bytes 4718592 | tf_op jit(solution)/shard_map/pallas_call | solution.py:183
  375.1 5.3 fusion.54
  380.4 6.5 collective-permute-start.23
  443.9 5.5 collective-permute-done.72
  458.3 53.5 %shard_map.741 = (bf16[1024,1152]{1,0:T(8,128)(2,1)}, f32[6,64,128]{2,1,0:T(8,128)}) custom-call(s32[2,4]{1,0:T(2,128)} %copy-done.8, bf16[1024,1152]{1,0:T(8,128)(2,1)} %copy-done.10, bf16[1024,128]{1,0:T(8,128)(2,1)} %copy-done.6, bf16[6,128,256]{2,1,0:T(8,128)(2,1)} %copy-done.5, s32[1024,128]{1,0:T(8,128)} %copy-done.4, s32[1,1024]{1,0:T(1,128)} %copy-done.7, ...), custom_call_target="tpu_custom_call" | custom-call | flops 8053063680 | bytes 9437184 | tf_op jit(solution)/shard_map/pallas_call | solution.py:213
  511.8 53.2 %shard_map.740 = (bf16[1024,1152]{1,0:T(8,128)(2,1)}, f32[6,64,128]{2,1,0:T(8,128)}) custom-call(s32[2,4]{1,0:T(2,128)} %copy-done.8, bf16[1024,1152]{1,0:T(8,128)(2,1)} %copy-done.9, bf16[1024,128]{1,0:T(8,128)(2,1)} %copy-done.6, bf16[6,128,256]{2,1,0:T(8,128)(2,1)} %copy-done.5, s32[1024,128]{1,0:T(8,128)} %copy-done.4, s32[1,1024]{1,0:T(1,128)} %copy-done.7, ...), custom_call_target="tpu_custom_call" | custom-call | flops 8053063680 | bytes 9437184 | tf_op jit(solution)/shard_map/pallas_call | solution.py:213
  596.8 7.6 collective-permute-start.60
  613.1 5.2 fusion.193
  626.8 5.9 collective-permute-done.70
  635.4 6.7 collective-permute-done.74
  652.4 14.0 %collective-permute-start.64 = (bf16[2,2,2,1,96,768]{5,4,3,2,1,0:T(8,128)(2,1)}, bf16[2,2,2,1,96,768]{5,4,3,2,1,0:T(8,128)(2,1)}, u32[]{:S(2)}, u32[]{:S(2)}) collective-permute-start(bf16[2,2,2,1,96,768]{5,4,3,2,1,0:T(8,128)(2,1)} %constant_dynamic-slice_fusion.13), channel_id=1, source_target_pairs={{0,4},{4,0},{1,5},{5,1},{2,6},{6,2},{3,7},{7,3},{8,12},{12,8},{9,1... | collective-permute-start | bytes 3538952 | tf_op jit(solution)/shard_map/ppermute | solution.py:301
  687.0 9.1 collective-permute-done.64
  714.9 16.4 %collective-permute-done.66 = bf16[1,1,2,1,96,768]{5,4,3,2,1,0:T(8,128)(2,1)S(1)} collective-permute-done((bf16[1,1,2,1,96,768]{5,4,3,2,1,0:T(8,128)(2,1)S(1)}, bf16[1,1,2,1,96,768]{5,4,3,2,1,0:T(8,128)(2,1)S(1)}, u32[]{:S(2)}, u32[]{:S(2)}) %collective-permute-start.66) | collective-permute-done | bytes 294944 | tf_op jit(solution)/shard_map/ppermute | solution.py:301
  763.1 9.3 fusion.190
  774.6 5.3 bitcast_convert_fusion
  787.8 5.2 bitcast_convert_fusion.1
  846.8 8.6 collective-permute-done.36
  876.7 13.6 %collective-permute-done.46 = bf16[2,2,1,2,1,144,512]{6,5,4,3,2,1,0:T(8,128)(2,1)S(1)} collective-permute-done((bf16[2,2,1,2,1,144,512]{6,5,4,3,2,1,0:T(8,128)(2,1)S(1)}, bf16[2,2,1,2,1,144,512]{6,5,4,3,2,1,0:T(8,128)(2,1)S(1)}, u32[]{:S(2)}, u32[]{:S(2)}) %collective-permute-start.46) | collective-permute-done | bytes 1179680 | tf_op jit(solution)/shard_map/ppermute | solution.py:301
  899.1 8.8 collective-permute-done.47
  914.3 9.9 collective-permute-done.48
  932.3 8.8 collective-permute-done.53
  949.0 6.6 concatenate.169
  960.1 6.3 convolution_add_fusion
  (927 shorter events, 547.5 us)
Async XLA Ops:
  7.3 228.9 %all-gather.3.cloned.1.call-start = ((), (), s32[]{:S(2)}) async-start(), calls=%async_computation.2 | async-start | bytes 5013504 | tf_op jit(solution)/shard_map/all_gather | solution.py:522
  14.6 326.0 %all-gather.5.cloned.1.call-start = ((), (), s32[]{:S(2)}) async-start(), calls=%async_computation.3 | async-start | bytes 5013504 | tf_op jit(solution)/shard_map/all_gather | solution.py:523
  18.6 23.8 %collective-permute-start.14 = (bf16[1,1,1,1,1,64,1280]{6,5,4,3,2,1,0:T(8,128)(2,1)}, bf16[1,1,1,1,1,64,1280]{6,5,4,3,2,1,0:T(8,128)(2,1)}, u32[]{:S(2)}, u32[]{:S(2)}) collective-permute-start(bf16[1,1,1,1,1,64,1280]{6,5,4,3,2,1,0:T(8,128)(2,1)} %maximum_bitcast_fusion.1), channel_id=1, source_target_pairs={{0,8},{8,0},{16,24},{24,16},{1,9},{9,1},{17,25},{25,17},{2,10},{10... | collective-permute-start | bytes 491528 | tf_op jit(solution)/shard_map/ppermute | solution.py:301
  42.0 36.2 %collective-permute-start.10 = (bf16[1,2,1,1,1,144,512]{6,5,4,3,2,1,0:T(8,128)(2,1)S(1)}, bf16[1,2,1,1,1,144,512]{6,5,4,3,2,1,0:T(8,128)(2,1)S(1)}, u32[]{:S(2)}, u32[]{:S(2)}) collective-permute-start(bf16[1,2,1,1,1,144,512]{6,5,4,3,2,1,0:T(8,128)(2,1)S(1)} %constant_dynamic-slice_fusion.45), channel_id=1, source_target_pairs={{0,16},{8,24},{16,0},{24,8},{1,17},{9,25},{17,1},{25,9},{2,18},{10... | collective-permute-start | bytes 884744 | tf_op jit(solution)/shard_map/ppermute | solution.py:301
  60.8 24.2 %collective-permute-start.15 = (bf16[1,2,1,1,1,64,1280]{6,5,4,3,2,1,0:T(8,128)(2,1)S(1)}, bf16[1,2,1,1,1,64,1280]{6,5,4,3,2,1,0:T(8,128)(2,1)S(1)}, u32[]{:S(2)}, u32[]{:S(2)}) collective-permute-start(bf16[1,2,1,1,1,64,1280]{6,5,4,3,2,1,0:T(8,128)(2,1)S(1)} %constant_dynamic-slice_fusion.41), channel_id=1, source_target_pairs={{0,16},{8,24},{16,0},{24,8},{1,17},{9,25},{17,1},{25,9},{2,18},{10... | collective-permute-start | bytes 983048 | tf_op jit(solution)/shard_map/ppermute | solution.py:301
  80.7 26.0 %collective-permute-start.3 = (bf16[2,2,2,1,1,64,512]{6,5,4,3,2,1,0:T(8,128)(2,1)S(1)}, bf16[2,2,2,1,1,64,512]{6,5,4,3,2,1,0:T(8,128)(2,1)S(1)}, u32[]{:S(2)}, u32[]{:S(2)}) collective-permute-start(bf16[2,2,2,1,1,64,512]{6,5,4,3,2,1,0:T(8,128)(2,1)S(1)} %constant_dynamic-slice_fusion.47), channel_id=1, source_target_pairs={{0,2},{2,0},{1,3},{3,1},{4,6},{6,4},{5,7},{7,5},{8,10},{10,8},{9,1... | collective-permute-start | bytes 1572872 | tf_op jit(solution)/shard_map/ppermute | solution.py:301
  84.3 39.5 %collective-permute-start.11 = (bf16[2,2,1,1,1,144,512]{6,5,4,3,2,1,0:T(8,128)(2,1)}, bf16[2,2,1,1,1,144,512]{6,5,4,3,2,1,0:T(8,128)(2,1)}, u32[]{:S(2)}, u32[]{:S(2)}) collective-permute-start(bf16[2,2,1,1,1,144,512]{6,5,4,3,2,1,0:T(8,128)(2,1)} %constant_dynamic-slice_fusion.44), channel_id=1, source_target_pairs={{0,2},{2,0},{1,3},{3,1},{4,6},{6,4},{5,7},{7,5},{8,10},{10,8},{9,1... | collective-permute-start | bytes 1769480 | tf_op jit(solution)/shard_map/ppermute | solution.py:301
  87.8 40.9 %collective-permute-start.16 = (bf16[2,2,1,1,1,64,1280]{6,5,4,3,2,1,0:T(8,128)(2,1)}, bf16[2,2,1,1,1,64,1280]{6,5,4,3,2,1,0:T(8,128)(2,1)}, u32[]{:S(2)}, u32[]{:S(2)}) collective-permute-start(bf16[2,2,1,1,1,64,1280]{6,5,4,3,2,1,0:T(8,128)(2,1)} %constant_dynamic-slice_fusion.40), channel_id=1, source_target_pairs={{0,4},{4,0},{1,5},{5,1},{2,6},{6,2},{3,7},{7,3},{8,12},{12,8},{9,1... | collective-permute-start | bytes 1966088 | tf_op jit(solution)/shard_map/ppermute | solution.py:301
  109.9 23.8 %collective-permute-start.4 = (bf16[2,2,2,2,1,64,512]{6,5,4,3,2,1,0:T(8,128)(2,1)}, bf16[2,2,2,2,1,64,512]{6,5,4,3,2,1,0:T(8,128)(2,1)}, u32[]{:S(2)}, u32[]{:S(2)}) collective-permute-start(bf16[2,2,2,2,1,64,512]{6,5,4,3,2,1,0:T(8,128)(2,1)} %constant_dynamic-slice_fusion.46), channel_id=1, source_target_pairs={{0,1},{1,0},{2,3},{3,2},{4,5},{5,4},{6,7},{7,6},{8,9},{9,8},{10,11... | collective-permute-start | bytes 3145736 | tf_op jit(solution)/shard_map/ppermute | solution.py:301
  127.2 35.4 %collective-permute-start.12 = (bf16[2,2,1,2,1,144,512]{6,5,4,3,2,1,0:T(8,128)(2,1)S(1)}, bf16[2,2,1,2,1,144,512]{6,5,4,3,2,1,0:T(8,128)(2,1)S(1)}, u32[]{:S(2)}, u32[]{:S(2)}) collective-permute-start(bf16[2,2,1,2,1,144,512]{6,5,4,3,2,1,0:T(8,128)(2,1)S(1)} %constant_dynamic-slice_fusion.43), channel_id=1, source_target_pairs={{0,4},{4,0},{1,5},{5,1},{2,6},{6,2},{3,7},{7,3},{8,12},{12,8},{9,1... | collective-permute-start | bytes 3538952 | tf_op jit(solution)/shard_map/ppermute | solution.py:301
  132.3 35.4 %collective-permute-start.17 = (bf16[2,2,2,1,1,64,1280]{6,5,4,3,2,1,0:T(8,128)(2,1)S(1)}, bf16[2,2,2,1,1,64,1280]{6,5,4,3,2,1,0:T(8,128)(2,1)S(1)}, u32[]{:S(2)}, u32[]{:S(2)}) collective-permute-start(bf16[2,2,2,1,1,64,1280]{6,5,4,3,2,1,0:T(8,128)(2,1)S(1)} %constant_dynamic-slice_fusion.39), channel_id=1, source_target_pairs={{0,2},{2,0},{1,3},{3,1},{4,6},{6,4},{5,7},{7,5},{8,10},{10,8},{9,1... | collective-permute-start | bytes 3932168 | tf_op jit(solution)/shard_map/ppermute | solution.py:301
  203.3 26.6 %all-to-all-start = ((bf16[16,4,8,768]{3,2,1,0:T(8,128)(2,1)}), bf16[16,4,8,768]{3,2,1,0:T(8,128)(2,1)}, u32[]{:S(2)}, u32[]{:S(2)}) async-start(bf16[16,4,8,768]{3,2,1,0:T(8,128)(2,1)} %fusion.67), calls=%async_computation | async-start | bytes 1572864 | tf_op jit(solution)/shard_map/all_to_all | solution.py:583
  380.4 48.1 %collective-permute-start.23 = (bf16[512,768]{1,0:T(8,128)(2,1)}, bf16[512,768]{1,0:T(8,128)(2,1)}, u32[]{:S(2)}, u32[]{:S(2)}) collective-permute-start(bf16[512,768]{1,0:T(8,128)(2,1)} %fusion.54), channel_id=1, source_target_pairs={{0,2},{2,0},{1,3},{3,1},{4,6},{6,4},{5,7},{7,5},{8,10},{10,8},{9,1... | collective-permute-start | bytes 2359304 | tf_op jit(solution)/shard_map/ppermute | solution.py:301
  413.0 28.0 %collective-permute-start.68 = (bf16[2,2,2,1,96,768]{5,4,3,2,1,0:T(8,128)(2,1)}, bf16[2,2,2,1,96,768]{5,4,3,2,1,0:T(8,128)(2,1)}, u32[]{:S(2)}, u32[]{:S(2)}) collective-permute-start(bf16[2,2,2,1,96,768]{5,4,3,2,1,0:T(8,128)(2,1)} %constant_dynamic-slice_fusion.9), channel_id=1, source_target_pairs={{0,4},{4,0},{1,5},{5,1},{2,6},{6,2},{3,7},{7,3},{8,12},{12,8},{9,1... | collective-permute-start | bytes 3538952 | tf_op jit(solution)/shard_map/ppermute | solution.py:301
  420.3 29.1 %collective-permute-start.72 = (bf16[1,2,2,2,96,768]{5,4,3,2,1,0:T(8,128)(2,1)}, bf16[1,2,2,2,96,768]{5,4,3,2,1,0:T(8,128)(2,1)}, u32[]{:S(2)}, u32[]{:S(2)}) collective-permute-start(bf16[1,2,2,2,96,768]{5,4,3,2,1,0:T(8,128)(2,1)} %constant_dynamic-slice_fusion.5), channel_id=1, source_target_pairs={{0,2},{2,0},{1,3},{3,1},{4,6},{6,4},{5,7},{7,5},{8,10},{10,8},{9,1... | collective-permute-start | bytes 3538952 | tf_op jit(solution)/shard_map/ppermute | solution.py:301
  428.0 24.6 %collective-permute-start.27 = (bf16[2,256,768]{2,1,0:T(8,128)(2,1)S(1)}, bf16[2,256,768]{2,1,0:T(8,128)(2,1)S(1)}, u32[]{:S(2)}, u32[]{:S(2)}) collective-permute-start(bf16[2,256,768]{2,1,0:T(8,128)(2,1)S(1)} %add_convert_fusion.10), channel_id=1, source_target_pairs={{0,1},{1,0},{2,3},{3,2},{4,5},{5,4},{6,7},{7,6},{8,9},{9,8},{10,11... | collective-permute-start | bytes 2359304 | tf_op jit(solution)/shard_map/ppermute | solution.py:301
  431.6 249.8 %collective-permute-start.24 = (bf16[2,2,256,768]{3,2,1,0:T(8,128)(2,1)}, bf16[2,2,256,768]{3,2,1,0:T(8,128)(2,1)}, u32[]{:S(2)}, u32[]{:S(2)}) collective-permute-start(bf16[2,2,256,768]{3,2,1,0:T(8,128)(2,1)} %maximum_select_fusion.4), channel_id=1, source_target_pairs={{0,1},{1,0},{2,3},{3,2},{4,5},{5,4},{6,7},{7,6},{8,9},{9,8},{10,11... | collective-permute-start | bytes 4718600 | tf_op jit(solution)/shard_map/ppermute | solution.py:301
  443.6 176.0 %collective-permute-start.69 = (bf16[1,2,2,1,96,768]{5,4,3,2,1,0:T(8,128)(2,1)}, bf16[1,2,2,1,96,768]{5,4,3,2,1,0:T(8,128)(2,1)}, u32[]{:S(2)}, u32[]{:S(2)}) collective-permute-start(bf16[1,2,2,1,96,768]{5,4,3,2,1,0:T(8,128)(2,1)} %constant_dynamic-slice_fusion.8), channel_id=1, source_target_pairs={{0,2},{2,0},{1,3},{3,1},{4,6},{6,4},{5,7},{7,5},{8,10},{10,8},{9,1... | collective-permute-start | bytes 1769480 | tf_op jit(solution)/shard_map/ppermute | solution.py:301
  451.9 169.3 %collective-permute-start.73 = (bf16[1,2,2,1,96,768]{5,4,3,2,1,0:T(8,128)(2,1)}, bf16[1,2,2,1,96,768]{5,4,3,2,1,0:T(8,128)(2,1)}, u32[]{:S(2)}, u32[]{:S(2)}) collective-permute-start(bf16[1,2,2,1,96,768]{5,4,3,2,1,0:T(8,128)(2,1)} %constant_dynamic-slice_fusion.4), channel_id=1, source_target_pairs={{0,4},{4,0},{1,5},{5,1},{2,6},{6,2},{3,7},{7,3},{8,12},{12,8},{9,1... | collective-permute-start | bytes 1769480 | tf_op jit(solution)/shard_map/ppermute | solution.py:301
  596.8 103.9 %collective-permute-start.60 = (bf16[1,2,2,2,96,768]{5,4,3,2,1,0:T(8,128)(2,1)}, bf16[1,2,2,2,96,768]{5,4,3,2,1,0:T(8,128)(2,1)}, u32[]{:S(2)}, u32[]{:S(2)}) collective-permute-start(bf16[1,2,2,2,96,768]{5,4,3,2,1,0:T(8,128)(2,1)} %constant_dynamic-slice_fusion.17), channel_id=1, source_target_pairs={{0,2},{2,0},{1,3},{3,1},{4,6},{6,4},{5,7},{7,5},{8,10},{10,8},{9,1... | collective-permute-start | bytes 3538952 | tf_op jit(solution)/shard_map/ppermute | solution.py:301
  609.4 58.4 %collective-permute-start.28 = (bf16[2,256,768]{2,1,0:T(8,128)(2,1)}, bf16[2,256,768]{2,1,0:T(8,128)(2,1)}, u32[]{:S(2)}, u32[]{:S(2)}) collective-permute-start(bf16[2,256,768]{2,1,0:T(8,128)(2,1)} %fusion.105), channel_id=1, source_target_pairs={{0,1},{1,0},{2,3},{3,2},{4,5},{5,4},{6,7},{7,6},{8,9},{9,8},{10,11... | collective-permute-start | bytes 2359304 | tf_op jit(solution)/shard_map/ppermute | solution.py:301
  619.6 53.2 %collective-permute-start.30 = (bf16[2,256,768]{2,1,0:T(8,128)(2,1)S(1)}, bf16[2,256,768]{2,1,0:T(8,128)(2,1)S(1)}, u32[]{:S(2)}, u32[]{:S(2)}) collective-permute-start(bf16[2,256,768]{2,1,0:T(8,128)(2,1)S(1)} %fusion.102), channel_id=1, source_target_pairs={{0,1},{1,0},{2,3},{3,2},{4,5},{5,4},{6,7},{7,6},{8,9},{9,8},{10,11... | collective-permute-start | bytes 2359304 | tf_op jit(solution)/shard_map/ppermute | solution.py:301
  652.4 43.7 %collective-permute-start.64 = (bf16[2,2,2,1,96,768]{5,4,3,2,1,0:T(8,128)(2,1)}, bf16[2,2,2,1,96,768]{5,4,3,2,1,0:T(8,128)(2,1)}, u32[]{:S(2)}, u32[]{:S(2)}) collective-permute-start(bf16[2,2,2,1,96,768]{5,4,3,2,1,0:T(8,128)(2,1)} %constant_dynamic-slice_fusion.13), channel_id=1, source_target_pairs={{0,4},{4,0},{1,5},{5,1},{2,6},{6,2},{3,7},{7,3},{8,12},{12,8},{9,1... | collective-permute-start | bytes 3538952 | tf_op jit(solution)/shard_map/ppermute | solution.py:301
  671.4 33.3 %collective-permute-start.29 = (bf16[256,768]{1,0:T(8,128)(2,1)}, bf16[256,768]{1,0:T(8,128)(2,1)}, u32[]{:S(2)}, u32[]{:S(2)}) collective-permute-start(bf16[256,768]{1,0:T(8,128)(2,1)} %fusion.139), channel_id=1, source_target_pairs={{0,2},{2,0},{1,3},{3,1},{4,6},{6,4},{5,7},{7,5},{8,10},{10,8},{9,1... | collective-permute-start | bytes 1179656 | tf_op jit(solution)/shard_map/ppermute | solution.py:301
  676.9 86.2 %all-to-all-start.1 = ((bf16[16,4,8,768]{3,2,1,0:T(8,128)(2,1)}), bf16[16,4,8,768]{3,2,1,0:T(8,128)(2,1)}, u32[]{:S(2)}, u32[]{:S(2)}) async-start(bf16[16,4,8,768]{3,2,1,0:T(8,128)(2,1)} %bitcast.105), calls=%async_computation.1 | async-start | bytes 1572864 | tf_op jit(solution)/shard_map/all_to_all | solution.py:661
  761.8 66.2 %collective-permute-start.82 = (f32[7714]{0:T(1024)}, f32[7714]{0:T(1024)}, u32[]{:S(2)}, u32[]{:S(2)}) collective-permute-start(f32[7714]{0:T(1024)} %add.1104), channel_id=1, source_target_pairs={{0,8},{8,0},{16,24},{24,16},{1,9},{9,1},{17,25},{25,17},{2,10},{10... | collective-permute-start | bytes 92576 | tf_op jit(solution)/shard_map/ppermute | solution.py:301
  786.6 72.1 %collective-permute-start.45 = (bf16[2,2,2,2,1,144,512]{6,5,4,3,2,1,0:T(8,128)(2,1)}, bf16[2,2,2,2,1,144,512]{6,5,4,3,2,1,0:T(8,128)(2,1)}, u32[]{:S(2)}, u32[]{:S(2)}) collective-permute-start(bf16[2,2,2,2,1,144,512]{6,5,4,3,2,1,0:T(8,128)(2,1)} %constant_dynamic-slice_fusion.26), channel_id=1, source_target_pairs={{0,1},{1,0},{2,3},{3,2},{4,5},{5,4},{6,7},{7,6},{8,9},{9,8},{10,11... | collective-permute-start | bytes 7077896 | tf_op jit(solution)/shard_map/ppermute | solution.py:301
  827.4 34.9 %collective-permute-start.50 = (bf16[2,2,2,2,1,64,1280]{6,5,4,3,2,1,0:T(8,128)(2,1)}, bf16[2,2,2,2,1,64,1280]{6,5,4,3,2,1,0:T(8,128)(2,1)}, u32[]{:S(2)}, u32[]{:S(2)}) collective-permute-start(bf16[2,2,2,2,1,64,1280]{6,5,4,3,2,1,0:T(8,128)(2,1)} %fusion.22), channel_id=1, source_target_pairs={{0,1},{1,0},{2,3},{3,2},{4,5},{5,4},{6,7},{7,6},{8,9},{9,8},{10,11... | collective-permute-start | bytes 7864328 | tf_op jit(solution)/shard_map/ppermute | solution.py:301
  862.2 28.2 %collective-permute-start.46 = (bf16[2,2,1,2,1,144,512]{6,5,4,3,2,1,0:T(8,128)(2,1)S(1)}, bf16[2,2,1,2,1,144,512]{6,5,4,3,2,1,0:T(8,128)(2,1)S(1)}, u32[]{:S(2)}, u32[]{:S(2)}) collective-permute-start(bf16[2,2,1,2,1,144,512]{6,5,4,3,2,1,0:T(8,128)(2,1)S(1)} %constant_dynamic-slice_fusion.25), channel_id=1, source_target_pairs={{0,4},{4,0},{1,5},{5,1},{2,6},{6,2},{3,7},{7,3},{8,12},{12,8},{9,1... | collective-permute-start | bytes 3538952 | tf_op jit(solution)/shard_map/ppermute | solution.py:301
  864.9 31.8 %collective-permute-start.51 = (bf16[2,2,2,1,1,64,1280]{6,5,4,3,2,1,0:T(8,128)(2,1)S(1)}, bf16[2,2,2,1,1,64,1280]{6,5,4,3,2,1,0:T(8,128)(2,1)S(1)}, u32[]{:S(2)}, u32[]{:S(2)}) collective-permute-start(bf16[2,2,2,1,1,64,1280]{6,5,4,3,2,1,0:T(8,128)(2,1)S(1)} %constant_dynamic-slice_fusion.21), channel_id=1, source_target_pairs={{0,2},{2,0},{1,3},{3,1},{4,6},{6,4},{5,7},{7,5},{8,10},{10,8},{9,1... | collective-permute-start | bytes 3932168 | tf_op jit(solution)/shard_map/ppermute | solution.py:301
  876.7 36.9 %collective-permute-start.39 = (bf16[1,1,1,1,1,64,512]{6,5,4,3,2,1,0:T(8,128)(2,1)S(1)}, bf16[1,1,1,1,1,64,512]{6,5,4,3,2,1,0:T(8,128)(2,1)S(1)}, u32[]{:S(2)}, u32[]{:S(2)}) collective-permute-start(bf16[1,1,1,1,1,64,512]{6,5,4,3,2,1,0:T(8,128)(2,1)S(1)} %constant_dynamic-slice_fusion.27), channel_id=1, source_target_pairs={{0,8},{8,0},{16,24},{24,16},{1,9},{9,1},{17,25},{25,17},{2,10},{10... | collective-permute-start | bytes 196616 | tf_op jit(solution)/shard_map/ppermute | solution.py:301
  897.1 27.3 %collective-permute-start.52 = (bf16[2,2,1,1,1,64,1280]{6,5,4,3,2,1,0:T(8,128)(2,1)S(1)}, bf16[2,2,1,1,1,64,1280]{6,5,4,3,2,1,0:T(8,128)(2,1)S(1)}, u32[]{:S(2)}, u32[]{:S(2)}) collective-permute-start(bf16[2,2,1,1,1,64,1280]{6,5,4,3,2,1,0:T(8,128)(2,1)S(1)} %constant_dynamic-slice_fusion.20), channel_id=1, source_target_pairs={{0,4},{4,0},{1,5},{5,1},{2,6},{6,2},{3,7},{7,3},{8,12},{12,8},{9,1... | collective-permute-start | bytes 1966088 | tf_op jit(solution)/shard_map/ppermute | solution.py:301
  (238 other events, 3489.2 us)
Sparse Core Ops, SparseCore 0:
  14.7 116.1 all-gather.2
  134.2 87.6 all-gather.4

commit v2 on v1

v2 whole, which is shorter than its diff:
```python
import functools

import jax
import jax.numpy as jnp
from jax import lax
from jax.experimental import pallas as pl
from jax.experimental.pallas import tpu as pltpu
from jax.sharding import Mesh
from jax.sharding import PartitionSpec as P

NB = 32
STEP = 5
NEGATIVE = -1000000000.0
SAFE = 2.0e8
NT = (((1,), (1,)), ((), ()))
NN = (((1,), (0,)), ((), ()))


def mm(a, b, dims=NN):
    return lax.dot_general(a, b, dims, preferred_element_type=jnp.float32)


def column(refs, head, kind, group, size):
    start = (kind * group + head % group) * size
    return refs[head // group].at[:, start : start + size]


def stage_heads(p_refs, kx_ref, tab_ref, q_scr, k_scr, heads, group, size):
    kx = kx_ref[...]
    for h in range(heads):
        mixed = mm(kx, tab_ref[h]).astype(jnp.bfloat16)
        q_scr[h, :, : 256 - size] = mixed[:, : 256 - size]
        q_scr[h, :, 256 - size :] = column(p_refs, h, 0, group, size)[...] * jnp.bfloat16(size**-0.5)
        k_scr[h, :, :128] = kx
        k_scr[h, :, 128 : 256 - size] = kx[:, : 128 - size]
        k_scr[h, :, 256 - size :] = column(p_refs, h, 1, group, size)[...]


def bound_ok(q_scr, k_scr, heads, size):
    big_q, big_k = 0.0, 0.0
    for h in range(heads):
        big_q = jnp.maximum(big_q, jnp.max(jnp.abs(q_scr[h, :, 256 - size :].astype(jnp.float32))))
        big_k = jnp.maximum(big_k, jnp.max(jnp.abs(k_scr[h, :, 256 - size :].astype(jnp.float32))))
    return big_q * big_k * size < SAFE


def window(win_ref, chunk, exact, length, tile):
    if exact:
        return 0, length // tile
    return pl.multiple_of(win_ref[0, chunk], 128), win_ref[1, chunk]


def sweep(count, tile, body, carry):
    carry = lax.fori_loop(0, count // 2, lambda t, c: body(t * 2 * tile, 2 * tile, c), carry)
    return lax.fori_loop(
        0, count % 2, lambda t, c: body(count // 2 * 2 * tile, tile, c), carry
    )


def forward_kernel(*refs, heads, group, size, chunk_rows, tile, beside):
    p_refs = refs[: heads // group]
    (
        win_ref, kx_ref, tab_ref, segc_ref, segr_ref, o_ref, lse_ref,
        q_scr, k_scr, vt_scr, s_scr, ot_scr,
    ) = refs[heads // group :]
    length = kx_ref.shape[0]
    chunks = length // chunk_rows
    stage_heads(p_refs, kx_ref, tab_ref, q_scr, k_scr, heads, group, size)
    for h in range(heads):
        values = column(p_refs, h, 2, group, size)[...]
        vt_scr[h] = values.astype(jnp.float32).T.astype(jnp.bfloat16)
    safe = bound_ok(q_scr, k_scr, heads, size)
    lse_ref[...] = jnp.zeros_like(lse_ref)

    def run(exact):
        def one_chunk(item, _):
            lead, c = (0, item) if beside == heads else (item // chunks * beside, item % chunks)
            start, count = window(win_ref, c, exact, length, tile)
            first = pl.multiple_of(c * chunk_rows, chunk_rows)
            queries = pl.ds(first, chunk_rows)

            def score(at, tile, tops):
                row = pl.multiple_of(at, 128)
                src = pl.multiple_of(start + at, 128)
                found = []
                for u in range(beside):
                    s = mm(k_scr[lead + u, pl.ds(src, tile), :], q_scr[lead + u, queries, :], NT)
                    if exact:
                        s = jnp.where(segc_ref[pl.ds(src, tile), :1] == segr_ref[:, queries], s, NEGATIVE)
                    s_scr[u, pl.ds(row, tile), :] = s
                    found.append(
                        jnp.maximum(tops[u], jnp.max(s.reshape(tile // 8, 8, chunk_rows), axis=0))
                    )
                return tuple(found)

            tops = sweep(
                count, tile, score, (jnp.full((8, chunk_rows), -3.0e38, jnp.float32),) * beside
            )
            tops = [jnp.max(top, axis=0, keepdims=True) for top in tops]
            ot_scr[pl.ds(lead, beside), :, queries] = jnp.zeros((beside, size, chunk_rows), jnp.float32)

            def mix(at, tile, totals):
                row = pl.multiple_of(at, 128)
                src = pl.multiple_of(start + at, 128)
                found = []
                for u in range(beside):
                    p = jnp.exp(s_scr[u, pl.ds(row, tile), :] - tops[u])
                    found.append(totals[u] + jnp.sum(p.reshape(tile // 8, 8, chunk_rows), axis=0))
                    ot_scr[lead + u, :, queries] += mm(
                        vt_scr[lead + u, :, pl.ds(src, tile)], p.astype(jnp.bfloat16)
                    )
                return tuple(found)

            totals = sweep(
                count, tile, mix, (jnp.zeros((8, chunk_rows), jnp.float32),) * beside
            )
            for u in range(beside):
                total = jnp.sum(totals[u], axis=0, keepdims=True)
                lse_ref[pl.ds(lead + u, 1), queries] = tops[u] + jnp.log(total)
                ot_scr[lead + u, :, queries] = ot_scr[lead + u, :, queries] / total
            return 0

        lax.fori_loop(0, heads // beside * chunks, one_chunk, 0)

    pl.when(safe)(functools.partial(run, False))
    pl.when(jnp.logical_not(safe))(functools.partial(run, True))
    for h in range(heads):
        o_ref[:, h * size : (h + 1) * size] = ot_scr[h].T.astype(jnp.bfloat16)


def backward_kernel(*refs, heads, group, size, chunk_rows, tile, offset, beside):
    groups = heads // group
    p_refs, refs = refs[:groups], refs[groups:]
    win_ref, kx_ref, tab_ref, segc_ref, segr_ref, o_ref, lse_ref, g_ref = refs[:8]
    d_refs, span_ref = refs[8 : 8 + groups], refs[8 + groups]
    q_scr, k_scr, kt_scr, v_scr, g_scr, dk_scr, dv_scr, dq_scr, dl_scr = refs[9 + groups :]
    length = kx_ref.shape[0]
    chunks = length // chunk_rows
    stage_heads(p_refs, kx_ref, tab_ref, q_scr, k_scr, heads, group, size)
    safe = bound_ok(q_scr, k_scr, heads, size)
    for h in range(heads):
        kt_scr[h] = k_scr[h, :, 128:].astype(jnp.float32).T.astype(jnp.bfloat16)
        v_scr[h] = column(p_refs, h, 2, group, size)[...]
        g = g_ref[:, offset + h * size : offset + (h + 1) * size]
        g_scr[h] = g
        o = o_ref[:, h * size : (h + 1) * size]
        mixed = g.astype(jnp.float32) * o.astype(jnp.float32)
        dl_scr[pl.ds(h, 1), :] = jnp.sum(mixed.T, axis=0, keepdims=True)
    dk_scr[...] = jnp.zeros_like(dk_scr)
    dv_scr[...] = jnp.zeros_like(dv_scr)
    dq_scr[...] = jnp.zeros_like(dq_scr)

    def run(exact):
        def one_chunk(item, _):
            lead, c = (0, item) if beside == heads else (item // chunks * beside, item % chunks)
            start, count = window(win_ref, c, exact, length, tile)
            first = pl.multiple_of(c * chunk_rows, chunk_rows)
            queries = pl.ds(first, chunk_rows)

            def step(at, tile, _):
                keys = pl.ds(pl.multiple_of(start + at, 128), tile)
                for u in range(beside):
                    h = lead + u
                    g = g_scr[h, queries, :]
                    s = mm(k_scr[h, keys, :], q_scr[h, queries, :], NT)
                    if exact:
                        s = jnp.where(segc_ref[keys, :1] == segr_ref[:, queries], s, NEGATIVE)
                    p = jnp.exp(s - lse_ref[pl.ds(h, 1), queries])
                    dp = mm(v_scr[h, keys, :], g, NT)
                    ds = (p * (dp - dl_scr[pl.ds(h, 1), queries])).astype(jnp.bfloat16)
                    dv_scr[h, keys, :] += mm(p.astype(jnp.bfloat16), g)
                    dk_scr[h, keys, :] += mm(ds, q_scr[h, queries, 256 - size :])
                    dq_scr[h, :, queries] += mm(kt_scr[h, :, keys], ds)
                return 0

            return sweep(count, tile, step, 0)

        lax.fori_loop(0, heads // beside * chunks, one_chunk, 0)

    pl.when(safe)(functools.partial(run, False))
    pl.when(jnp.logical_not(safe))(functools.partial(run, True))
    for h in range(heads):
        own, keys, values = (column(d_refs, h, kind, group, size) for kind in range(3))
        own[...] = (dq_scr[h, 128 - size :, :] * size**-0.5).T.astype(jnp.bfloat16)
        keys[...] = dk_scr[h].astype(jnp.bfloat16)
        values[...] = dv_scr[h].astype(jnp.bfloat16)
        thr = dq_scr[h, : 128 - size, :]
        upper = thr.astype(jnp.bfloat16)
        lower = (thr - upper.astype(jnp.float32)).astype(jnp.bfloat16)
        span_ref[h] = mm(upper, kx_ref[...]) + mm(lower, kx_ref[...])


CHUNK = 256
TILE = 256
VMEM = pltpu.VMEM


def attend_forward(proj, around, size):
    length, total = proj[0].shape
    group = total // (3 * size)
    heads = len(proj) * group
    full = pl.BlockSpec(memory_space=pltpu.VMEM)
    return pl.pallas_call(
        functools.partial(
            forward_kernel, heads=heads, group=group, size=size, chunk_rows=CHUNK, tile=TILE,
            beside=heads,
        ),
        in_specs=[full] * len(proj) + [pl.BlockSpec(memory_space=pltpu.SMEM)] + [full] * 4,
        out_specs=[full, full],
        out_shape=[
            jax.ShapeDtypeStruct((length, heads * size), jnp.bfloat16),
            jax.ShapeDtypeStruct((8, length), jnp.float32),
        ],
        scratch_shapes=[
            VMEM((heads, length, 256), jnp.bfloat16),
            VMEM((heads, length, 256), jnp.bfloat16),
            VMEM((heads, size, length), jnp.bfloat16),
            VMEM((heads, length, CHUNK), jnp.float32),
            VMEM((heads, size, length), jnp.float32),
        ],
        compiler_params=pltpu.CompilerParams(vmem_limit_bytes=48 * 1024 * 1024),
        cost_estimate=pl.CostEstimate(flops=0, bytes_accessed=0, transcendentals=0),
    )(*proj, *around)


def attend_backward(proj, around, out, lse, grads, stream, size):
    length, total = proj[0].shape
    group = total // (3 * size)
    heads = len(proj) * group
    full = pl.BlockSpec(memory_space=pltpu.VMEM)
    found = pl.pallas_call(
        functools.partial(
            backward_kernel, heads=heads, group=group, size=size, chunk_rows=CHUNK, tile=TILE,
            offset=stream * heads * size, beside=heads,
        ),
        in_specs=[full] * len(proj) + [pl.BlockSpec(memory_space=pltpu.SMEM)] + [full] * 7,
        out_specs=[full] * (len(proj) + 1),
        out_shape=[jax.ShapeDtypeStruct((length, total), jnp.bfloat16)] * len(proj)
        + [jax.ShapeDtypeStruct((heads, 128 - size, 128), jnp.float32)],
        scratch_shapes=[
            VMEM((heads, length, 256), jnp.bfloat16),
            VMEM((heads, length, 256), jnp.bfloat16),
            VMEM((heads, 128, length), jnp.bfloat16),
            VMEM((heads, length, size), jnp.bfloat16),
            VMEM((heads, length, size), jnp.bfloat16),
            VMEM((heads, length, size), jnp.float32),
            VMEM((heads, length, size), jnp.float32),
            VMEM((heads, 128, length), jnp.float32),
            VMEM((8, length), jnp.float32),
        ],
        compiler_params=pltpu.CompilerParams(vmem_limit_bytes=56 * 1024 * 1024),
        cost_estimate=pl.CostEstimate(flops=0, bytes_accessed=0, transcendentals=0),
    )(*proj, *around, out, lse, grads)
    return found[:-1], found[-1]


def attention_windows(segment_row, chunk_rows, tile):
    length = segment_row.shape[0]
    heads_of = segment_row[::chunk_rows]
    tails_of = segment_row[chunk_rows - 1 :: chunk_rows]
    low = jnp.sum((segment_row[None, :] < heads_of[:, None]).astype(jnp.int32), axis=1)
    high = jnp.sum((segment_row[None, :] <= tails_of[:, None]).astype(jnp.int32), axis=1)
    start = low // 128 * 128
    count = (high - start + tile - 1) // tile
    start = jnp.minimum(start, length - count * tile)
    return jnp.stack([start, count]).astype(jnp.int32)


def attention_tables(span_tables):
    _, heads, buckets, _ = span_tables.shape
    upper = lax.reduce_precision(span_tables, 8, 7)
    lower = (span_tables - upper).astype(jnp.bfloat16)
    def diag(t):
        z = jnp.zeros_like(t[0])
        return jnp.concatenate([jnp.concatenate([t[0], z], 2), jnp.concatenate([z, t[1]], 2)], 1)
    hi, lo = diag(upper.astype(jnp.bfloat16)), diag(lower)
    level = jnp.arange(64)
    away = jnp.where((level[:, None] != level[None, :]), NEGATIVE, 0.0)
    segs = jnp.where((level[:, None] < 4) & (level[None, :] < 4), away, 0.0).astype(jnp.bfloat16)
    segs = jnp.broadcast_to(segs[None], (heads, 64, 64))
    zero = jnp.zeros((heads, 64, 64), jnp.bfloat16)
    top = jnp.concatenate([hi, zero, lo, zero], 2)
    bottom = jnp.concatenate([zero, segs, zero, zero], 2)
    return jnp.concatenate([top, bottom], 1)


def token_marks(boxes_page, segment_row, buckets):
    levels = jnp.arange(buckets, dtype=jnp.int32)[None, :]
    kinds = jnp.arange(64, dtype=jnp.int32)[None, :]
    return jnp.concatenate(
        [boxes_page[0][:, None] == levels, boxes_page[1][:, None] == levels, segment_row[:, None] == kinds],
        axis=1,
    ).astype(jnp.bfloat16)


NORM_EPS = 1e-05
RELATIVE = 0.5
RATE_FLOOR = 0.001
PRECISE = lax.Precision.HIGHEST
LOW = jnp.bfloat16
WIDE = jnp.float32
AXES = ("dz", "dx", "my", "core")
DP = ("dz", "dx")
MP = ("my", "core")
CHIPS = ("dz", "dx", "my")
OWNERS = ("my", "dz", "dx")
FORWARD_TAPS = tuple((col, row) for col in range(3) for row in range(3))
BACKWARD_TAPS = tuple((2 - col, 2 - row) for col in range(3) for row in range(3))


def swap(values, axis, reach):
    count = lax.axis_size(axis)
    return lax.ppermute(values, axis, [(i, i ^ reach) for i in range(count)])


def exchange(values, flips):
    if len({axis for axis, _ in flips}) == 1:
        return swap(values, flips[0][0], sum(reach for _, reach in flips))
    (one, far), (two, near) = flips
    count = lax.axis_size(two)
    pairs = [
        (i * count + k, (i ^ far) * count + (k ^ near))
        for i in range(lax.axis_size(one))
        for k in range(count)
    ]
    return lax.ppermute(values, (one, two), pairs)


def bits_of(axis):
    reach, found = lax.axis_size(axis) // 2, []
    while reach:
        found.append((axis, reach))
        reach //= 2
    return found


def bits(axes):
    return [bit for axis in axes for bit in bits_of(axis)]


def rounds_of(order):
    found = []
    for axes in order:
        places = bits(axes)
        found += [tuple(places[n : n + 2]) for n in range(0, len(places), 2)]
    return found


def flips_of(group):
    return [(bit,) for bit in group] + ([group] if len(group) == 2 else [])


def side(bit):
    return lax.axis_index(bit[0]) // bit[1] % 2


def tie(values, *after):
    if not after:
        return values
    return lax.optimization_barrier((values,) + after)[0]


class Gather:
    def __init__(self, shard, order, owners):
        self.places = bits(owners)
        self.rounds = rounds_of(order)[::-1]
        self.sides = [side(place) for place in self.places]
        self.shape = shard.shape
        self.done = []
        self.held = shard.reshape((1,) * len(self.places) + shard.shape)
        whole = jnp.zeros((2,) * len(self.places) + shard.shape, shard.dtype)
        self.whole = lax.dynamic_update_slice(whole, self.held, self.corner())

    def corner(self, flips=()):
        return [
            0 if place in self.done else (1 - mine if place in flips else mine)
            for place, mine in zip(self.places, self.sides)
        ] + [0] * len(self.shape)

    def step(self, before=(), fill=()):
        group = self.rounds.pop()
        sent = tie(self.held, *before)
        arrived = []
        for flips in flips_of(group):
            got = tie(exchange(sent, flips), *fill)
            self.whole = lax.dynamic_update_slice(self.whole, got, self.corner(flips))
            arrived.append(got)
        self.done += group
        if self.rounds:
            sizes = [2 if place in self.done else 1 for place in self.places] + list(self.shape)
            self.held = lax.dynamic_slice(self.whole, self.corner(), sizes)
        return tuple(arrived)

    def value(self):
        return self.whole.reshape((-1,) + self.shape[1:])


class Scatter:
    def __init__(self, blocks, order, owners, axis=0):
        self.live = bits(owners)
        self.count = len(self.live)
        self.rounds = rounds_of(order)[::-1]
        self.parts = [value.reshape((2,) * self.count + (-1,) + value.shape[1:]) for value in blocks]
        self.axis = self.count + axis
        self.held = None
        self.busy = False

    def pick(self, group, flips):
        def cut(value):
            for bit in group:
                mine = side(bit)
                place = 1 - mine if bit in flips else mine
                value = lax.dynamic_slice_in_dim(value, place, 1, self.live.index(bit))
            return value

        if self.held is None:
            return jnp.concatenate([cut(value) for value in self.parts], axis=self.axis)
        return sum(cut(value).astype(WIDE) for value in self.held).astype(LOW)

    def send(self, *after):
        group = self.rounds.pop()
        self.flying = tuple(
            exchange(tie(self.pick(group, flips), *after), flips) for flips in flips_of(group)
        )
        self.kept = self.pick(group, ())
        for bit in group:
            self.live[self.live.index(bit)] = None
        self.busy = True
        return self

    def take(self, *after):
        if self.busy:
            flying = lax.optimization_barrier(self.flying + after)[: len(self.flying)]
            self.held = [self.kept] + list(flying)
            self.busy = False
        return self

    def step(self, *after):
        self.take(*after)
        return self.send() if self.rounds else self

    def land(self, values):
        found = lax.optimization_barrier((values,) + self.flying)
        self.held = [self.kept] + list(found[1:])
        self.busy = False
        if self.rounds:
            self.send()
        return found[0]

    def value(self):
        total = sum(value.astype(WIDE) for value in self.held)
        return total.reshape(total.shape[self.count :])


def total_over(values, axes):
    for bit in bits(axes):
        values = values + swap(values, *bit)
    return values


def by_side(bit, own, other, axis):
    return jnp.where(
        side(bit) == 0, jnp.stack([own, other], axis), jnp.stack([other, own], axis)
    )


def own_quarters(page, quarter):
    parts = page.reshape((-1, 2, quarter) + page.shape[1:])
    own = lax.dynamic_index_in_dim(parts, lax.axis_index("core"), 1, keepdims=False)
    return own.reshape((-1,) + page.shape[1:])


def add_both(partial, quarter, *after):
    parts = partial.reshape((-1, 2, quarter) + partial.shape[1:])
    core = lax.axis_index("core")
    sent = lax.dynamic_index_in_dim(parts, 1 - core, 1, keepdims=False)
    kept = lax.dynamic_index_in_dim(parts, core, 1, keepdims=False)
    got = tie(swap(sent.astype(LOW), "core", 1), *after)
    return (kept + got.astype(WIDE)).reshape((-1,) + partial.shape[1:])


def extended(cells, sides, width):
    for axis, dim in sides:
        count = lax.axis_size(axis)
        ends = count - 1
        head = lax.slice_in_dim(cells, 0, width, axis=dim)
        tail = lax.slice_in_dim(cells, cells.shape[dim] - width, cells.shape[dim], axis=dim)
        cells = jnp.concatenate(
            [
                lax.ppermute(tail, axis, [(i, i + 1) for i in range(ends)]),
                cells,
                lax.ppermute(head, axis, [(i + 1, i) for i in range(ends)]),
            ],
            axis=dim,
        )
    return cells


def smooth(values):
    return jax.nn.gelu(values, approximate=True)


def smooth_back(values, upstream):
    return jax.vjp(smooth, values)[1](upstream)[0]


def row_mean(values):
    return jnp.mean(values, axis=-1, keepdims=True)


def first_norm_kernel(text_ref, visual_ref, mine_ref, other_ref, params_ref, hat_ref, scale_ref, low_ref):
    first = text_ref[...].astype(WIDE) + visual_ref[...].astype(WIDE)
    first = first + (mine_ref[...].astype(WIDE) + other_ref[...].astype(WIDE))
    centre = first - row_mean(first)
    scale = lax.rsqrt(row_mean(centre * centre) + NORM_EPS)
    hat = centre * scale
    hat_ref[...] = hat
    scale_ref[...] = scale
    low_ref[...] = (hat * params_ref[0:1, :] + params_ref[1:2, :]).astype(LOW)


def second_norm_kernel(hat_ref, mine_ref, other_ref, upstream_ref, params_ref, out_ref, grad_ref, low_ref, sums_ref):
    normed = hat_ref[...] * params_ref[0:1, :] + params_ref[1:2, :]
    down = mine_ref[...].astype(WIDE) + other_ref[...].astype(WIDE)
    second = normed + (down + params_ref[4:5, :])
    centre = second - row_mean(second)
    scale = lax.rsqrt(row_mean(centre * centre) + NORM_EPS)
    hat = centre * scale
    out_ref[...] = (hat * params_ref[2:3, :] + params_ref[3:4, :]).astype(LOW)
    upstream = upstream_ref[...].astype(WIDE)
    inner = upstream * params_ref[2:3, :]
    grad = scale * (inner - row_mean(inner) - hat * row_mean(inner * hat))
    grad_ref[...] = grad
    low = grad.astype(LOW)
    low_ref[...] = low
    sums_ref[0:1, :] += jnp.sum(upstream * hat, axis=0, keepdims=True)
    sums_ref[1:2, :] += jnp.sum(upstream, axis=0, keepdims=True)
    sums_ref[2:3, :] += jnp.sum(low.astype(WIDE), axis=0, keepdims=True)


def first_back_kernel(grad_ref, mine_ref, other_ref, hat_ref, scale_ref, params_ref, first_ref, low_ref, sums_ref):
    upstream = grad_ref[...] + (mine_ref[...].astype(WIDE) + other_ref[...].astype(WIDE))
    hat = hat_ref[...]
    inner = upstream * params_ref[0:1, :]
    grad = scale_ref[...] * (inner - row_mean(inner) - hat * row_mean(inner * hat))
    first_ref[...] = grad
    low_ref[...] = grad.astype(LOW)
    sums_ref[0:1, :] += jnp.sum(upstream * hat, axis=0, keepdims=True)
    sums_ref[1:2, :] += jnp.sum(upstream, axis=0, keepdims=True)


def row_kernel(kernel, rows, given, made):
    length = given[0].shape[0]
    shapes = [value.shape for value in given] + [shape for shape, _ in made]

    def body(*refs):
        def block(number, _):
            here = pl.ds(pl.multiple_of(number * rows, rows), rows)
            kernel(*(ref.at[here] if shape[0] == length else ref for ref, shape in zip(refs, shapes)))
            return 0

        for ref, shape in zip(refs[len(given) :], shapes[len(given) :]):
            if shape[0] != length:
                ref[...] = jnp.zeros_like(ref)
        lax.fori_loop(0, length // rows, block, 0)

    whole = pl.BlockSpec(memory_space=pltpu.VMEM)
    return pl.pallas_call(
        body,
        in_specs=[whole] * len(given),
        out_specs=[whole] * len(made),
        out_shape=[jax.ShapeDtypeStruct(shape, kind) for shape, kind in made],
        compiler_params=pltpu.CompilerParams(vmem_limit_bytes=32 * 1024 * 1024),
        cost_estimate=pl.CostEstimate(flops=0, bytes_accessed=0, transcendentals=0),
    )(*given)


def relative_select(buckets, reach_max):
    offsets = (
        jnp.arange(buckets, dtype=jnp.int32)[None, :]
        - jnp.arange(buckets, dtype=jnp.int32)[:, None]
    )
    clipped = jnp.clip(offsets, -reach_max, reach_max) + reach_max
    return (
        clipped[:, :, None] == jnp.arange(2 * reach_max + 1, dtype=jnp.int32)[None, None, :]
    ).astype(WIDE)


def stacked_taps(padded, across, downward, anchors):
    return jnp.concatenate(
        [
            padded[:, from_col : from_col + across, from_row : from_row + downward, :]
            for from_col, from_row in anchors
        ],
        axis=-1,
    )


def dot(left, right, dims="nn"):
    first = 0 if dims[0] == "t" else 1
    second = 1 if dims[1] == "t" else 0
    return lax.dot_general(
        left, right, (((first,), (second,)), ((), ())), preferred_element_type=WIDE
    )


def factored_step(weight, gradient, rows_old, cols_old, row_piece, col_piece, row_mean, weight_mean, sizes):
    decay_rate = 1.0 - STEP ** (-0.8)
    rows_next = decay_rate * rows_old + (1.0 - decay_rate) * row_piece / sizes[1]
    cols_next = decay_rate * cols_old + (1.0 - decay_rate) * col_piece / sizes[0]
    second = rows_next[..., :, None] * cols_next[..., None, :] / row_mean[..., None, None]
    step_rate = RELATIVE * jnp.maximum(RATE_FLOOR, jnp.sqrt(weight_mean))
    weight_next = weight - step_rate[..., None, None] * (gradient * lax.rsqrt(second))
    return (gradient, weight_next, rows_next, cols_next, weight_next.astype(LOW))


def moment_step(parameter, gradient, moment, reduce_axes):
    decay_rate = 1.0 - STEP ** (-0.8)
    moment_next = decay_rate * moment + (1.0 - decay_rate) * gradient * gradient
    rms_value = jnp.sqrt(jnp.mean(parameter * parameter, axis=reduce_axes, keepdims=True))
    return (
        gradient,
        moment_next,
        parameter
        - RELATIVE * jnp.maximum(RATE_FLOOR, rms_value) * gradient * lax.rsqrt(moment_next),
    )


def pack(parts):
    flat = [part.reshape(-1) for part in parts]
    return jnp.concatenate(
        [jnp.pad(part, (0, -part.size % 1024)).reshape(-1, 8, 128) for part in flat]
    )


def unpack(packed, like):
    found, cursor = [], 0
    for part in like:
        tiles = -(-part.size // 1024)
        flat = packed[cursor : cursor + tiles].reshape(-1)
        found.append(flat[: part.size].reshape(part.shape))
        cursor += tiles
    return found


def join(parts):
    return jnp.concatenate([part.reshape(-1) for part in parts])


def split(flat, like):
    found, cursor = [], 0
    for part in like:
        found.append(flat[cursor : cursor + part.size].reshape(part.shape))
        cursor += part.size
    return found


def on_device(
    image, text, cotangent, segments, boxes,
    reduce_weight, reduce_weight_rows, reduce_weight_cols,
    spatial_weight, spatial_weight_rows, spatial_weight_cols,
    expand_weight, expand_weight_rows, expand_weight_cols,
    visual_proj, visual_proj_rows, visual_proj_cols,
    attn_in, attn_in_rows, attn_in_cols,
    attn_out, attn_out_rows, attn_out_cols,
    ffn_up, ffn_up_rows, ffn_up_cols,
    ffn_down, ffn_down_rows, ffn_down_cols,
    norm_params, norm_moment, up_bias, up_moment, tables, table_moment,
):
    dp_count = lax.axis_size(DP)
    pair = lax.axis_size("my")
    mp_count = 2 * pair
    my, core = lax.axis_index("my"), lax.axis_index("core")
    mp_index = lax.axis_index(MP)
    length, width = text.shape[1:]
    quarter = length // mp_count
    heads = tables.shape[2]
    size = width // heads
    group = heads // mp_count
    part = group * size
    units = ffn_up.shape[1]
    pages, across, down, channels = image.shape
    middle = spatial_weight.shape[1]

    flat_in = attn_in.astype(LOW).transpose(2, 0, 1, 3).reshape(attn_in.shape[2], 2, 3 * part)
    flat_out = attn_out.astype(LOW).transpose(2, 0, 1)
    layer_in = [
        jnp.concatenate([flat_in[:, stream], flat_out[:, stream]], axis=1) for stream in range(2)
    ]
    layer_ffn = jnp.concatenate([ffn_up.astype(LOW), ffn_down.astype(LOW).T], axis=1)
    base = visual_proj.shape[0]
    spatial_low = spatial_weight.astype(LOW)
    blocks, extra = divmod(spatial_low.shape[0], base)
    section_low = [spatial_low[n * base : (n + 1) * base] for n in range(blocks)]
    section_low.append(spatial_low[blocks * base :].reshape(base, -1))
    section_low.append(expand_weight.astype(LOW).reshape(base, middle))
    section_low.append(visual_proj.astype(LOW))
    section_low.append(reduce_weight.astype(LOW))
    section_low = jnp.concatenate(section_low, axis=1)
    section_whole = lax.all_gather(section_low, AXES, axis=0, tiled=True)
    ffn_whole = lax.all_gather(layer_ffn, OWNERS, axis=0, tiled=True).reshape(pair, width, -1)
    old_weights = (reduce_weight, spatial_weight, expand_weight, visual_proj, attn_in, attn_out, ffn_up, ffn_down)
    old_rows = (
        reduce_weight_rows, spatial_weight_rows, expand_weight_rows, visual_proj_rows,
        attn_in_rows, attn_out_rows, ffn_up_rows, ffn_down_rows,
    )
    copies = (1, 1, 1, 1, mp_count, dp_count, mp_count, dp_count)
    halves = [Gather(half, (("dz",), ("dx", "my")), OWNERS) for half in layer_in]
    while len(halves[0].rounds) > 1:
        for half in halves:
            half.step()
    old_parts = [jnp.sum(weight * weight, axis=(-2, -1)) for weight in old_weights]
    old_parts += [jnp.sum(rows, axis=-1) / times for rows, times in zip(old_rows, copies)]
    old_sums = join(old_parts)

    section_whole = section_whole.reshape(dp_count * mp_count, base, -1)
    ends = [blocks * middle, extra * middle // base, middle, width, middle]
    ends = [sum(ends[: n + 1]) for n in range(len(ends))]
    weight_reduce = section_whole[:, :, ends[3] :].reshape(channels, middle)
    halves[0].step()
    first_wait = (halves[0].whole, old_sums)
    reduced = jnp.einsum(
        "pwhc,cd->pwhd",
        tie(image, *first_wait),
        weight_reduce,
        preferred_element_type=WIDE,
    )
    hidden_one = smooth(reduced).astype(LOW)
    beside = extended(hidden_one, ((DP, 2),), 1)
    section_whole = tie(section_whole, hidden_one)
    weight_spatial = [section_whole[:, :, n * middle : (n + 1) * middle] for n in range(blocks)]
    weight_spatial.append(
        section_whole[:, :, ends[0] : ends[1]].reshape(dp_count * mp_count, extra, middle)
    )
    weight_spatial = jnp.concatenate(weight_spatial, axis=1).reshape(-1, middle)
    weight_expand = section_whole[:, :, ends[1] : ends[2]].reshape(middle, channels)
    weight_proj = section_whole[:, :, ends[2] : ends[3]].reshape(channels, width)
    padded = extended(beside, ((MP, 1),), 1)
    tap_stack = stacked_taps(tie(padded, weight_spatial), across, down, FORWARD_TAPS)
    convolved = jnp.einsum("pwhk,kd->pwhd", tap_stack, weight_spatial, preferred_element_type=WIDE)
    hidden_two = smooth(convolved).astype(LOW)
    expanded = jnp.einsum("pwhc,cd->pwhd", hidden_two, weight_expand, preferred_element_type=WIDE)
    summed_pre = image.astype(WIDE) + expanded
    feature_low = smooth(summed_pre).astype(LOW)
    visual_rows = jnp.einsum(
        "pwhc,cd->pwhd", feature_low, weight_proj, preferred_element_type=WIDE
    ).astype(LOW)
    attn_text = halves[0].value().reshape(pair, width, 4 * part)

    bucket_select = relative_select(NB, (tables.shape[1] - 1) // 2)
    own_tables = tables.reshape(tables.shape[:2] + (pair, 2, group))
    own_tables = lax.dynamic_index_in_dim(own_tables, core, 3, keepdims=False).reshape(
        tables.shape[:2] + (pair * group,)
    )
    span_tables = jnp.einsum("abr,trh->thab", bucket_select, own_tables, precision=PRECISE)
    head_tables = attention_tables(span_tables)
    page_segments = lax.dynamic_index_in_dim(segments, my, 0, keepdims=False)
    page_boxes = lax.dynamic_index_in_dim(boxes, my, 0, keepdims=False)
    marks = token_marks(page_boxes, page_segments, NB)
    windows = attention_windows(page_segments, CHUNK, TILE)
    segment_cols = jnp.broadcast_to(page_segments[:, None], (length, 128))
    around = (windows, marks, head_tables, segment_cols, page_segments[None])
    text_page = lax.dynamic_index_in_dim(text, my, 0, keepdims=False)
    upstream_page = lax.dynamic_index_in_dim(cotangent, my, 0, keepdims=False)

    weight_up = [ffn_whole[y, :, :units] for y in range(pair)]
    weight_down = [ffn_whole[y, :, units:] for y in range(pair)]

    visual_own = lax.all_to_all(visual_rows, CHIPS, split_axis=0, concat_axis=0, tiled=True)

    text_source = tie(text_page, visual_rows)
    weight_in = [[attn_text[y, :, : 3 * part] for y in range(pair)]]
    projected_text = [dot(text_source, weight).astype(LOW) for weight in weight_in[0]]
    attended_text, logs_text = attend_forward(projected_text, around, size)
    halves[1].step((), (attended_text,))
    attn_visual = halves[1].value().reshape(pair, width, 4 * part)
    weight_in.append([attn_visual[y, :, : 3 * part] for y in range(pair)])
    weight_out = jnp.concatenate(
        [whole[y, :, 3 * part :] for whole in (attn_text, attn_visual) for y in range(pair)], axis=1
    )
    visual_own = (
        tie(visual_own, attended_text)
        .reshape(dp_count, pair, across, down, width)
        .transpose(1, 2, 0, 3, 4)
        .reshape(pair, quarter, width)
    )
    visual_page = by_side(("core", 1), visual_own, swap(visual_own, "core", 1), 1)
    visual_page = visual_page.reshape(length, width)
    projected_visual = [dot(visual_page, weight).astype(LOW) for weight in weight_in[1]]
    attended_visual, logs_visual = attend_forward(projected_visual, around, size)
    attended = jnp.concatenate([attended_text, attended_visual], axis=1)
    attention = dot(attended, weight_out, "nt").astype(LOW)
    hat_one, scale_one, normed_low = row_kernel(
        first_norm_kernel,
        256,
        (text_page, visual_page, attention, swap(attention, "core", 1), norm_params),
        (((length, width), WIDE), ((length, 1), WIDE), ((length, width), LOW)),
    )
    own_bias = lax.dynamic_index_in_dim(up_bias.reshape(pair, 2, units), core, 1, keepdims=False)
    hidden_pre = [dot(normed_low, weight_up[y]) + own_bias[y] for y in range(pair)]
    hidden_low = [smooth(pre).astype(LOW) for pre in hidden_pre]
    down_part = sum(dot(hidden_low[y], weight_down[y], "nt") for y in range(pair)).astype(LOW)
    out_page, second_grad, down_low, second_sums = row_kernel(
        second_norm_kernel,
        256,
        (hat_one, down_part, swap(down_part, "core", 1), upstream_page, norm_params),
        (((length, width), LOW), ((length, width), WIDE), ((length, width), LOW), ((8, width), WIDE)),
    )

    out_own = own_quarters(out_page, quarter).reshape(pair, quarter, width)
    out_got = swap(out_own, "my", 1)

    hidden_grad_low = [
        smooth_back(hidden_pre[y], dot(down_low, weight_down[y])).astype(LOW) for y in range(pair)
    ]
    normed_part = sum(dot(hidden_grad_low[y], weight_up[y], "nt") for y in range(pair)).astype(LOW)
    up_part = jnp.stack([jnp.sum(part_low.astype(WIDE), axis=0) for part_low in hidden_grad_low])
    normed_other = swap(normed_part, "core", 1)
    ffn_parts = []
    for y in range(pair):
        ffn_parts.append(dot(normed_low, hidden_grad_low[y], "tn").astype(LOW))
        ffn_parts.append(dot(down_low, hidden_low[y], "tn").astype(LOW))
    normed_other = tie(normed_other, *ffn_parts)
    ffn_grad = jnp.concatenate(ffn_parts).reshape(pair, 2, dp_count, -1, units)
    ffn_grad = ffn_grad.transpose(0, 2, 1, 3, 4).reshape(-1, units)
    ffn_shard = lax.psum_scatter(ffn_grad, OWNERS, scatter_dimension=0, tiled=True).astype(WIDE)
    first_grad, attention_low, first_sums = row_kernel(
        first_back_kernel,
        256,
        (second_grad, normed_part, normed_other, hat_one, scale_one, norm_params),
        (((length, width), WIDE), ((length, width), LOW), ((8, width), WIDE)),
    )
    norm_part = jnp.concatenate([first_sums[:2], second_sums[:3]])
    norm_part = norm_part * (core == 0).astype(WIDE)
    head_grads = dot(attention_low, weight_out).astype(LOW)
    out_got = tie(out_got, head_grads)
    out_other = swap(out_got, "core", 1)
    grad_out = dot(attention_low, attended, "tn").astype(LOW)

    def attention_grads(stream, source, grads):
        found = []
        for y in range(pair):
            place = (stream * pair + y) * part
            own = [dot(source, grads[y], "tn").astype(LOW), grad_out[:, place : place + part]]
            found.append(jnp.concatenate(own, axis=1))
        return jnp.concatenate(found)

    def source_part(stream, grads):
        return sum(dot(grads[y], weight_in[stream][y], "nt") for y in range(pair))

    visual_back, span_visual = attend_backward(
        projected_visual, around, attended_visual, logs_visual, tie(head_grads, grad_out), 1, size
    )
    first_own = own_quarters(first_grad, quarter)
    visual_own_grad = add_both(source_part(1, visual_back), quarter)
    visual_low = (first_own + visual_own_grad).astype(LOW)
    out_other = by_side(("core", 1), out_got, tie(out_other, visual_low), 1)
    out_local = by_side(("my", 1), out_page.reshape(out_other.shape), out_other, 0)
    out_local = out_local.reshape(text.shape)
    visual_sent = (
        visual_low.reshape(pair, across, dp_count, down, width)
        .transpose(2, 0, 1, 3, 4)
        .reshape(pages, across, down, width)
    )
    visual_grad = lax.all_to_all(visual_sent, CHIPS, split_axis=0, concat_axis=0, tiled=True)
    grad_one = attention_grads(1, tie(visual_page, visual_sent), visual_back)
    sum_one = Scatter([grad_one], (("dx",), ("my",), ("dz",)), OWNERS).send()
    text_grads, span_text = attend_backward(
        projected_text, around, attended_text, logs_text, tie(head_grads, grad_one), 0, size
    )
    grad_text = attention_grads(0, text_page, text_grads)
    sum_two = Scatter([grad_text], (("my",), ("dx",), ("dz",)), OWNERS).send()
    visual_grad = sum_one.land(tie(visual_grad, grad_text))

    feature_grad = jnp.einsum("pwhd,cd->pwhc", visual_grad, weight_proj, preferred_element_type=WIDE)
    pre_grad = smooth_back(summed_pre, feature_grad)
    expanded_low = pre_grad.astype(LOW)
    conv_grad = smooth_back(
        convolved,
        jnp.einsum("pwhd,cd->pwhc", expanded_low, weight_expand, preferred_element_type=WIDE),
    ).astype(LOW)
    back_beside = extended(conv_grad, ((DP, 2),), 1)
    grad_proj = dot(
        feature_low.reshape(-1, channels), tie(visual_grad, conv_grad).reshape(-1, width), "tn"
    ).astype(LOW)
    grad_expand = dot(
        hidden_two.reshape(-1, middle), tie(expanded_low, grad_proj).reshape(-1, channels), "tn"
    )
    grad_expand = grad_expand.astype(LOW).reshape(-1, middle)
    back_beside = sum_two.land(tie(back_beside, grad_expand))
    back_padded = extended(back_beside, ((MP, 1),), 1)
    sum_side = Scatter(
        [grad_expand, grad_proj], (("core",), ("dx",), ("my",), ("dz",)), AXES, 1
    ).send()
    back_padded = sum_one.land(back_padded)
    back_taps = stacked_taps(back_padded, across, down, BACKWARD_TAPS).reshape(
        conv_grad.shape[:3] + (9, middle)
    )
    reduced_grad = smooth_back(
        reduced,
        jnp.einsum(
            "pwhko,kio->pwhi",
            back_taps,
            weight_spatial.reshape(9, middle, middle),
            preferred_element_type=WIDE,
        ),
    ).astype(LOW)
    grad_spatial = dot(
        tap_stack.reshape(-1, 9 * middle), sum_side.land(tie(conv_grad, reduced_grad)).reshape(-1, middle), "tn"
    ).astype(LOW)
    grad_reduce = dot(
        image.reshape(-1, channels),
        sum_two.land(tie(reduced_grad, grad_spatial)).reshape(-1, middle),
        "tn",
    ).astype(LOW)
    sum_last = Scatter(
        [grad_spatial, grad_reduce], (("core",), ("dx", "my"), ("dz",)), AXES
    ).send()
    reduced_grad = sum_one.land(tie(reduced_grad, grad_reduce))
    image_grad_local = pre_grad + jnp.einsum(
        "pwhd,cd->pwhc", reduced_grad, weight_reduce, preferred_element_type=WIDE
    )
    text_grads = [sum_last.land(tie(text_grads[0], image_grad_local))] + list(text_grads[1:])
    text_part = source_part(0, text_grads)
    text_own = first_own + add_both(sum_side.land(text_part), quarter)
    text_back = text_own.reshape(pair, quarter, width)
    text_sent = lax.dynamic_index_in_dim(text_back, 1 - my, 0, keepdims=False)
    text_kept = lax.dynamic_index_in_dim(text_back, my, 0, keepdims=False)
    text_grad_local = by_side(
        ("my", 1), text_kept, swap(text_sent.astype(LOW), "my", 1).astype(WIDE), 0
    )
    for tree in (sum_two, sum_one):
        while tree.rounds:
            tree.step(text_own)
        tree.take(text_own)

    up_shard, down_shard = jnp.split(ffn_shard, 2)
    one_shard, two_shard = sum_one.value(), sum_two.value()
    in_shard = jnp.stack([two_shard[:, : 3 * part], one_shard[:, : 3 * part]])
    in_shard = in_shard.reshape(2, -1, 3, part).transpose(0, 2, 1, 3)
    out_shard = jnp.stack([two_shard[:, 3 * part :], one_shard[:, 3 * part :]]).transpose(0, 2, 1)
    image_sets = (
        (reduce_weight, reduce_weight_rows, reduce_weight_cols),
        (spatial_weight, spatial_weight_rows, spatial_weight_cols),
        (expand_weight, expand_weight_rows, expand_weight_cols),
        (visual_proj, visual_proj_rows, visual_proj_cols),
    )
    layer_sets = (
        (attn_in, attn_in_rows, attn_in_cols, in_shard, dp_count, mp_count, True),
        (attn_out, attn_out_rows, attn_out_cols, out_shard, mp_count, dp_count, False),
        (ffn_up, ffn_up_rows, ffn_up_cols, up_shard, dp_count, mp_count, True),
        (ffn_down, ffn_down_rows, ffn_down_cols, down_shard.T, mp_count, dp_count, False),
    )
    row_parts = [jnp.sum(entry[3] * entry[3], axis=-1) for entry in layer_sets]
    col_parts = [jnp.sum(entry[3] * entry[3], axis=-2) for entry in layer_sets]
    over_dp = [(cols if entry[6] else rows) for rows, cols, entry in zip(row_parts, col_parts, layer_sets)]
    over_mp = [(rows if entry[6] else cols) for rows, cols, entry in zip(row_parts, col_parts, layer_sets)]
    span_sum = span_text + span_visual
    span_sum = jnp.stack([span_sum[:, :NB, :NB], span_sum[:, NB : 2 * NB, NB : 2 * NB]])
    table_part = jnp.einsum("abr,thba->trh", bucket_select, span_sum, precision=PRECISE)
    table_term = jnp.zeros(tables.shape[:2] + (pair, 2, group), WIDE)
    table_term = lax.dynamic_update_slice(
        table_term, table_part.reshape(tables.shape[:2] + (pair, 1, group)), (0, 0, 0, core, 0)
    ).reshape(tables.shape)
    up_term = lax.dynamic_update_slice(
        jnp.zeros((pair, 2, units), WIDE), up_part[:, None], (0, core, 0)
    ).reshape(up_bias.shape)
    while sum_side.rounds:
        sum_side.step()
    while sum_last.rounds:
        sum_last.step()
    sum_last.take(*row_parts)
    last_shard, side_shard = sum_last.value(), sum_side.take().value()
    spatial_rows = spatial_weight.shape[0]
    image_grads = (
        last_shard[spatial_rows:],
        last_shard[:spatial_rows],
        side_shard[:, :middle].reshape(expand_weight.shape),
        side_shard[:, middle:],
    )
    late = [jnp.sum(gradient * gradient, axis=-2) for gradient in image_grads]
    squares = [jnp.sum(rows, axis=-1) for rows in row_parts]
    over_all = [norm_part, up_term, table_term, old_sums, join(squares)] + late
    packed = pack(over_all)
    summed = total_over(jnp.concatenate([packed, pack(over_dp)]), DP)
    dp_sums = unpack(summed[packed.shape[0] :], over_dp)
    summed = total_over(jnp.concatenate([summed[: packed.shape[0]], pack(over_mp)]), MP)
    mp_sums = unpack(summed[packed.shape[0] :], over_mp)
    sums = unpack(summed, over_all)
    norm_gradient, up_gradient, table_gradient, old_sums, squares_total = sums[:5]
    image_cols = sums[5:]
    old_sums = split(old_sums, old_parts)
    weight_squares, rows_before = old_sums[:8], old_sums[8:]
    squares_total = split(squares_total, squares)

    decay_rate = 1.0 - STEP ** (-0.8)
    layer_results = []
    for number, (weight, rows_old, cols_old, gradient, row_split, col_split, flag) in enumerate(layer_sets):
        sizes = (weight.shape[-2] * row_split, weight.shape[-1] * col_split)
        rows_sum = mp_sums[number] if flag else dp_sums[number]
        cols_sum = dp_sums[number] if flag else mp_sums[number]
        mean = (
            decay_rate * rows_before[4 + number]
            + (1.0 - decay_rate) * squares_total[number] / sizes[1]
        ) / sizes[0]
        layer_results.append(
            factored_step(
                weight, gradient, rows_old, cols_old, rows_sum, cols_sum, mean,
                weight_squares[4 + number] / (sizes[0] * sizes[1]), sizes,
            )
        )
    norm_parts = moment_step(norm_params, norm_gradient, norm_moment, (1,))
    bias_parts = moment_step(up_bias, up_gradient, up_moment, (0,))
    table_parts = moment_step(tables, table_gradient, table_moment, (1, 2))

    image_results = []
    for number, (weight, rows_old, cols_old) in enumerate(image_sets):
        gradient = image_grads[number]
        sizes = (weight.shape[0] * dp_count * mp_count, weight.shape[1])
        rows_sum = jnp.sum(gradient * gradient, axis=-1)
        mean = (
            decay_rate * rows_before[number]
            + (1.0 - decay_rate) * jnp.sum(image_cols[number], axis=-1) / sizes[1]
        ) / sizes[0]
        image_results.append(
            factored_step(
                weight, gradient, rows_old, cols_old, rows_sum, image_cols[number], mean,
                weight_squares[number] / (sizes[0] * sizes[1]), sizes,
            )
        )
    flat = [value for result in image_results + layer_results for value in result]
    return (
        (out_local, text_grad_local, image_grad_local)
        + tuple(flat)
        + norm_parts
        + bias_parts
        + table_parts
    )


def solution(mesh):
    whole = mesh.shape["dp"], mesh.shape["mp"]
    devices = mesh.devices.reshape(whole[0] // 2, 2, whole[1] // 2, 2)
    flat, rows, none = P(AXES, None), P(AXES), P()
    image_weight_in = (flat, rows, none)
    image_weight_out = (flat, flat, rows, none, flat)
    in_spec, in_rows, in_cols = P(None, None, DP, MP), P(None, None, DP), P(None, None, MP)
    out_spec, out_rows, out_cols = P(None, MP, DP), P(None, MP), P(None, DP)
    up_spec, up_rows, up_cols = P(DP, MP), P(DP), P(MP)
    down_spec, down_rows, down_cols = P(MP, DP), P(MP), P(DP)
    placed = (
        (P(None, MP, DP, None), P(DP, None, None), P(DP, None, None), P(DP, None), P(DP, None, None))
        + image_weight_in * 4
        + (in_spec, in_rows, in_cols, out_spec, out_rows, out_cols)
        + (up_spec, up_rows, up_cols, down_spec, down_rows, down_cols)
        + (none,) * 6
    )
    given = (
        (P(DP, None, None), P(DP, MP, None), P(None, MP, DP, None))
        + image_weight_out * 4
        + (in_spec, in_spec, in_rows, in_cols, in_spec)
        + (out_spec, out_spec, out_rows, out_cols, out_spec)
        + (up_spec, up_spec, up_rows, up_cols, up_spec)
        + (down_spec, down_spec, down_rows, down_cols, down_spec)
        + (none,) * 9
    )
    return jax.shard_map(
        on_device, mesh=Mesh(devices, AXES), in_specs=placed, out_specs=given, check_vma=False
    )
```

time: 1030 us -> 746 us (0.72)
  waiting for transfers between devices: 256 us -> 153 us
  Pallas kernels: 173 us -> 71.1 us
  other arithmetic: 125 us -> 101 us
  starting transfers between devices: 136 us -> 115 us
  matrix products: 125 us -> 107 us
  local copies, waits for them, and re-layouts: 173 us -> 156 us
    ppermute x78 -> x46, waiting for transfers between devices: 225 us -> 109 us  [swap(): return lax.ppermute(values, axis, [(i, i ^ reach) for i in range(count)])]
    pallas_call x2, Pallas kernels: 107 us -> 41.1 us  [attend_backward(): pl.pallas_call(functools.partial(backward_kernel, heads=heads, group=grou...]
    pallas_call x2, Pallas kernels: 66.3 us -> 20.2 us  [attend_forward(): pl.pallas_call(functools.partial(forward_kernel, heads=heads, group=group...]
    ppermute x78 -> x46, starting transfers between devices: 111 us -> 72.2 us  [swap(): return lax.ppermute(values, axis, [(i, i ^ reach) for i in range(count)])]
    all_gather x1, waiting for transfers between devices: 0.01 us -> 35.8 us  [on_device(): section_whole = lax.all_gather(section_low, AXES, axis=0, tiled=True)]
    dot_general x5 -> x1, matrix products: 23 us -> 2.35 us  [on_device(): jnp.einsum('pwhc,cd->pwhd', tie(image, *first_wait), weight_reduce, prefe...]
    dynamic_slice x44 -> x9, local copies, waits for them, and re-layouts: 31.7 us -> 12.8 us  [the longest x6 8.83 us: cut(): value = lax.dynamic_slice_in_dim(value, place, 1, self.live.index(bit))]
    dot_general x21 -> x31, matrix products: 62.7 us -> 80.3 us  [dot(): lax.dot_general(left, right, (((first,), (second,)), ((), ())), preferred...]
  transfers between devices with their start and end apart: 90 -> 62, of which waited for: 41 -> 25; matrix products, arithmetic and copies ran while one was open for 35% -> 39% of each run, Pallas kernels for 17% -> 9%
where the time goes in v2:
time: 746 us; the launch traced here: 734 us
  local copies, waits for them, and re-layouts  156 us (21%)
  waiting for transfers between devices  153 us (21%)
  starting transfers between devices  115 us (15%)
  matrix products  107 us (14%)
  other arithmetic  101 us (14%)
  Pallas kernels  71.1 us (10%)
  between operations  30.9 us (4%)
    ppermute x46, waiting for transfers between devices, swap(): return lax.ppermute(values, axis, [(i, i ^ reach) for i in range(count)])  109 us
    dot_general x31, matrix products, dot(): lax.dot_general(left, right, (((first,), (second,)), ((), ())), preferred...  80.3 us
    ppermute x46, starting transfers between devices, swap(): return lax.ppermute(values, axis, [(i, i ^ reach) for i in range(count)])  72.2 us
    unnamed x407, local copies, waits for them, and re-layouts  41.2 us
    pallas_call x2, Pallas kernels, attend_backward(): pl.pallas_call(functools.partial(backward_kernel, heads=heads, group=grou...  41.1 us
    all_gather x1, waiting for transfers between devices, on_device(): section_whole = lax.all_gather(section_low, AXES, axis=0, tiled=True)  35.8 us
    pallas_call x2, Pallas kernels, attend_forward(): pl.pallas_call(functools.partial(forward_kernel, heads=heads, group=group...  20.2 us
    dynamic_update_slice x12, local copies, waits for them, and re-layouts, step(): self.whole = lax.dynamic_update_slice(self.whole, got, self.corner(flips))  18.4 us
  transfers between devices with their start and end apart: 62, of which 25 were waited for; matrix products, arithmetic and copies ran while one was open for 39% of the time, Pallas kernels for 9%

profile of v2, /device:TPU:0, one launch (start us, length us, event | category | flops | bytes accessed | tf_op | source)
XLA Modules:
  0.0 734.1 jit_solution(2134414213375451016)
XLA Ops:
  22.3 4.0 collective-permute-start
  75.1 7.1 concatenate.130
  84.8 4.6 collective-permute-start.13
  93.2 4.7 collective-permute-done.5
  99.8 35.8 %all-gather.3.cloned.1.call-done = bf16[2048,2944]{1,0:T(8,128)(2,1)} async-done(((bf16[64,2944]{1,0:T(8,128)(2,1)}), bf16[2048,2944]{1,0:T(8,128)(2,1)}) %all-gather.3.cloned.1.call-update) | async-done | bytes 12058640 | tf_op jit(solution)/shard_map/all_gather | solution.py:700
  153.8 4.4 reshape.973
  179.8 12.2 %all-to-all-start = ((bf16[16,4,8,768]{3,2,1,0:T(8,128)(2,1)}), bf16[16,4,8,768]{3,2,1,0:T(8,128)(2,1)}, u32[]{:S(2)}, u32[]{:S(2)}) async-start(bf16[16,4,8,768]{3,2,1,0:T(8,128)(2,1)} %convolution_convert_fusion.15), calls=%async_computation | async-start | bytes 1572864 | tf_op jit(solution)/shard_map/all_to_all | solution.py:769
  212.3 10.2 %shard_map.738 = (bf16[1024,384]{1,0:T(8,128)(2,1)S(1)}, f32[8,1024]{1,0:T(8,128)S(1)}) custom-call(bf16[1024,576]{1,0:T(8,128)(2,1)S(1)} %convolution_convert_fusion.5.refs_0_, bf16[1024,576]{1,0:T(8,128)(2,1)S(1)} %convolution_convert_fusion.4.refs_1_, s32[2,4]{1,0:T(2,128)S(1)} %pad_add_fusion.refs_2_, bf16[1024,128]{1,0:T(8,128)(2,1)S(1)} %copy-done.4, ...), custom_call_target="tpu_custom_call" | custom-call | tf_op jit(solution)/shard_map/pallas_call | solution.py:203
  228.7 11.3 %collective-permute-done.15 = bf16[1,2,2,1,96,768]{5,4,3,2,1,0:T(8,128)(2,1)} collective-permute-done((bf16[1,2,2,1,96,768]{5,4,3,2,1,0:T(8,128)(2,1)}, bf16[1,2,2,1,96,768]{5,4,3,2,1,0:T(8,128)(2,1)}, u32[]{:S(2)}, u32[]{:S(2)}) %collective-permute-start.15) | collective-permute-done | bytes 589856 | tf_op jit(solution)/shard_map/ppermute | solution.py:313
  254.3 9.9 %shard_map.739 = (bf16[1024,384]{1,0:T(8,128)(2,1)S(1)}, f32[8,1024]{1,0:T(8,128)S(1)}) custom-call(bf16[1024,576]{1,0:T(8,128)(2,1)S(1)} %convolution_convert_fusion.3.refs_0_, bf16[1024,576]{1,0:T(8,128)(2,1)S(1)} %convolution_convert_fusion.2.refs_1_, s32[2,4]{1,0:T(2,128)S(1)} %pad_add_fusion.refs_2_, bf16[1024,128]{1,0:T(8,128)(2,1)S(1)} %copy-done.4, ...), custom_call_target="tpu_custom_call" | custom-call | tf_op jit(solution)/shard_map/pallas_call | solution.py:203
  299.8 5.5 shard_map.741
  309.0 3.9 convert_reduce_fusion.1
  320.2 3.9 collective-permute-start.19
  337.7 19.9 %shard_map.743 = (bf16[1024,576]{1,0:T(8,128)(2,1)}, bf16[1024,576]{1,0:T(8,128)(2,1)}, f32[6,64,128]{2,1,0:T(8,128)}) custom-call(bf16[1024,576]{1,0:T(8,128)(2,1)} %copy-done.14, bf16[1024,576]{1,0:T(8,128)(2,1)} %copy-done.13, s32[2,4]{1,0:T(2,128)} %copy-done.32, bf16[1024,128]{1,0:T(8,128)(2,1)} %add_convert_fusion.15.refs_3_, ...), custom_call_target="tpu_custom_call" | custom-call | tf_op jit(solution)/shard_map/pallas_call | solution.py:231
  365.4 4.9 copy.290
  380.1 10.4 %all-to-all-start.1 = ((bf16[16,4,8,768]{3,2,1,0:T(8,128)(2,1)}), bf16[16,4,8,768]{3,2,1,0:T(8,128)(2,1)}, u32[]{:S(2)}, u32[]{:S(2)}) async-start(bf16[16,4,8,768]{3,2,1,0:T(8,128)(2,1)} %bitcast.84), calls=%async_computation.1 | async-start | bytes 1572864 | tf_op jit(solution)/shard_map/all_to_all | solution.py:865
  395.0 21.2 %shard_map.744 = (bf16[1024,576]{1,0:T(8,128)(2,1)}, bf16[1024,576]{1,0:T(8,128)(2,1)}, f32[6,64,128]{2,1,0:T(8,128)}) custom-call(bf16[1024,576]{1,0:T(8,128)(2,1)} %copy-done.12, bf16[1024,576]{1,0:T(8,128)(2,1)} %copy-done.11, s32[2,4]{1,0:T(2,128)} %copy-done.32, bf16[1024,128]{1,0:T(8,128)(2,1)} %add_convert_fusion.15.refs_3_, ...), custom_call_target="tpu_custom_call" | custom-call | tf_op jit(solution)/shard_map/pallas_call | solution.py:231
  419.8 7.0 collective-permute-start.23
  442.2 16.9 %collective-permute-done.23 = bf16[2,2,2,1,96,768]{5,4,3,2,1,0:T(8,128)(2,1)} collective-permute-done((bf16[2,2,2,1,96,768]{5,4,3,2,1,0:T(8,128)(2,1)}, bf16[2,2,2,1,96,768]{5,4,3,2,1,0:T(8,128)(2,1)}, u32[]{:S(2)}, u32[]{:S(2)}) %collective-permute-start.23) | collective-permute-done | bytes 1179680 | tf_op jit(solution)/shard_map/ppermute | solution.py:313
  459.1 7.3 fusion.121
  468.6 5.4 bitcast_convert_fusion.1
  511.9 4.4 bitcast_convert_fusion
  516.3 4.1 collective-permute-done.31
  535.2 4.5 fusion.52
  539.8 3.9 collective-permute-start.32
  551.6 4.6 collective-permute-done.34
  566.9 7.2 collective-permute-done.45
  597.7 4.6 add_convert_fusion.7
  604.3 7.4 %collective-permute-done.48 = bf16[2,2,1,1,1,64,1280]{6,5,4,3,2,1,0:T(8,128)(2,1)S(1)} collective-permute-done((bf16[2,2,1,1,1,64,1280]{6,5,4,3,2,1,0:T(8,128)(2,1)S(1)}, bf16[2,2,1,1,1,64,1280]{6,5,4,3,2,1,0:T(8,128)(2,1)S(1)}, u32[]{:S(2)}, u32[]{:S(2)}) %collective-permute-start.48) | collective-permute-done | bytes 655392 | tf_op jit(solution)/shard_map/ppermute | solution.py:313
  618.2 4.8 collective-permute-done.49
  627.0 21.4 %collective-permute-done.40 = bf16[2,2,1,1,1,208,512]{6,5,4,3,2,1,0:T(8,128)(2,1)} collective-permute-done((bf16[2,2,1,1,1,208,512]{6,5,4,3,2,1,0:T(8,128)(2,1)}, bf16[2,2,1,1,1,208,512]{6,5,4,3,2,1,0:T(8,128)(2,1)}, u32[]{:S(2)}, u32[]{:S(2)}) %collective-permute-start.40) | collective-permute-done | bytes 852000 | tf_op jit(solution)/shard_map/ppermute | solution.py:313
  656.1 8.1 %collective-permute-done.42 = bf16[1,1,1,1,1,208,512]{6,5,4,3,2,1,0:T(8,128)(2,1)S(1)} collective-permute-done((bf16[1,1,1,1,1,208,512]{6,5,4,3,2,1,0:T(8,128)(2,1)S(1)}, bf16[1,1,1,1,1,208,512]{6,5,4,3,2,1,0:T(8,128)(2,1)S(1)}, u32[]{:S(2)}, u32[]{:S(2)}) %collective-permute-start.42) | collective-permute-done | bytes 213024 | tf_op jit(solution)/shard_map/ppermute | solution.py:313
  (809 shorter events, 417.6 us)
Async XLA Ops:
  7.3 128.4 %all-gather.3.cloned.1.call-start = ((), (), s32[]{:S(2)}) async-start(), calls=%async_computation.3 | async-start | bytes 12435456 | tf_op jit(solution)/shard_map/all_gather | solution.py:700
  16.5 263.8 %all-gather.5.cloned.1.call-start = ((), (), s32[]{:S(2)}) async-start(), calls=%async_computation.4 | async-start | bytes 5013504 | tf_op jit(solution)/shard_map/all_gather | solution.py:701
  22.3 26.1 %collective-permute-start = (bf16[1,1,1,1,96,768]{4,5,3,2,1,0:T(8,128)(2,1)}, bf16[1,1,1,1,96,768]{4,5,3,2,1,0:T(8,128)(2,1)}, u32[]{:S(2)}, u32[]{:S(2)}) collective-permute-start(bf16[1,1,1,1,96,768]{4,5,3,2,1,0:T(8,128)(2,1)} %maximum_bitcast_fusion.1), channel_id=1, source_target_pairs={{0,16},{8,24},{16,0},{24,8},{1,17},{9,25},{17,1},{25,9},{2,18},{10... | collective-permute-start | bytes 442376 | tf_op jit(solution)/shard_map/ppermute | solution.py:313
  26.3 25.3 %collective-permute-start.1 = (bf16[1,1,1,1,96,768]{4,5,3,2,1,0:T(8,128)(2,1)}, bf16[1,1,1,1,96,768]{4,5,3,2,1,0:T(8,128)(2,1)}, u32[]{:S(2)}, u32[]{:S(2)}) collective-permute-start(bf16[1,1,1,1,96,768]{4,5,3,2,1,0:T(8,128)(2,1)} %maximum_bitcast_fusion.1), channel_id=1, source_target_pairs={{0,8},{8,0},{16,24},{24,16},{1,9},{9,1},{17,25},{25,17},{2,10},{10... | collective-permute-start | bytes 442376 | tf_op jit(solution)/shard_map/ppermute | solution.py:313
  27.9 27.0 %collective-permute-start.2 = (bf16[1,1,1,1,96,768]{4,5,3,2,1,0:T(8,128)(2,1)}, bf16[1,1,1,1,96,768]{4,5,3,2,1,0:T(8,128)(2,1)}, u32[]{:S(2)}, u32[]{:S(2)}) collective-permute-start(bf16[1,1,1,1,96,768]{4,5,3,2,1,0:T(8,128)(2,1)} %maximum_bitcast_fusion.1), channel_id=1, source_target_pairs={{0,24},{8,16},{16,8},{24,0},{1,25},{9,17},{17,9},{25,1},{2,26},{10... | collective-permute-start | bytes 442376 | tf_op jit(solution)/shard_map/ppermute | solution.py:313
  28.6 167.1 %collective-permute-start.11 = (bf16[1,1,1,1,96,768]{4,5,3,2,1,0:T(8,128)(2,1)}, bf16[1,1,1,1,96,768]{4,5,3,2,1,0:T(8,128)(2,1)}, u32[]{:S(2)}, u32[]{:S(2)}) collective-permute-start(bf16[1,1,1,1,96,768]{4,5,3,2,1,0:T(8,128)(2,1)} %maximum_bitcast_fusion.2), channel_id=1, source_target_pairs={{0,16},{8,24},{16,0},{24,8},{1,17},{9,25},{17,1},{25,9},{2,18},{10... | collective-permute-start | bytes 442376 | tf_op jit(solution)/shard_map/ppermute | solution.py:313
  30.5 166.3 %collective-permute-start.12 = (bf16[1,1,1,1,96,768]{4,5,3,2,1,0:T(8,128)(2,1)}, bf16[1,1,1,1,96,768]{4,5,3,2,1,0:T(8,128)(2,1)}, u32[]{:S(2)}, u32[]{:S(2)}) collective-permute-start(bf16[1,1,1,1,96,768]{4,5,3,2,1,0:T(8,128)(2,1)} %maximum_bitcast_fusion.2), channel_id=1, source_target_pairs={{0,8},{8,0},{16,24},{24,16},{1,9},{9,1},{17,25},{25,17},{2,10},{10... | collective-permute-start | bytes 442376 | tf_op jit(solution)/shard_map/ppermute | solution.py:313
  60.3 24.5 %collective-permute-start.3 = (bf16[1,2,2,1,96,768]{5,4,3,2,1,0:T(8,128)(2,1)}, bf16[1,2,2,1,96,768]{5,4,3,2,1,0:T(8,128)(2,1)}, u32[]{:S(2)}, u32[]{:S(2)}) collective-permute-start(bf16[1,2,2,1,96,768]{5,4,3,2,1,0:T(8,128)(2,1)} %constant_dynamic-slice_fusion.19), channel_id=1, source_target_pairs={{0,4},{4,0},{1,5},{5,1},{2,6},{6,2},{3,7},{7,3},{8,12},{12,8},{9,1... | collective-permute-start | bytes 1769480 | tf_op jit(solution)/shard_map/ppermute | solution.py:313
  62.9 28.3 %collective-permute-start.4 = (bf16[1,2,2,1,96,768]{5,4,3,2,1,0:T(8,128)(2,1)}, bf16[1,2,2,1,96,768]{5,4,3,2,1,0:T(8,128)(2,1)}, u32[]{:S(2)}, u32[]{:S(2)}) collective-permute-start(bf16[1,2,2,1,96,768]{5,4,3,2,1,0:T(8,128)(2,1)} %constant_dynamic-slice_fusion.19), channel_id=1, source_target_pairs={{0,2},{2,0},{1,3},{3,1},{4,6},{6,4},{5,7},{7,5},{8,10},{10,8},{9,1... | collective-permute-start | bytes 1769480 | tf_op jit(solution)/shard_map/ppermute | solution.py:313
  65.6 32.3 %collective-permute-start.5 = (bf16[1,2,2,1,96,768]{5,4,3,2,1,0:T(8,128)(2,1)}, bf16[1,2,2,1,96,768]{5,4,3,2,1,0:T(8,128)(2,1)}, u32[]{:S(2)}, u32[]{:S(2)}) collective-permute-start(bf16[1,2,2,1,96,768]{5,4,3,2,1,0:T(8,128)(2,1)} %constant_dynamic-slice_fusion.19), channel_id=1, source_target_pairs={{0,6},{2,4},{4,2},{6,0},{1,7},{3,5},{5,3},{7,1},{8,14},{10,12},{12... | collective-permute-start | bytes 1769480 | tf_op jit(solution)/shard_map/ppermute | solution.py:326
  84.8 113.1 %collective-permute-start.13 = (bf16[1,1,1,1,96,768]{4,5,3,2,1,0:T(8,128)(2,1)}, bf16[1,1,1,1,96,768]{4,5,3,2,1,0:T(8,128)(2,1)}, u32[]{:S(2)}, u32[]{:S(2)}) collective-permute-start(bf16[1,1,1,1,96,768]{4,5,3,2,1,0:T(8,128)(2,1)} %maximum_bitcast_fusion.2), channel_id=1, source_target_pairs={{0,24},{8,16},{16,8},{24,0},{1,25},{9,17},{17,9},{25,1},{2,26},{10... | collective-permute-start | bytes 442376 | tf_op jit(solution)/shard_map/ppermute | solution.py:313
  141.1 17.0 %collective-permute-start.6 = (bf16[16,4,1,512]{3,2,1,0:T(2,128)(2,1)}, bf16[16,4,1,512]{3,2,1,0:T(2,128)(2,1)}, u32[]{:S(2)}, u32[]{:S(2)}) collective-permute-start(bf16[16,4,1,512]{3,2,1,0:T(2,128)(2,1)} %get-tuple-element.501), channel_id=1, source_target_pairs={{0,4},{4,8},{8,12},{12,16},{16,20},{20,24},{24,28},{1,5},{5,9},{9,... | collective-permute-start | bytes 196616 | tf_op jit(solution)/shard_map/ppermute | solution.py:490
  179.8 43.8 %all-to-all-start = ((bf16[16,4,8,768]{3,2,1,0:T(8,128)(2,1)}), bf16[16,4,8,768]{3,2,1,0:T(8,128)(2,1)}, u32[]{:S(2)}, u32[]{:S(2)}) async-start(bf16[16,4,8,768]{3,2,1,0:T(8,128)(2,1)} %convolution_convert_fusion.15), calls=%async_computation | async-start | bytes 1572864 | tf_op jit(solution)/shard_map/all_to_all | solution.py:769
  192.1 394.0 %reduce-scatter.2.cloned.1.call-start = ((), (), s32[]{:S(2)}) async-start(), calls=%async_computation.5 | async-start | bytes 5013504 | tf_op jit(solution)/shard_map/reduce_scatter | solution.py:826
  202.9 25.8 %collective-permute-start.16 = (bf16[1,2,2,1,96,768]{5,4,3,2,1,0:T(8,128)(2,1)}, bf16[1,2,2,1,96,768]{5,4,3,2,1,0:T(8,128)(2,1)}, u32[]{:S(2)}, u32[]{:S(2)}) collective-permute-start(bf16[1,2,2,1,96,768]{5,4,3,2,1,0:T(8,128)(2,1)} %constant_dynamic-slice_fusion.15), channel_id=1, source_target_pairs={{0,6},{2,4},{4,2},{6,0},{1,7},{3,5},{5,3},{7,1},{8,14},{10,12},{12... | collective-permute-start | bytes 1769480 | tf_op jit(solution)/shard_map/ppermute | solution.py:326
  205.7 34.3 %collective-permute-start.15 = (bf16[1,2,2,1,96,768]{5,4,3,2,1,0:T(8,128)(2,1)}, bf16[1,2,2,1,96,768]{5,4,3,2,1,0:T(8,128)(2,1)}, u32[]{:S(2)}, u32[]{:S(2)}) collective-permute-start(bf16[1,2,2,1,96,768]{5,4,3,2,1,0:T(8,128)(2,1)} %constant_dynamic-slice_fusion.15), channel_id=1, source_target_pairs={{0,2},{2,0},{1,3},{3,1},{4,6},{6,4},{5,7},{7,5},{8,10},{10,8},{9,1... | collective-permute-start | bytes 1769480 | tf_op jit(solution)/shard_map/ppermute | solution.py:313
  206.3 34.1 %collective-permute-start.14 = (bf16[1,2,2,1,96,768]{5,4,3,2,1,0:T(8,128)(2,1)}, bf16[1,2,2,1,96,768]{5,4,3,2,1,0:T(8,128)(2,1)}, u32[]{:S(2)}, u32[]{:S(2)}) collective-permute-start(bf16[1,2,2,1,96,768]{5,4,3,2,1,0:T(8,128)(2,1)} %constant_dynamic-slice_fusion.15), channel_id=1, source_target_pairs={{0,4},{4,0},{1,5},{5,1},{2,6},{6,2},{3,7},{7,3},{8,12},{12,8},{9,1... | collective-permute-start | bytes 1769480 | tf_op jit(solution)/shard_map/ppermute | solution.py:313
  225.1 22.6 %collective-permute-start.10 = (bf16[2,256,768]{2,1,0:T(8,128)(2,1)S(1)}, bf16[2,256,768]{2,1,0:T(8,128)(2,1)S(1)}, u32[]{:S(2)}, u32[]{:S(2)}) collective-permute-start(bf16[2,256,768]{2,1,0:T(8,128)(2,1)S(1)} %bitcast.479), channel_id=1, source_target_pairs={{0,1},{1,0},{2,3},{3,2},{4,5},{5,4},{6,7},{7,6},{8,9},{9,8},{10,11... | collective-permute-start | bytes 2359304 | tf_op jit(solution)/shard_map/ppermute | solution.py:313
  320.2 50.2 %collective-permute-start.19 = (bf16[2,256,768]{2,1,0:T(8,128)(2,1)}, bf16[2,256,768]{2,1,0:T(8,128)(2,1)}, u32[]{:S(2)}, u32[]{:S(2)}) collective-permute-start(bf16[2,256,768]{2,1,0:T(8,128)(2,1)} %dynamic-slice_bitcast_fusion.2), channel_id=1, source_target_pairs={{0,2},{2,0},{1,3},{3,1},{4,6},{6,4},{5,7},{7,5},{8,10},{10,8},{9,1... | collective-permute-start | bytes 2359304 | tf_op jit(solution)/shard_map/ppermute | solution.py:313
  370.4 68.3 %collective-permute-start.21 = (bf16[2,256,768]{2,1,0:T(8,128)(2,1)}, bf16[2,256,768]{2,1,0:T(8,128)(2,1)}, u32[]{:S(2)}, u32[]{:S(2)}) collective-permute-start(bf16[2,256,768]{2,1,0:T(8,128)(2,1)} %collective-permute-done.19), channel_id=1, source_target_pairs={{0,1},{1,0},{2,3},{3,2},{4,5},{5,4},{6,7},{7,6},{8,9},{9,8},{10,11... | collective-permute-start | bytes 2359304 | tf_op jit(solution)/shard_map/ppermute | solution.py:313
  380.1 62.1 %all-to-all-start.1 = ((bf16[16,4,8,768]{3,2,1,0:T(8,128)(2,1)}), bf16[16,4,8,768]{3,2,1,0:T(8,128)(2,1)}, u32[]{:S(2)}, u32[]{:S(2)}) async-start(bf16[16,4,8,768]{3,2,1,0:T(8,128)(2,1)} %bitcast.84), calls=%async_computation.1 | async-start | bytes 1572864 | tf_op jit(solution)/shard_map/all_to_all | solution.py:865
  419.8 39.3 %collective-permute-start.23 = (bf16[2,2,2,1,96,768]{5,4,3,2,1,0:T(8,128)(2,1)}, bf16[2,2,2,1,96,768]{5,4,3,2,1,0:T(8,128)(2,1)}, u32[]{:S(2)}, u32[]{:S(2)}) collective-permute-start(bf16[2,2,2,1,96,768]{5,4,3,2,1,0:T(8,128)(2,1)} %constant_dynamic-slice_fusion.12), channel_id=1, source_target_pairs={{0,4},{4,0},{1,5},{5,1},{2,6},{6,2},{3,7},{7,3},{8,12},{12,8},{9,1... | collective-permute-start | bytes 3538952 | tf_op jit(solution)/shard_map/ppermute | solution.py:313
  433.5 59.9 %collective-permute-start.26 = (bf16[1,2,2,2,96,768]{5,4,3,2,1,0:T(8,128)(2,1)}, bf16[1,2,2,2,96,768]{5,4,3,2,1,0:T(8,128)(2,1)}, u32[]{:S(2)}, u32[]{:S(2)}) collective-permute-start(bf16[1,2,2,2,96,768]{5,4,3,2,1,0:T(8,128)(2,1)} %constant_dynamic-slice_fusion.11), channel_id=1, source_target_pairs={{0,2},{2,0},{1,3},{3,1},{4,6},{6,4},{5,7},{7,5},{8,10},{10,8},{9,1... | collective-permute-start | bytes 3538952 | tf_op jit(solution)/shard_map/ppermute | solution.py:313
  501.9 18.5 %collective-permute-start.31 = (bf16[1,2,2,1,96,768]{5,4,3,2,1,0:T(8,128)(2,1)}, bf16[1,2,2,1,96,768]{5,4,3,2,1,0:T(8,128)(2,1)}, u32[]{:S(2)}, u32[]{:S(2)}) collective-permute-start(bf16[1,2,2,1,96,768]{5,4,3,2,1,0:T(8,128)(2,1)} %get-tuple-element.462), channel_id=1, source_target_pairs={{0,4},{4,0},{1,5},{5,1},{2,6},{6,2},{3,7},{7,3},{8,12},{12,8},{9,1... | collective-permute-start | bytes 1769480 | tf_op jit(solution)/shard_map/ppermute | solution.py:313
  532.0 56.5 %collective-permute-start.35 = (bf16[2,2,2,2,1,208,512]{6,5,4,3,2,1,0:T(8,128)(2,1)}, bf16[2,2,2,2,1,208,512]{6,5,4,3,2,1,0:T(8,128)(2,1)}, u32[]{:S(2)}, u32[]{:S(2)}) collective-permute-start(bf16[2,2,2,2,1,208,512]{6,5,4,3,2,1,0:T(8,128)(2,1)} %pad_maximum_fusion.2), channel_id=1, source_target_pairs={{0,1},{1,0},{2,3},{3,2},{4,5},{5,4},{6,7},{7,6},{8,9},{9,8},{10,11... | collective-permute-start | bytes 10223624 | tf_op jit(solution)/shard_map/ppermute | solution.py:313
  548.0 44.3 %collective-permute-start.36 = (bf16[2,2,1,2,1,64,1280]{6,5,4,3,2,1,0:T(8,128)(2,1)}, bf16[2,2,1,2,1,64,1280]{6,5,4,3,2,1,0:T(8,128)(2,1)}, u32[]{:S(2)}, u32[]{:S(2)}) collective-permute-start(bf16[2,2,1,2,1,64,1280]{6,5,4,3,2,1,0:T(8,128)(2,1)} %get-tuple-element.458), channel_id=1, source_target_pairs={{0,4},{4,0},{1,5},{5,1},{2,6},{6,2},{3,7},{7,3},{8,12},{12,8},{9,1... | collective-permute-start | bytes 3932168 | tf_op jit(solution)/shard_map/ppermute | solution.py:313
  594.0 17.7 %collective-permute-start.48 = (bf16[2,2,1,1,1,64,1280]{6,5,4,3,2,1,0:T(8,128)(2,1)S(1)}, bf16[2,2,1,1,1,64,1280]{6,5,4,3,2,1,0:T(8,128)(2,1)S(1)}, u32[]{:S(2)}, u32[]{:S(2)}) collective-permute-start(bf16[2,2,1,1,1,64,1280]{6,5,4,3,2,1,0:T(8,128)(2,1)S(1)} %get-tuple-element.471), channel_id=1, source_target_pairs={{0,2},{2,0},{1,3},{3,1},{4,6},{6,4},{5,7},{7,5},{8,10},{10,8},{9,1... | collective-permute-start | bytes 1966088 | tf_op jit(solution)/shard_map/ppermute | solution.py:313
  594.9 20.4 %collective-permute-start.37 = (bf16[2,256,768]{2,1,0:T(8,128)(2,1)S(1)}, bf16[2,256,768]{2,1,0:T(8,128)(2,1)S(1)}, u32[]{:S(2)}, u32[]{:S(2)}) collective-permute-start(bf16[2,256,768]{2,1,0:T(8,128)(2,1)S(1)} %fusion.60), channel_id=1, source_target_pairs={{0,1},{1,0},{2,3},{3,2},{4,5},{5,4},{6,7},{7,6},{8,9},{9,8},{10,11... | collective-permute-start | bytes 2359304 | tf_op jit(solution)/shard_map/ppermute | solution.py:313
  602.3 24.7 %collective-permute-start.39 = (bf16[2,2,1,1,1,208,512]{6,5,4,3,2,1,0:T(8,128)(2,1)}, bf16[2,2,1,1,1,208,512]{6,5,4,3,2,1,0:T(8,128)(2,1)}, u32[]{:S(2)}, u32[]{:S(2)}) collective-permute-start(bf16[2,2,1,1,1,208,512]{6,5,4,3,2,1,0:T(8,128)(2,1)} %get-tuple-element.455), channel_id=1, source_target_pairs={{0,4},{4,0},{1,5},{5,1},{2,6},{6,2},{3,7},{7,3},{8,12},{12,8},{9,1... | collective-permute-start | bytes 2555912 | tf_op jit(solution)/shard_map/ppermute | solution.py:313
  602.5 45.9 %collective-permute-start.40 = (bf16[2,2,1,1,1,208,512]{6,5,4,3,2,1,0:T(8,128)(2,1)}, bf16[2,2,1,1,1,208,512]{6,5,4,3,2,1,0:T(8,128)(2,1)}, u32[]{:S(2)}, u32[]{:S(2)}) collective-permute-start(bf16[2,2,1,1,1,208,512]{6,5,4,3,2,1,0:T(8,128)(2,1)} %get-tuple-element.456), channel_id=1, source_target_pairs={{0,2},{2,0},{1,3},{3,1},{4,6},{6,4},{5,7},{7,5},{8,10},{10,8},{9,1... | collective-permute-start | bytes 2555912 | tf_op jit(solution)/shard_map/ppermute | solution.py:313
  623.1 25.3 %collective-permute-start.41 = (bf16[2,2,1,1,1,208,512]{6,5,4,3,2,1,0:T(8,128)(2,1)}, bf16[2,2,1,1,1,208,512]{6,5,4,3,2,1,0:T(8,128)(2,1)}, u32[]{:S(2)}, u32[]{:S(2)}) collective-permute-start(bf16[2,2,1,1,1,208,512]{6,5,4,3,2,1,0:T(8,128)(2,1)} %get-tuple-element.454), channel_id=1, source_target_pairs={{0,6},{2,4},{4,2},{6,0},{1,7},{3,5},{5,3},{7,1},{8,14},{10,12},{12... | collective-permute-start | bytes 2555912 | tf_op jit(solution)/shard_map/ppermute | solution.py:326
  623.6 55.1 %collective-permute-start.38 = (bf16[256,768]{1,0:T(8,128)(2,1)}, bf16[256,768]{1,0:T(8,128)(2,1)}, u32[]{:S(2)}, u32[]{:S(2)}) collective-permute-start(bf16[256,768]{1,0:T(8,128)(2,1)} %fusion.82), channel_id=1, source_target_pairs={{0,2},{2,0},{1,3},{3,1},{4,6},{6,4},{5,7},{7,5},{8,10},{10,8},{9,1... | collective-permute-start | bytes 1179656 | tf_op jit(solution)/shard_map/ppermute | solution.py:313
  (208 other events, 2631.8 us)
Sparse Core Ops, SparseCore 0:
  16.6 119.0 all-gather.2
  139.0 95.8 all-gather.4
  370.4 155.4 reduce-scatter.1

commit v3 on v2

--- a/solution.py
+++ b/solution.py
@@ -379,7 +379,7 @@
 
     def step(self, before=(), fill=()):
         group = self.rounds.pop()
-        sent = tie(self.held, *before)
+        sent = lax.optimization_barrier((self.held,) + tuple(before))[0]
         arrived = []
         for flips in flips_of(group):
             got = tie(exchange(sent, flips), *fill)
@@ -400,10 +400,14 @@
         self.live = bits(owners)
         self.count = len(self.live)
         self.rounds = rounds_of(order)[::-1]
-        self.parts = [value.reshape((2,) * self.count + (-1,) + value.shape[1:]) for value in blocks]
+        self.parts = [[value.reshape((2,) * self.count + (-1,) + value.shape[1:])] for value in blocks]
         self.axis = self.count + axis
-        self.held = None
         self.busy = False
+
+    def merged(self, other):
+        self.parts = self.parts + other.parts
+        self.axis = self.count
+        return self
 
     def pick(self, group, flips):
         def cut(value):
@@ -413,9 +417,13 @@
                 value = lax.dynamic_slice_in_dim(value, place, 1, self.live.index(bit))
             return value
 
-        if self.held is None:
-            return jnp.concatenate([cut(value) for value in self.parts], axis=self.axis)
-        return sum(cut(value).astype(WIDE) for value in self.held).astype(LOW)
+        found = []
+        for addends in self.parts:
+            if len(addends) == 1:
+                found.append(cut(addends[0]))
+            else:
+                found.append(sum(cut(value).astype(WIDE) for value in addends).astype(LOW))
+        return jnp.concatenate(found, axis=self.axis)
 
     def send(self, *after):
         group = self.rounds.pop()
@@ -431,7 +439,7 @@
     def take(self, *after):
         if self.busy:
             flying = lax.optimization_barrier(self.flying + after)[: len(self.flying)]
-            self.held = [self.kept] + list(flying)
+            self.parts = [[self.kept] + list(flying)]
             self.busy = False
         return self
 
@@ -439,16 +447,16 @@
         self.take(*after)
         return self.send() if self.rounds else self
 
-    def land(self, values):
+    def land(self, values, go_on=True):
         found = lax.optimization_barrier((values,) + self.flying)
-        self.held = [self.kept] + list(found[1:])
+        self.parts = [[self.kept] + list(found[1:])]
         self.busy = False
-        if self.rounds:
+        if self.rounds and go_on:
             self.send()
         return found[0]
 
     def value(self):
-        total = sum(value.astype(WIDE) for value in self.held)
+        total = sum(value.astype(WIDE) for value in self.parts[0])
         return total.reshape(total.shape[self.count :])
 
 
@@ -706,9 +714,10 @@
     )
     copies = (1, 1, 1, 1, mp_count, dp_count, mp_count, dp_count)
     halves = [Gather(half, (("dz",), ("dx", "my")), OWNERS) for half in layer_in]
-    while len(halves[0].rounds) > 1:
-        for half in halves:
-            half.step()
+    while halves[0].rounds:
+        halves[0].step()
+    while len(halves[1].rounds) > 1:
+        halves[1].step((halves[0].whole,))
     old_parts = [jnp.sum(weight * weight, axis=(-2, -1)) for weight in old_weights]
     old_parts += [jnp.sum(rows, axis=-1) / times for rows, times in zip(old_rows, copies)]
     old_sums = join(old_parts)
@@ -717,7 +726,6 @@
     ends = [blocks * middle, extra * middle // base, middle, width, middle]
     ends = [sum(ends[: n + 1]) for n in range(len(ends))]
     weight_reduce = section_whole[:, :, ends[3] :].reshape(channels, middle)
-    halves[0].step()
     first_wait = (halves[0].whole, old_sums)
     reduced = jnp.einsum(
         "pwhc,cd->pwhd",
@@ -726,7 +734,8 @@
         preferred_element_type=WIDE,
     )
     hidden_one = smooth(reduced).astype(LOW)
-    beside = extended(hidden_one, ((DP, 2),), 1)
+    beside = extended(tie(hidden_one, halves[1].held), ((DP, 2),), 1)
+    halves[1].step((beside,))
     section_whole = tie(section_whole, hidden_one)
     weight_spatial = [section_whole[:, :, n * middle : (n + 1) * middle] for n in range(blocks)]
     weight_spatial.append(
@@ -768,11 +777,10 @@
 
     visual_own = lax.all_to_all(visual_rows, CHIPS, split_axis=0, concat_axis=0, tiled=True)
 
-    text_source = tie(text_page, visual_rows)
+    text_source = tie(text_page, visual_rows, halves[1].whole)
     weight_in = [[attn_text[y, :, : 3 * part] for y in range(pair)]]
     projected_text = [dot(text_source, weight).astype(LOW) for weight in weight_in[0]]
     attended_text, logs_text = attend_forward(projected_text, around, size)
-    halves[1].step((), (attended_text,))
     attn_visual = halves[1].value().reshape(pair, width, 4 * part)
     weight_in.append([attn_visual[y, :, : 3 * part] for y in range(pair)])
     weight_out = jnp.concatenate(
@@ -892,7 +900,7 @@
     sum_side = Scatter(
         [grad_expand, grad_proj], (("core",), ("dx",), ("my",), ("dz",)), AXES, 1
     ).send()
-    back_padded = sum_one.land(back_padded)
+    back_padded = sum_one.land(back_padded, False)
     back_taps = stacked_taps(back_padded, across, down, BACKWARD_TAPS).reshape(
         conv_grad.shape[:3] + (9, middle)
     )
@@ -910,13 +918,14 @@
     ).astype(LOW)
     grad_reduce = dot(
         image.reshape(-1, channels),
-        sum_two.land(tie(reduced_grad, grad_spatial)).reshape(-1, middle),
+        sum_two.land(tie(reduced_grad, grad_spatial), False).reshape(-1, middle),
         "tn",
     ).astype(LOW)
     sum_last = Scatter(
         [grad_spatial, grad_reduce], (("core",), ("dx", "my"), ("dz",)), AXES
     ).send()
-    reduced_grad = sum_one.land(tie(reduced_grad, grad_reduce))
+    sum_both = sum_one.merged(sum_two).send()
+    reduced_grad = tie(reduced_grad, grad_reduce)
     image_grad_local = pre_grad + jnp.einsum(
         "pwhd,cd->pwhc", reduced_grad, weight_reduce, preferred_element_type=WIDE
     )
@@ -929,13 +938,21 @@
     text_grad_local = by_side(
         ("my", 1), text_kept, swap(text_sent.astype(LOW), "my", 1).astype(WIDE), 0
     )
-    for tree in (sum_two, sum_one):
-        while tree.rounds:
-            tree.step(text_own)
-        tree.take(text_own)
-
+    while sum_both.rounds:
+        sum_both.step(text_own)
+    both_shard = sum_both.take(text_own).value()
+
+    (
+        reduce_weight, spatial_weight, expand_weight, visual_proj, attn_in, attn_out, ffn_up, ffn_down,
+        norm_params, norm_moment, up_bias, up_moment, tables, table_moment,
+    ) = lax.optimization_barrier(
+        (
+            reduce_weight, spatial_weight, expand_weight, visual_proj, attn_in, attn_out, ffn_up, ffn_down,
+            norm_params, norm_moment, up_bias, up_moment, tables, table_moment, grad_reduce,
+        )
+    )[:14]
     up_shard, down_shard = jnp.split(ffn_shard, 2)
-    one_shard, two_shard = sum_one.value(), sum_two.value()
+    one_shard, two_shard = jnp.split(both_shard, 2)
     in_shard = jnp.stack([two_shard[:, : 3 * part], one_shard[:, : 3 * part]])
     in_shard = in_shard.reshape(2, -1, 3, part).transpose(0, 2, 1, 3)
     out_shard = jnp.stack([two_shard[:, 3 * part :], one_shard[:, 3 * part :]]).transpose(0, 2, 1)

time: 746 us -> 733 us (0.983)
  starting transfers between devices: 115 us -> 93.8 us
  local copies, waits for them, and re-layouts: 156 us -> 138 us
  Pallas kernels: 71.1 us -> 87.2 us
  waiting for transfers between devices: 153 us -> 164 us
    all_gather x1, waiting for transfers between devices: 35.8 us -> 13.2 us  [on_device(): section_whole = lax.all_gather(section_low, AXES, axis=0, tiled=True)]
    ppermute x3, waiting for transfers between devices: 6.62 us -> 28.7 us  [exchange(): return lax.ppermute(values, (one, two), pairs)]
    ppermute x46 -> x43, waiting for transfers between devices: 109 us -> 122 us  [swap(): return lax.ppermute(values, axis, [(i, i ^ reach) for i in range(count)])]
    pallas_call x2, Pallas kernels: 41.1 us -> 51.5 us  [attend_backward(): pl.pallas_call(functools.partial(backward_kernel, heads=heads, group=grou...]
    ppermute x46 -> x43, starting transfers between devices: 72.2 us -> 62.2 us  [swap(): return lax.ppermute(values, axis, [(i, i ^ reach) for i in range(count)])]
    unnamed x407 -> x405, local copies, waits for them, and re-layouts: 41.2 us -> 37.6 us
  transfers between devices with their start and end apart: 62 -> 59, of which waited for: 25 -> 24; matrix products, arithmetic and copies ran while one was open for 39% -> 37% of each run, Pallas kernels for 9% -> 11%
where the time goes in v3:
time: 733 us; the launch traced here: 722 us
  waiting for transfers between devices  164 us (22%)
  local copies, waits for them, and re-layouts  138 us (19%)
  other arithmetic  105 us (14%)
  matrix products  103 us (14%)
  starting transfers between devices  93.8 us (13%)
  Pallas kernels  87.2 us (12%)
  between operations  31.1 us (4%)
    ppermute x43, waiting for transfers between devices, swap(): return lax.ppermute(values, axis, [(i, i ^ reach) for i in range(count)])  122 us
    dot_general x31, matrix products, dot(): lax.dot_general(left, right, (((first,), (second,)), ((), ())), preferred...  75.7 us
    ppermute x43, starting transfers between devices, swap(): return lax.ppermute(values, axis, [(i, i ^ reach) for i in range(count)])  62.2 us
    pallas_call x2, Pallas kernels, attend_backward(): pl.pallas_call(functools.partial(backward_kernel, heads=heads, group=grou...  51.5 us
    unnamed x405, local copies, waits for them, and re-layouts  37.6 us
    ppermute x3, waiting for transfers between devices, exchange(): return lax.ppermute(values, (one, two), pairs)  28.7 us
    pallas_call x2, Pallas kernels, attend_forward(): pl.pallas_call(functools.partial(forward_kernel, heads=heads, group=group...  25.9 us
    convert_element_type x9, other arithmetic, pick(): sum((cut(value).astype(WIDE) for value in addends)).astype(LOW)  17.4 us
  transfers between devices with their start and end apart: 59, of which 24 were waited for; matrix products, arithmetic and copies ran while one was open for 37% of the time, Pallas kernels for 11%

profile of v3, /device:TPU:0, one launch (start us, length us, event | category | flops | bytes accessed | tf_op | source)
XLA Modules:
  0.0 722.4 jit_solution(11737551875367125003)
XLA Ops:
  23.3 4.0 collective-permute-start
  54.5 4.3 collective-permute-start.3
  65.4 14.8 %collective-permute-done.3 = bf16[1,2,2,1,96,768]{5,4,3,2,1,0:T(8,128)(2,1)} collective-permute-done((bf16[1,2,2,1,96,768]{5,4,3,2,1,0:T(8,128)(2,1)}, bf16[1,2,2,1,96,768]{5,4,3,2,1,0:T(8,128)(2,1)}, u32[]{:S(2)}, u32[]{:S(2)}) %collective-permute-start.3) | collective-permute-done | bytes 589856 | tf_op jit(solution)/shard_map/ppermute | solution.py:313
  83.1 12.6 %collective-permute-done.5 = bf16[1,2,2,1,96,768]{5,4,3,2,1,0:T(8,128)(2,1)S(1)} collective-permute-done((bf16[1,2,2,1,96,768]{5,4,3,2,1,0:T(8,128)(2,1)}, bf16[1,2,2,1,96,768]{5,4,3,2,1,0:T(8,128)(2,1)S(1)}, u32[]{:S(2)}, u32[]{:S(2)}) %collective-permute-start.5) | collective-permute-done | bytes 589856 | tf_op jit(solution)/shard_map/ppermute | solution.py:326
  106.4 7.1 concatenate.150
  118.2 8.0 %collective-permute-done.8 = bf16[1,1,1,1,96,768]{4,5,3,2,1,0:T(8,128)(2,1)} collective-permute-done((bf16[1,1,1,1,96,768]{4,5,3,2,1,0:T(8,128)(2,1)S(1)}, bf16[1,1,1,1,96,768]{4,5,3,2,1,0:T(8,128)(2,1)}, u32[]{:S(2)}, u32[]{:S(2)}) %collective-permute-start.8) | collective-permute-done | bytes 147488 | tf_op jit(solution)/shard_map/ppermute | solution.py:313
  128.2 13.2 %all-gather.3.cloned.1.call-done = bf16[2048,2944]{1,0:T(8,128)(2,1)} async-done(((bf16[64,2944]{1,0:T(8,128)(2,1)}), bf16[2048,2944]{1,0:T(8,128)(2,1)}) %all-gather.3.cloned.1.call-update) | async-done | bytes 12058640 | tf_op jit(solution)/shard_map/all_gather | solution.py:708
  148.4 5.2 collective-permute-start.9
  171.5 4.1 collective-permute-start.14
  189.3 8.9 %all-to-all-start = ((bf16[16,4,8,768]{3,2,1,0:T(8,128)(2,1)}), bf16[16,4,8,768]{3,2,1,0:T(8,128)(2,1)S(1)}, u32[]{:S(2)}, u32[]{:S(2)}) async-start(bf16[16,4,8,768]{3,2,1,0:T(8,128)(2,1)} %convolution_convert_fusion.15), calls=%async_computation | async-start | bytes 1572864 | tf_op jit(solution)/shard_map/all_to_all | solution.py:778
  203.0 16.0 %collective-permute-done.15 = bf16[1,2,2,1,96,768]{5,4,3,2,1,0:T(8,128)(2,1)} collective-permute-done((bf16[1,2,2,1,96,768]{5,4,3,2,1,0:T(8,128)(2,1)}, bf16[1,2,2,1,96,768]{5,4,3,2,1,0:T(8,128)(2,1)}, u32[]{:S(2)}, u32[]{:S(2)}) %collective-permute-start.15) | collective-permute-done | bytes 589856 | tf_op jit(solution)/shard_map/ppermute | solution.py:326
  226.9 13.1 %shard_map.738 = (bf16[1024,384]{1,0:T(8,128)(2,1)S(1)}, f32[8,1024]{1,0:T(8,128)S(1)}) custom-call(bf16[1024,576]{1,0:T(8,128)(2,1)S(1)} %convolution_convert_fusion.5.refs_0_, bf16[1024,576]{1,0:T(8,128)(2,1)S(1)} %convolution_convert_fusion.4.refs_1_, s32[2,4]{1,0:T(2,128)S(1)} %pad_add_fusion.refs_2_, bf16[1024,128]{1,0:T(8,128)(2,1)S(1)} %add_convert_fusion.15.refs_3_, ...), custom_call_target="tpu_custom_call" | custom-call | tf_op jit(solution)/shard_map/pallas_call | solution.py:203
  249.1 12.8 %shard_map.739 = (bf16[1024,384]{1,0:T(8,128)(2,1)S(1)}, f32[8,1024]{1,0:T(8,128)S(1)}) custom-call(bf16[1024,576]{1,0:T(8,128)(2,1)S(1)} %convolution_convert_fusion.3.refs_0_, bf16[1024,576]{1,0:T(8,128)(2,1)S(1)} %convolution_convert_fusion.2.refs_1_, s32[2,4]{1,0:T(2,128)S(1)} %pad_add_fusion.refs_2_, bf16[1024,128]{1,0:T(8,128)(2,1)S(1)} %add_convert_fusion.15.refs_3_, ...), custom_call_target="tpu_custom_call" | custom-call | tf_op jit(solution)/shard_map/pallas_call | solution.py:203
  292.4 5.5 shard_map.741
  326.5 25.4 %shard_map.743 = (bf16[1024,576]{1,0:T(8,128)(2,1)}, bf16[1024,576]{1,0:T(8,128)(2,1)}, f32[6,64,128]{2,1,0:T(8,128)}) custom-call(bf16[1024,576]{1,0:T(8,128)(2,1)} %copy-done.14, bf16[1024,576]{1,0:T(8,128)(2,1)} %copy-done.13, s32[2,4]{1,0:T(2,128)} %copy-done.32, bf16[1024,128]{1,0:T(8,128)(2,1)} %copy-done.4, bf16[6,128,256]{2,1,0:T(8,128)(2,1)} %copy-done.3, ...), custom_call_target="tpu_custom_call" | custom-call | tf_op jit(solution)/shard_map/pallas_call | solution.py:231
  358.2 4.8 copy.290
  372.8 4.5 all-to-all-start.1
  381.8 26.0 %shard_map.744 = (bf16[1024,576]{1,0:T(8,128)(2,1)}, bf16[1024,576]{1,0:T(8,128)(2,1)}, f32[6,64,128]{2,1,0:T(8,128)}) custom-call(bf16[1024,576]{1,0:T(8,128)(2,1)} %copy-done.12, bf16[1024,576]{1,0:T(8,128)(2,1)} %copy-done.11, s32[2,4]{1,0:T(2,128)} %copy-done.32, bf16[1024,128]{1,0:T(8,128)(2,1)} %copy-done.4, bf16[6,128,256]{2,1,0:T(8,128)(2,1)} %copy-done.3, ...), custom_call_target="tpu_custom_call" | custom-call | tf_op jit(solution)/shard_map/pallas_call | solution.py:231
  429.9 4.5 fusion.52
  434.5 12.8 %collective-permute-done.23 = bf16[2,2,2,1,96,768]{5,4,3,2,1,0:T(8,128)(2,1)} collective-permute-done((bf16[2,2,2,1,96,768]{5,4,3,2,1,0:T(8,128)(2,1)}, bf16[2,2,2,1,96,768]{5,4,3,2,1,0:T(8,128)(2,1)}, u32[]{:S(2)}, u32[]{:S(2)}) %collective-permute-start.23) | collective-permute-done | bytes 1179680 | tf_op jit(solution)/shard_map/ppermute | solution.py:313
  447.3 7.2 fusion.122
  456.7 5.4 bitcast_convert_fusion.1
  499.6 4.4 bitcast_convert_fusion
  531.0 3.9 collective-permute-start.44
  543.8 5.3 collective-permute-done.43
  549.2 12.2 %collective-permute-done.42 = bf16[1,1,1,1,192,768]{5,4,3,2,1,0:T(8,128)(2,1)} collective-permute-done((bf16[1,1,1,1,192,768]{5,4,3,2,1,0:T(8,128)(2,1)}, bf16[1,1,1,1,192,768]{5,4,3,2,1,0:T(8,128)(2,1)}, u32[]{:S(2)}, u32[]{:S(2)}) %collective-permute-start.42) | collective-permute-done | bytes 294944 | tf_op jit(solution)/shard_map/ppermute | solution.py:313
  585.1 4.7 add_convert_fusion.7
  592.8 6.8 collective-permute-done.45
  605.3 7.7 %collective-permute-done.46 = bf16[1,1,1,1,1,64,1280]{6,5,4,3,2,1,0:T(8,128)(2,1)S(1)} collective-permute-done((bf16[1,1,1,1,1,64,1280]{6,5,4,3,2,1,0:T(8,128)(2,1)S(1)}, bf16[1,1,1,1,1,64,1280]{6,5,4,3,2,1,0:T(8,128)(2,1)S(1)}, u32[]{:S(2)}, u32[]{:S(2)}) %collective-permute-start.46) | collective-permute-done | bytes 163872 | tf_op jit(solution)/shard_map/ppermute | solution.py:313
  616.8 19.5 %collective-permute-done.37 = bf16[2,2,1,1,1,208,512]{6,5,4,3,2,1,0:T(8,128)(2,1)} collective-permute-done((bf16[2,2,1,1,1,208,512]{6,5,4,3,2,1,0:T(8,128)(2,1)}, bf16[2,2,1,1,1,208,512]{6,5,4,3,2,1,0:T(8,128)(2,1)}, u32[]{:S(2)}, u32[]{:S(2)}) %collective-permute-start.37) | collective-permute-done | bytes 852000 | tf_op jit(solution)/shard_map/ppermute | solution.py:313
  643.2 10.9 %collective-permute-done.39 = bf16[1,1,1,1,1,208,512]{6,5,4,3,2,1,0:T(8,128)(2,1)S(1)} collective-permute-done((bf16[1,1,1,1,1,208,512]{6,5,4,3,2,1,0:T(8,128)(2,1)S(1)}, bf16[1,1,1,1,1,208,512]{6,5,4,3,2,1,0:T(8,128)(2,1)S(1)}, u32[]{:S(2)}, u32[]{:S(2)}) %collective-permute-start.39) | collective-permute-done | bytes 213024 | tf_op jit(solution)/shard_map/ppermute | solution.py:313
  657.1 4.1 collective-permute-start.49
  (809 shorter events, 391.3 us)
Async XLA Ops:
  7.3 134.1 %all-gather.3.cloned.1.call-start = ((), (), s32[]{:S(2)}) async-start(), calls=%async_computation.3 | async-start | bytes 12435456 | tf_op jit(solution)/shard_map/all_gather | solution.py:708
  16.5 261.5 %all-gather.5.cloned.1.call-start = ((), (), s32[]{:S(2)}) async-start(), calls=%async_computation.4 | async-start | bytes 5013504 | tf_op jit(solution)/shard_map/all_gather | solution.py:709
  23.3 24.0 %collective-permute-start = (bf16[1,1,1,1,96,768]{4,5,3,2,1,0:T(8,128)(2,1)}, bf16[1,1,1,1,96,768]{4,5,3,2,1,0:T(8,128)(2,1)}, u32[]{:S(2)}, u32[]{:S(2)}) collective-permute-start(bf16[1,1,1,1,96,768]{4,5,3,2,1,0:T(8,128)(2,1)} %maximum_bitcast_fusion.1), channel_id=1, source_target_pairs={{0,16},{8,24},{16,0},{24,8},{1,17},{9,25},{17,1},{25,9},{2,18},{10... | collective-permute-start | bytes 442376 | tf_op jit(solution)/shard_map/ppermute | solution.py:313
  27.4 21.7 %collective-permute-start.1 = (bf16[1,1,1,1,96,768]{4,5,3,2,1,0:T(8,128)(2,1)}, bf16[1,1,1,1,96,768]{4,5,3,2,1,0:T(8,128)(2,1)}, u32[]{:S(2)}, u32[]{:S(2)}) collective-permute-start(bf16[1,1,1,1,96,768]{4,5,3,2,1,0:T(8,128)(2,1)} %maximum_bitcast_fusion.1), channel_id=1, source_target_pairs={{0,8},{8,0},{16,24},{24,16},{1,9},{9,1},{17,25},{25,17},{2,10},{10... | collective-permute-start | bytes 442376 | tf_op jit(solution)/shard_map/ppermute | solution.py:313
  28.9 21.8 %collective-permute-start.2 = (bf16[1,1,1,1,96,768]{4,5,3,2,1,0:T(8,128)(2,1)}, bf16[1,1,1,1,96,768]{4,5,3,2,1,0:T(8,128)(2,1)}, u32[]{:S(2)}, u32[]{:S(2)}) collective-permute-start(bf16[1,1,1,1,96,768]{4,5,3,2,1,0:T(8,128)(2,1)} %maximum_bitcast_fusion.1), channel_id=1, source_target_pairs={{0,24},{8,16},{16,8},{24,0},{1,25},{9,17},{17,9},{25,1},{2,26},{10... | collective-permute-start | bytes 442376 | tf_op jit(solution)/shard_map/ppermute | solution.py:313
  54.5 25.7 %collective-permute-start.3 = (bf16[1,2,2,1,96,768]{5,4,3,2,1,0:T(8,128)(2,1)}, bf16[1,2,2,1,96,768]{5,4,3,2,1,0:T(8,128)(2,1)}, u32[]{:S(2)}, u32[]{:S(2)}) collective-permute-start(bf16[1,2,2,1,96,768]{5,4,3,2,1,0:T(8,128)(2,1)} %constant_dynamic-slice_fusion.19), channel_id=1, source_target_pairs={{0,4},{4,0},{1,5},{5,1},{2,6},{6,2},{3,7},{7,3},{8,12},{12,8},{9,1... | collective-permute-start | bytes 1769480 | tf_op jit(solution)/shard_map/ppermute | solution.py:313
  60.8 21.4 %collective-permute-start.4 = (bf16[1,2,2,1,96,768]{5,4,3,2,1,0:T(8,128)(2,1)}, bf16[1,2,2,1,96,768]{5,4,3,2,1,0:T(8,128)(2,1)S(1)}, u32[]{:S(2)}, u32[]{:S(2)}) collective-permute-start(bf16[1,2,2,1,96,768]{5,4,3,2,1,0:T(8,128)(2,1)} %constant_dynamic-slice_fusion.19), channel_id=1, source_target_pairs={{0,2},{2,0},{1,3},{3,1},{4,6},{6,4},{5,7},{7,5},{8,10},{10,8},{9,1... | collective-permute-start | bytes 1769480 | tf_op jit(solution)/shard_map/ppermute | solution.py:313
  63.7 32.0 %collective-permute-start.5 = (bf16[1,2,2,1,96,768]{5,4,3,2,1,0:T(8,128)(2,1)}, bf16[1,2,2,1,96,768]{5,4,3,2,1,0:T(8,128)(2,1)S(1)}, u32[]{:S(2)}, u32[]{:S(2)}) collective-permute-start(bf16[1,2,2,1,96,768]{5,4,3,2,1,0:T(8,128)(2,1)} %constant_dynamic-slice_fusion.19), channel_id=1, source_target_pairs={{0,6},{2,4},{4,2},{6,0},{1,7},{3,5},{5,3},{7,1},{8,14},{10,12},{12... | collective-permute-start | bytes 1769480 | tf_op jit(solution)/shard_map/ppermute | solution.py:326
  96.6 21.2 %collective-permute-start.6 = (bf16[1,1,1,1,96,768]{4,5,3,2,1,0:T(8,128)(2,1)S(1)}, bf16[1,1,1,1,96,768]{4,5,3,2,1,0:T(8,128)(2,1)S(1)}, u32[]{:S(2)}, u32[]{:S(2)}) collective-permute-start(bf16[1,1,1,1,96,768]{4,5,3,2,1,0:T(8,128)(2,1)S(1)} %maximum_bitcast_fusion.2), channel_id=1, source_target_pairs={{0,16},{8,24},{16,0},{24,8},{1,17},{9,25},{17,1},{25,9},{2,18},{10... | collective-permute-start | bytes 442376 | tf_op jit(solution)/shard_map/ppermute | solution.py:313
  98.2 19.9 %collective-permute-start.7 = (bf16[1,1,1,1,96,768]{4,5,3,2,1,0:T(8,128)(2,1)S(1)}, bf16[1,1,1,1,96,768]{4,5,3,2,1,0:T(8,128)(2,1)S(1)}, u32[]{:S(2)}, u32[]{:S(2)}) collective-permute-start(bf16[1,1,1,1,96,768]{4,5,3,2,1,0:T(8,128)(2,1)S(1)} %maximum_bitcast_fusion.2), channel_id=1, source_target_pairs={{0,8},{8,0},{16,24},{24,16},{1,9},{9,1},{17,25},{25,17},{2,10},{10... | collective-permute-start | bytes 442376 | tf_op jit(solution)/shard_map/ppermute | solution.py:313
  146.8 16.3 %collective-permute-start.10 = (bf16[16,4,1,512]{3,2,1,0:T(2,128)(2,1)}, bf16[16,4,1,512]{3,2,1,0:T(2,128)(2,1)S(1)}, u32[]{:S(2)}, u32[]{:S(2)}) collective-permute-start(bf16[16,4,1,512]{3,2,1,0:T(2,128)(2,1)} %get-tuple-element.526), channel_id=1, source_target_pairs={{4,0},{8,4},{12,8},{16,12},{20,16},{24,20},{28,24},{5,1},{9,5},{13... | collective-permute-start | bytes 196616 | tf_op jit(solution)/shard_map/ppermute | solution.py:500
  169.7 29.2 %collective-permute-start.13 = (bf16[1,2,2,1,96,768]{5,4,3,2,1,0:T(8,128)(2,1)}, bf16[1,2,2,1,96,768]{5,4,3,2,1,0:T(8,128)(2,1)}, u32[]{:S(2)}, u32[]{:S(2)}) collective-permute-start(bf16[1,2,2,1,96,768]{5,4,3,2,1,0:T(8,128)(2,1)} %constant_dynamic-slice_fusion.18), channel_id=1, source_target_pairs={{0,4},{4,0},{1,5},{5,1},{2,6},{6,2},{3,7},{7,3},{8,12},{12,8},{9,1... | collective-permute-start | bytes 1769480 | tf_op jit(solution)/shard_map/ppermute | solution.py:313
  171.5 29.5 %collective-permute-start.14 = (bf16[1,2,2,1,96,768]{5,4,3,2,1,0:T(8,128)(2,1)}, bf16[1,2,2,1,96,768]{5,4,3,2,1,0:T(8,128)(2,1)}, u32[]{:S(2)}, u32[]{:S(2)}) collective-permute-start(bf16[1,2,2,1,96,768]{5,4,3,2,1,0:T(8,128)(2,1)} %constant_dynamic-slice_fusion.18), channel_id=1, source_target_pairs={{0,2},{2,0},{1,3},{3,1},{4,6},{6,4},{5,7},{7,5},{8,10},{10,8},{9,1... | collective-permute-start | bytes 1769480 | tf_op jit(solution)/shard_map/ppermute | solution.py:313
  175.7 43.3 %collective-permute-start.15 = (bf16[1,2,2,1,96,768]{5,4,3,2,1,0:T(8,128)(2,1)}, bf16[1,2,2,1,96,768]{5,4,3,2,1,0:T(8,128)(2,1)}, u32[]{:S(2)}, u32[]{:S(2)}) collective-permute-start(bf16[1,2,2,1,96,768]{5,4,3,2,1,0:T(8,128)(2,1)} %constant_dynamic-slice_fusion.18), channel_id=1, source_target_pairs={{0,6},{2,4},{4,2},{6,0},{1,7},{3,5},{5,3},{7,1},{8,14},{10,12},{12... | collective-permute-start | bytes 1769480 | tf_op jit(solution)/shard_map/ppermute | solution.py:326
  189.3 51.7 %all-to-all-start = ((bf16[16,4,8,768]{3,2,1,0:T(8,128)(2,1)}), bf16[16,4,8,768]{3,2,1,0:T(8,128)(2,1)S(1)}, u32[]{:S(2)}, u32[]{:S(2)}) async-start(bf16[16,4,8,768]{3,2,1,0:T(8,128)(2,1)} %convolution_convert_fusion.15), calls=%async_computation | async-start | bytes 1572864 | tf_op jit(solution)/shard_map/all_to_all | solution.py:778
  198.2 375.7 %reduce-scatter.2.cloned.1.call-start = ((), (), s32[]{:S(2)}) async-start(), calls=%async_computation.5 | async-start | bytes 5013504 | tf_op jit(solution)/shard_map/reduce_scatter | solution.py:834
  312.8 50.4 %collective-permute-start.19 = (bf16[2,256,768]{2,1,0:T(8,128)(2,1)}, bf16[2,256,768]{2,1,0:T(8,128)(2,1)}, u32[]{:S(2)}, u32[]{:S(2)}) collective-permute-start(bf16[2,256,768]{2,1,0:T(8,128)(2,1)} %dynamic-slice_bitcast_fusion.2), channel_id=1, source_target_pairs={{0,2},{2,0},{1,3},{3,1},{4,6},{6,4},{5,7},{7,5},{8,10},{10,8},{9,1... | collective-permute-start | bytes 2359304 | tf_op jit(solution)/shard_map/ppermute | solution.py:313
  363.2 62.6 %collective-permute-start.21 = (bf16[2,256,768]{2,1,0:T(8,128)(2,1)}, bf16[2,256,768]{2,1,0:T(8,128)(2,1)}, u32[]{:S(2)}, u32[]{:S(2)}) collective-permute-start(bf16[2,256,768]{2,1,0:T(8,128)(2,1)} %collective-permute-done.19), channel_id=1, source_target_pairs={{0,1},{1,0},{2,3},{3,2},{4,5},{5,4},{6,7},{7,6},{8,9},{9,8},{10,11... | collective-permute-start | bytes 2359304 | tf_op jit(solution)/shard_map/ppermute | solution.py:313
  372.8 61.6 %all-to-all-start.1 = ((bf16[16,4,8,768]{3,2,1,0:T(8,128)(2,1)}), bf16[16,4,8,768]{3,2,1,0:T(8,128)(2,1)}, u32[]{:S(2)}, u32[]{:S(2)}) async-start(bf16[16,4,8,768]{3,2,1,0:T(8,128)(2,1)} %bitcast.84), calls=%async_computation.1 | async-start | bytes 1572864 | tf_op jit(solution)/shard_map/all_to_all | solution.py:873
  412.7 34.6 %collective-permute-start.23 = (bf16[2,2,2,1,96,768]{5,4,3,2,1,0:T(8,128)(2,1)}, bf16[2,2,2,1,96,768]{5,4,3,2,1,0:T(8,128)(2,1)}, u32[]{:S(2)}, u32[]{:S(2)}) collective-permute-start(bf16[2,2,2,1,96,768]{5,4,3,2,1,0:T(8,128)(2,1)} %constant_dynamic-slice_fusion.12), channel_id=1, source_target_pairs={{0,4},{4,0},{1,5},{5,1},{2,6},{6,2},{3,7},{7,3},{8,12},{12,8},{9,1... | collective-permute-start | bytes 3538952 | tf_op jit(solution)/shard_map/ppermute | solution.py:313
  420.7 59.9 %collective-permute-start.26 = (bf16[1,2,2,2,96,768]{5,4,3,2,1,0:T(8,128)(2,1)}, bf16[1,2,2,2,96,768]{5,4,3,2,1,0:T(8,128)(2,1)}, u32[]{:S(2)}, u32[]{:S(2)}) collective-permute-start(bf16[1,2,2,2,96,768]{5,4,3,2,1,0:T(8,128)(2,1)} %constant_dynamic-slice_fusion.11), channel_id=1, source_target_pairs={{0,2},{2,0},{1,3},{3,1},{4,6},{6,4},{5,7},{7,5},{8,10},{10,8},{9,1... | collective-permute-start | bytes 3538952 | tf_op jit(solution)/shard_map/ppermute | solution.py:313
  483.5 16.1 %collective-permute-start.30 = (bf16[2,2,2,2,1,64,1280]{6,5,4,3,2,1,0:T(8,128)(2,1)S(1)}, bf16[2,2,2,2,1,64,1280]{6,5,4,3,2,1,0:T(8,128)(2,1)S(1)}, u32[]{:S(2)}, u32[]{:S(2)}) collective-permute-start(bf16[2,2,2,2,1,64,1280]{6,5,4,3,2,1,0:T(8,128)(2,1)S(1)} %pad_maximum_fusion.3), channel_id=1, source_target_pairs={{0,1},{1,0},{2,3},{3,2},{4,5},{5,4},{6,7},{7,6},{8,9},{9,8},{10,11... | collective-permute-start | bytes 7864328 | tf_op jit(solution)/shard_map/ppermute | solution.py:313
  488.3 18.9 %collective-permute-start.31 = (bf16[1,2,2,1,96,768]{5,4,3,2,1,0:T(8,128)(2,1)}, bf16[1,2,2,1,96,768]{5,4,3,2,1,0:T(8,128)(2,1)}, u32[]{:S(2)}, u32[]{:S(2)}) collective-permute-start(bf16[1,2,2,1,96,768]{5,4,3,2,1,0:T(8,128)(2,1)} %get-tuple-element.484), channel_id=1, source_target_pairs={{0,4},{4,0},{1,5},{5,1},{2,6},{6,2},{3,7},{7,3},{8,12},{12,8},{9,1... | collective-permute-start | bytes 1769480 | tf_op jit(solution)/shard_map/ppermute | solution.py:313
  519.2 57.2 %collective-permute-start.32 = (bf16[2,2,2,2,1,208,512]{6,5,4,3,2,1,0:T(8,128)(2,1)}, bf16[2,2,2,2,1,208,512]{6,5,4,3,2,1,0:T(8,128)(2,1)}, u32[]{:S(2)}, u32[]{:S(2)}) collective-permute-start(bf16[2,2,2,2,1,208,512]{6,5,4,3,2,1,0:T(8,128)(2,1)} %pad_maximum_fusion.2), channel_id=1, source_target_pairs={{0,1},{1,0},{2,3},{3,2},{4,5},{5,4},{6,7},{7,6},{8,9},{9,8},{10,11... | collective-permute-start | bytes 10223624 | tf_op jit(solution)/shard_map/ppermute | solution.py:313
  523.2 57.0 %collective-permute-start.33 = (bf16[2,2,1,2,1,64,1280]{6,5,4,3,2,1,0:T(8,128)(2,1)}, bf16[2,2,1,2,1,64,1280]{6,5,4,3,2,1,0:T(8,128)(2,1)}, u32[]{:S(2)}, u32[]{:S(2)}) collective-permute-start(bf16[2,2,1,2,1,64,1280]{6,5,4,3,2,1,0:T(8,128)(2,1)} %get-tuple-element.478), channel_id=1, source_target_pairs={{0,4},{4,0},{1,5},{5,1},{2,6},{6,2},{3,7},{7,3},{8,12},{12,8},{9,1... | collective-permute-start | bytes 3932168 | tf_op jit(solution)/shard_map/ppermute | solution.py:313
  536.4 24.9 %collective-permute-start.42 = (bf16[1,1,1,1,192,768]{5,4,3,2,1,0:T(8,128)(2,1)}, bf16[1,1,1,1,192,768]{5,4,3,2,1,0:T(8,128)(2,1)}, u32[]{:S(2)}, u32[]{:S(2)}) collective-permute-start(bf16[1,1,1,1,192,768]{5,4,3,2,1,0:T(8,128)(2,1)} %pad_maximum_fusion.10), channel_id=1, source_target_pairs={{0,16},{8,24},{16,0},{24,8},{1,17},{9,25},{17,1},{25,9},{2,18},{10... | collective-permute-start | bytes 884744 | tf_op jit(solution)/shard_map/ppermute | solution.py:313
  582.0 17.7 %collective-permute-start.45 = (bf16[2,2,1,1,1,64,1280]{6,5,4,3,2,1,0:T(8,128)(2,1)S(1)}, bf16[2,2,1,1,1,64,1280]{6,5,4,3,2,1,0:T(8,128)(2,1)S(1)}, u32[]{:S(2)}, u32[]{:S(2)}) collective-permute-start(bf16[2,2,1,1,1,64,1280]{6,5,4,3,2,1,0:T(8,128)(2,1)S(1)} %get-tuple-element.491), channel_id=1, source_target_pairs={{0,2},{2,0},{1,3},{3,1},{4,6},{6,4},{5,7},{7,5},{8,10},{10,8},{9,1... | collective-permute-start | bytes 1966088 | tf_op jit(solution)/shard_map/ppermute | solution.py:313
  582.3 20.7 %collective-permute-start.34 = (bf16[2,256,768]{2,1,0:T(8,128)(2,1)S(1)}, bf16[2,256,768]{2,1,0:T(8,128)(2,1)S(1)}, u32[]{:S(2)}, u32[]{:S(2)}) collective-permute-start(bf16[2,256,768]{2,1,0:T(8,128)(2,1)S(1)} %fusion.60), channel_id=1, source_target_pairs={{0,1},{1,0},{2,3},{3,2},{4,5},{5,4},{6,7},{7,6},{8,9},{9,8},{10,11... | collective-permute-start | bytes 2359304 | tf_op jit(solution)/shard_map/ppermute | solution.py:313
  589.8 27.0 %collective-permute-start.36 = (bf16[2,2,1,1,1,208,512]{6,5,4,3,2,1,0:T(8,128)(2,1)}, bf16[2,2,1,1,1,208,512]{6,5,4,3,2,1,0:T(8,128)(2,1)}, u32[]{:S(2)}, u32[]{:S(2)}) collective-permute-start(bf16[2,2,1,1,1,208,512]{6,5,4,3,2,1,0:T(8,128)(2,1)} %get-tuple-element.475), channel_id=1, source_target_pairs={{0,4},{4,0},{1,5},{5,1},{2,6},{6,2},{3,7},{7,3},{8,12},{12,8},{9,1... | collective-permute-start | bytes 2555912 | tf_op jit(solution)/shard_map/ppermute | solution.py:313
  591.0 45.2 %collective-permute-start.37 = (bf16[2,2,1,1,1,208,512]{6,5,4,3,2,1,0:T(8,128)(2,1)}, bf16[2,2,1,1,1,208,512]{6,5,4,3,2,1,0:T(8,128)(2,1)}, u32[]{:S(2)}, u32[]{:S(2)}) collective-permute-start(bf16[2,2,1,1,1,208,512]{6,5,4,3,2,1,0:T(8,128)(2,1)} %get-tuple-element.476), channel_id=1, source_target_pairs={{0,2},{2,0},{1,3},{3,1},{4,6},{6,4},{5,7},{7,5},{8,10},{10,8},{9,1... | collective-permute-start | bytes 2555912 | tf_op jit(solution)/shard_map/ppermute | solution.py:313
  613.0 23.3 %collective-permute-start.38 = (bf16[2,2,1,1,1,208,512]{6,5,4,3,2,1,0:T(8,128)(2,1)}, bf16[2,2,1,1,1,208,512]{6,5,4,3,2,1,0:T(8,128)(2,1)}, u32[]{:S(2)}, u32[]{:S(2)}) collective-permute-start(bf16[2,2,1,1,1,208,512]{6,5,4,3,2,1,0:T(8,128)(2,1)} %get-tuple-element.474), channel_id=1, source_target_pairs={{0,6},{2,4},{4,2},{6,0},{1,7},{3,5},{5,3},{7,1},{8,14},{10,12},{12... | collective-permute-start | bytes 2555912 | tf_op jit(solution)/shard_map/ppermute | solution.py:326
  613.2 53.8 %collective-permute-start.35 = (bf16[256,768]{1,0:T(8,128)(2,1)}, bf16[256,768]{1,0:T(8,128)(2,1)}, u32[]{:S(2)}, u32[]{:S(2)}) collective-permute-start(bf16[256,768]{1,0:T(8,128)(2,1)} %fusion.82), channel_id=1, source_target_pairs={{0,2},{2,0},{1,3},{3,1},{4,6},{6,4},{5,7},{7,5},{8,10},{10,8},{9,1... | collective-permute-start | bytes 1179656 | tf_op jit(solution)/shard_map/ppermute | solution.py:313
  (206 other events, 2544.3 us)
Sparse Core Ops, SparseCore 0:
  16.6 124.7 all-gather.2
  144.7 100.8 all-gather.4
  363.2 146.0 reduce-scatter.1

commit v4 on v3

--- a/solution.py
+++ b/solution.py
@@ -940,7 +940,7 @@
     )
     while sum_both.rounds:
         sum_both.step(text_own)
-    both_shard = sum_both.take(text_own).value()
+    both_shard = sum_both.take(text_own, *sum_last.flying).value()
 
     (
         reduce_weight, spatial_weight, expand_weight, visual_proj, attn_in, attn_out, ffn_up, ffn_down,

time: 733 us -> 715 us (0.975)
  starting transfers between devices: 93.8 us -> 121 us
  waiting for transfers between devices: 164 us -> 139 us
  Pallas kernels: 87.2 us -> 69.9 us
    ppermute x43, waiting for transfers between devices: 122 us -> 97.5 us  [swap(): return lax.ppermute(values, axis, [(i, i ^ reach) for i in range(count)])]
    ppermute x43, starting transfers between devices: 62.2 us -> 85.1 us  [swap(): return lax.ppermute(values, axis, [(i, i ^ reach) for i in range(count)])]
    pallas_call x2, Pallas kernels: 51.5 us -> 40.2 us  [attend_backward(): pl.pallas_call(functools.partial(backward_kernel, heads=heads, group=grou...]
    unnamed x405 -> x419, local copies, waits for them, and re-layouts: 37.6 us -> 37.5 us
  transfers between devices with their start and end apart: 59 -> 59, of which waited for: 24 -> 24; matrix products, arithmetic and copies ran while one was open for 37% -> 38% of each run, Pallas kernels for 11% -> 9%
where the time goes in v4:
time: 715 us; the launch traced here: 706 us
  waiting for transfers between devices  139 us (19%)
  local copies, waits for them, and re-layouts  134 us (19%)
  starting transfers between devices  121 us (17%)
  other arithmetic  105 us (15%)
  matrix products  105 us (15%)
  Pallas kernels  69.9 us (10%)
  between operations  31.1 us (4%)
    ppermute x43, waiting for transfers between devices, swap(): return lax.ppermute(values, axis, [(i, i ^ reach) for i in range(count)])  97.5 us
    ppermute x43, starting transfers between devices, swap(): return lax.ppermute(values, axis, [(i, i ^ reach) for i in range(count)])  85.1 us
    dot_general x31, matrix products, dot(): lax.dot_general(left, right, (((first,), (second,)), ((), ())), preferred...  76.1 us
    pallas_call x2, Pallas kernels, attend_backward(): pl.pallas_call(functools.partial(backward_kernel, heads=heads, group=grou...  40.2 us
    unnamed x419, local copies, waits for them, and re-layouts  37.5 us
    ppermute x3, waiting for transfers between devices, exchange(): return lax.ppermute(values, (one, two), pairs)  28.5 us
    pallas_call x2, Pallas kernels, attend_forward(): pl.pallas_call(functools.partial(forward_kernel, heads=heads, group=group...  20 us
    convert_element_type x9, other arithmetic, pick(): sum((cut(value).astype(WIDE) for value in addends)).astype(LOW)  18.9 us
  transfers between devices with their start and end apart: 59, of which 24 were waited for; matrix products, arithmetic and copies ran while one was open for 38% of the time, Pallas kernels for 9%

profile of v4, /device:TPU:0, one launch (start us, length us, event | category | flops | bytes accessed | tf_op | source)
XLA Modules:
  0.0 705.6 jit_solution(16973670327055558550)
XLA Ops:
  54.5 4.3 collective-permute-start.3
  65.4 14.8 %collective-permute-done.3 = bf16[1,2,2,1,96,768]{5,4,3,2,1,0:T(8,128)(2,1)} collective-permute-done((bf16[1,2,2,1,96,768]{5,4,3,2,1,0:T(8,128)(2,1)}, bf16[1,2,2,1,96,768]{5,4,3,2,1,0:T(8,128)(2,1)}, u32[]{:S(2)}, u32[]{:S(2)}) %collective-permute-start.3) | collective-permute-done | bytes 589856 | tf_op jit(solution)/shard_map/ppermute | solution.py:313
  83.1 12.6 %collective-permute-done.5 = bf16[1,2,2,1,96,768]{5,4,3,2,1,0:T(8,128)(2,1)S(1)} collective-permute-done((bf16[1,2,2,1,96,768]{5,4,3,2,1,0:T(8,128)(2,1)}, bf16[1,2,2,1,96,768]{5,4,3,2,1,0:T(8,128)(2,1)S(1)}, u32[]{:S(2)}, u32[]{:S(2)}) %collective-permute-start.5) | collective-permute-done | bytes 589856 | tf_op jit(solution)/shard_map/ppermute | solution.py:326
  106.4 7.1 %concatenate.150 = f32[28]{0:T(128)} concatenate(f32[1]{0:T(128)} %bitcast.7, f32[1]{0:T(128)} %bitcast.8, f32[1]{0:T(128)} %bitcast.9, f32[1]{0:T(128)} %bitcast.10, f32[6]{0:T(128)S(1)} %reshape.914, f32[2]{0:T(128)S(1)} %copy-done.142, f32[1]{0:T(128)} %bitcast.11, f32[1]{0:T(128)} %bitcast.12, f32[1]{0:T(128)} %bitcast.13, f32[1]{0:T(128)} %bitcast.14, f32[1]{0:T(128)} %bitcast.15, ...), dimensions={0} | concatenate | bytes 224 | tf_op jit(solution)/shard_map/concatenate | solution.py:655
  118.2 8.0 %collective-permute-done.8 = bf16[1,1,1,1,96,768]{4,5,3,2,1,0:T(8,128)(2,1)} collective-permute-done((bf16[1,1,1,1,96,768]{4,5,3,2,1,0:T(8,128)(2,1)S(1)}, bf16[1,1,1,1,96,768]{4,5,3,2,1,0:T(8,128)(2,1)}, u32[]{:S(2)}, u32[]{:S(2)}) %collective-permute-start.8) | collective-permute-done | bytes 147488 | tf_op jit(solution)/shard_map/ppermute | solution.py:313
  128.3 13.1 %all-gather.3.cloned.1.call-done = bf16[2048,2944]{1,0:T(8,128)(2,1)} async-done(((bf16[64,2944]{1,0:T(8,128)(2,1)}), bf16[2048,2944]{1,0:T(8,128)(2,1)}) %all-gather.3.cloned.1.call-update) | async-done | bytes 12058640 | tf_op jit(solution)/shard_map/all_gather | solution.py:708
  148.4 5.2 collective-permute-start.9
  189.4 8.7 %all-to-all-start = ((bf16[16,4,8,768]{3,2,1,0:T(8,128)(2,1)}), bf16[16,4,8,768]{3,2,1,0:T(8,128)(2,1)S(1)}, u32[]{:S(2)}, u32[]{:S(2)}) async-start(bf16[16,4,8,768]{3,2,1,0:T(8,128)(2,1)} %convolution_convert_fusion.15), calls=%async_computation | async-start | bytes 1572864 | tf_op jit(solution)/shard_map/all_to_all | solution.py:778
  203.3 15.8 %collective-permute-done.15 = bf16[1,2,2,1,96,768]{5,4,3,2,1,0:T(8,128)(2,1)} collective-permute-done((bf16[1,2,2,1,96,768]{5,4,3,2,1,0:T(8,128)(2,1)}, bf16[1,2,2,1,96,768]{5,4,3,2,1,0:T(8,128)(2,1)}, u32[]{:S(2)}, u32[]{:S(2)}) %collective-permute-start.15) | collective-permute-done | bytes 589856 | tf_op jit(solution)/shard_map/ppermute | solution.py:326
  226.9 10.0 %shard_map.738 = (bf16[1024,384]{1,0:T(8,128)(2,1)S(1)}, f32[8,1024]{1,0:T(8,128)S(1)}) custom-call(bf16[1024,576]{1,0:T(8,128)(2,1)S(1)} %convolution_convert_fusion.5.refs_0_, bf16[1024,576]{1,0:T(8,128)(2,1)S(1)} %convolution_convert_fusion.4.refs_1_, s32[2,4]{1,0:T(2,128)S(1)} %pad_add_fusion.refs_2_, bf16[1024,128]{1,0:T(8,128)(2,1)S(1)} %add_convert_fusion.15.refs_3_, ...), custom_call_target="tpu_custom_call" | custom-call | tf_op jit(solution)/shard_map/pallas_call | solution.py:203
  246.1 9.9 %shard_map.739 = (bf16[1024,384]{1,0:T(8,128)(2,1)S(1)}, f32[8,1024]{1,0:T(8,128)S(1)}) custom-call(bf16[1024,576]{1,0:T(8,128)(2,1)S(1)} %convolution_convert_fusion.3.refs_0_, bf16[1024,576]{1,0:T(8,128)(2,1)S(1)} %convolution_convert_fusion.2.refs_1_, s32[2,4]{1,0:T(2,128)S(1)} %pad_add_fusion.refs_2_, bf16[1024,128]{1,0:T(8,128)(2,1)S(1)} %add_convert_fusion.15.refs_3_, ...), custom_call_target="tpu_custom_call" | custom-call | tf_op jit(solution)/shard_map/pallas_call | solution.py:203
  286.6 5.5 shard_map.741
  324.7 20.3 %shard_map.743 = (bf16[1024,576]{1,0:T(8,128)(2,1)}, bf16[1024,576]{1,0:T(8,128)(2,1)}, f32[6,64,128]{2,1,0:T(8,128)}) custom-call(bf16[1024,576]{1,0:T(8,128)(2,1)} %copy-done.14, bf16[1024,576]{1,0:T(8,128)(2,1)} %copy-done.13, s32[2,4]{1,0:T(2,128)} %copy-done.32, bf16[1024,128]{1,0:T(8,128)(2,1)} %copy-done.4, bf16[6,128,256]{2,1,0:T(8,128)(2,1)} %copy-done.3, ...), custom_call_target="tpu_custom_call" | custom-call | tf_op jit(solution)/shard_map/pallas_call | solution.py:231
  351.5 4.8 copy.290
  366.1 9.9 %all-to-all-start.1 = ((bf16[16,4,8,768]{3,2,1,0:T(8,128)(2,1)}), bf16[16,4,8,768]{3,2,1,0:T(8,128)(2,1)}, u32[]{:S(2)}, u32[]{:S(2)}) async-start(bf16[16,4,8,768]{3,2,1,0:T(8,128)(2,1)} %bitcast.84), calls=%async_computation.1 | async-start | bytes 1572864 | tf_op jit(solution)/shard_map/all_to_all | solution.py:873
  383.7 19.9 %shard_map.744 = (bf16[1024,576]{1,0:T(8,128)(2,1)}, bf16[1024,576]{1,0:T(8,128)(2,1)}, f32[6,64,128]{2,1,0:T(8,128)}) custom-call(bf16[1024,576]{1,0:T(8,128)(2,1)} %copy-done.12, bf16[1024,576]{1,0:T(8,128)(2,1)} %copy-done.11, s32[2,4]{1,0:T(2,128)} %copy-done.32, bf16[1024,128]{1,0:T(8,128)(2,1)} %copy-done.4, bf16[6,128,256]{2,1,0:T(8,128)(2,1)} %copy-done.3, ...), custom_call_target="tpu_custom_call" | custom-call | tf_op jit(solution)/shard_map/pallas_call | solution.py:231
  413.3 6.5 collective-permute-start.26
  420.8 9.4 %fusion.122 = (bf16[16,4,8,2048]{3,2,1,0:T(8,128)(2,1)S(1)}, f32[16,4,8,2048]{3,2,1,0:T(8,128)}) fusion(f32[16,4,8,2048]{3,2,1,0:T(8,128)} %copy-done.175, bf16[16,4,8,768]{3,2,1,0:T(8,128)(2,1)} %all-to-all-done.1, bf16[2048,768,1,1]{1,0,3,2:T(8,128)(2,1)} %bitcast.481), kind=kOutput, calls=%fused_computation.473 | convolution fusion | flops 1631584256 | bytes 14417920 | tf_op jit(solution)/shard_map/pwhd,cd->pwhc/dot_general | solution.py:883
  432.4 5.4 bitcast_convert_fusion.1
  473.8 4.4 bitcast_convert_fusion
  486.9 4.3 constant_dynamic-slice_fusion.3
  493.4 4.4 collective-permute-start.32
  507.2 4.6 fusion.52
  523.2 6.0 collective-permute-start.44
  541.2 5.1 collective-permute-done.33
  553.0 4.6 add_convert_fusion.7
  557.6 7.1 %collective-permute-done.45 = bf16[2,2,1,1,1,64,1280]{6,5,4,3,2,1,0:T(8,128)(2,1)S(1)} collective-permute-done((bf16[2,2,1,1,1,64,1280]{6,5,4,3,2,1,0:T(8,128)(2,1)S(1)}, bf16[2,2,1,1,1,64,1280]{6,5,4,3,2,1,0:T(8,128)(2,1)S(1)}, u32[]{:S(2)}, u32[]{:S(2)}) %collective-permute-start.45) | collective-permute-done | bytes 655392 | tf_op jit(solution)/shard_map/ppermute | solution.py:313
  572.5 6.1 collective-permute-done.46
  589.6 12.0 %collective-permute-done.42 = bf16[1,1,1,1,192,768]{5,4,3,2,1,0:T(8,128)(2,1)S(1)} collective-permute-done((bf16[1,1,1,1,192,768]{5,4,3,2,1,0:T(8,128)(2,1)S(1)}, bf16[1,1,1,1,192,768]{5,4,3,2,1,0:T(8,128)(2,1)S(1)}, u32[]{:S(2)}, u32[]{:S(2)}) %collective-permute-start.42) | collective-permute-done | bytes 294944 | tf_op jit(solution)/shard_map/ppermute | solution.py:313
  601.7 15.4 %collective-permute-done.37 = bf16[2,2,1,1,1,208,512]{6,5,4,3,2,1,0:T(8,128)(2,1)} collective-permute-done((bf16[2,2,1,1,1,208,512]{6,5,4,3,2,1,0:T(8,128)(2,1)}, bf16[2,2,1,1,1,208,512]{6,5,4,3,2,1,0:T(8,128)(2,1)}, u32[]{:S(2)}, u32[]{:S(2)}) %collective-permute-start.37) | collective-permute-done | bytes 852000 | tf_op jit(solution)/shard_map/ppermute | solution.py:313
  625.1 4.3 collective-permute-start.40
  633.9 4.6 collective-permute-done.41
  (823 shorter events, 400.3 us)
Async XLA Ops:
  7.3 134.1 %all-gather.3.cloned.1.call-start = ((), (), s32[]{:S(2)}) async-start(), calls=%async_computation.3 | async-start | bytes 12435456 | tf_op jit(solution)/shard_map/all_gather | solution.py:708
  16.5 255.7 %all-gather.5.cloned.1.call-start = ((), (), s32[]{:S(2)}) async-start(), calls=%async_computation.4 | async-start | bytes 5013504 | tf_op jit(solution)/shard_map/all_gather | solution.py:709
  23.3 24.0 %collective-permute-start = (bf16[1,1,1,1,96,768]{4,5,3,2,1,0:T(8,128)(2,1)}, bf16[1,1,1,1,96,768]{4,5,3,2,1,0:T(8,128)(2,1)}, u32[]{:S(2)}, u32[]{:S(2)}) collective-permute-start(bf16[1,1,1,1,96,768]{4,5,3,2,1,0:T(8,128)(2,1)} %maximum_bitcast_fusion.1), channel_id=1, source_target_pairs={{0,16},{8,24},{16,0},{24,8},{1,17},{9,25},{17,1},{25,9},{2,18},{10... | collective-permute-start | bytes 442376 | tf_op jit(solution)/shard_map/ppermute | solution.py:313
  27.4 21.7 %collective-permute-start.1 = (bf16[1,1,1,1,96,768]{4,5,3,2,1,0:T(8,128)(2,1)}, bf16[1,1,1,1,96,768]{4,5,3,2,1,0:T(8,128)(2,1)}, u32[]{:S(2)}, u32[]{:S(2)}) collective-permute-start(bf16[1,1,1,1,96,768]{4,5,3,2,1,0:T(8,128)(2,1)} %maximum_bitcast_fusion.1), channel_id=1, source_target_pairs={{0,8},{8,0},{16,24},{24,16},{1,9},{9,1},{17,25},{25,17},{2,10},{10... | collective-permute-start | bytes 442376 | tf_op jit(solution)/shard_map/ppermute | solution.py:313
  28.9 21.9 %collective-permute-start.2 = (bf16[1,1,1,1,96,768]{4,5,3,2,1,0:T(8,128)(2,1)}, bf16[1,1,1,1,96,768]{4,5,3,2,1,0:T(8,128)(2,1)}, u32[]{:S(2)}, u32[]{:S(2)}) collective-permute-start(bf16[1,1,1,1,96,768]{4,5,3,2,1,0:T(8,128)(2,1)} %maximum_bitcast_fusion.1), channel_id=1, source_target_pairs={{0,24},{8,16},{16,8},{24,0},{1,25},{9,17},{17,9},{25,1},{2,26},{10... | collective-permute-start | bytes 442376 | tf_op jit(solution)/shard_map/ppermute | solution.py:313
  54.5 25.7 %collective-permute-start.3 = (bf16[1,2,2,1,96,768]{5,4,3,2,1,0:T(8,128)(2,1)}, bf16[1,2,2,1,96,768]{5,4,3,2,1,0:T(8,128)(2,1)}, u32[]{:S(2)}, u32[]{:S(2)}) collective-permute-start(bf16[1,2,2,1,96,768]{5,4,3,2,1,0:T(8,128)(2,1)} %constant_dynamic-slice_fusion.19), channel_id=1, source_target_pairs={{0,4},{4,0},{1,5},{5,1},{2,6},{6,2},{3,7},{7,3},{8,12},{12,8},{9,1... | collective-permute-start | bytes 1769480 | tf_op jit(solution)/shard_map/ppermute | solution.py:313
  60.8 21.4 %collective-permute-start.4 = (bf16[1,2,2,1,96,768]{5,4,3,2,1,0:T(8,128)(2,1)}, bf16[1,2,2,1,96,768]{5,4,3,2,1,0:T(8,128)(2,1)S(1)}, u32[]{:S(2)}, u32[]{:S(2)}) collective-permute-start(bf16[1,2,2,1,96,768]{5,4,3,2,1,0:T(8,128)(2,1)} %constant_dynamic-slice_fusion.19), channel_id=1, source_target_pairs={{0,2},{2,0},{1,3},{3,1},{4,6},{6,4},{5,7},{7,5},{8,10},{10,8},{9,1... | collective-permute-start | bytes 1769480 | tf_op jit(solution)/shard_map/ppermute | solution.py:313
  63.7 32.0 %collective-permute-start.5 = (bf16[1,2,2,1,96,768]{5,4,3,2,1,0:T(8,128)(2,1)}, bf16[1,2,2,1,96,768]{5,4,3,2,1,0:T(8,128)(2,1)S(1)}, u32[]{:S(2)}, u32[]{:S(2)}) collective-permute-start(bf16[1,2,2,1,96,768]{5,4,3,2,1,0:T(8,128)(2,1)} %constant_dynamic-slice_fusion.19), channel_id=1, source_target_pairs={{0,6},{2,4},{4,2},{6,0},{1,7},{3,5},{5,3},{7,1},{8,14},{10,12},{12... | collective-permute-start | bytes 1769480 | tf_op jit(solution)/shard_map/ppermute | solution.py:326
  96.6 21.2 %collective-permute-start.6 = (bf16[1,1,1,1,96,768]{4,5,3,2,1,0:T(8,128)(2,1)S(1)}, bf16[1,1,1,1,96,768]{4,5,3,2,1,0:T(8,128)(2,1)S(1)}, u32[]{:S(2)}, u32[]{:S(2)}) collective-permute-start(bf16[1,1,1,1,96,768]{4,5,3,2,1,0:T(8,128)(2,1)S(1)} %maximum_bitcast_fusion.2), channel_id=1, source_target_pairs={{0,16},{8,24},{16,0},{24,8},{1,17},{9,25},{17,1},{25,9},{2,18},{10... | collective-permute-start | bytes 442376 | tf_op jit(solution)/shard_map/ppermute | solution.py:313
  98.2 19.8 %collective-permute-start.7 = (bf16[1,1,1,1,96,768]{4,5,3,2,1,0:T(8,128)(2,1)S(1)}, bf16[1,1,1,1,96,768]{4,5,3,2,1,0:T(8,128)(2,1)S(1)}, u32[]{:S(2)}, u32[]{:S(2)}) collective-permute-start(bf16[1,1,1,1,96,768]{4,5,3,2,1,0:T(8,128)(2,1)S(1)} %maximum_bitcast_fusion.2), channel_id=1, source_target_pairs={{0,8},{8,0},{16,24},{24,16},{1,9},{9,1},{17,25},{25,17},{2,10},{10... | collective-permute-start | bytes 442376 | tf_op jit(solution)/shard_map/ppermute | solution.py:313
  169.9 29.3 %collective-permute-start.13 = (bf16[1,2,2,1,96,768]{5,4,3,2,1,0:T(8,128)(2,1)}, bf16[1,2,2,1,96,768]{5,4,3,2,1,0:T(8,128)(2,1)}, u32[]{:S(2)}, u32[]{:S(2)}) collective-permute-start(bf16[1,2,2,1,96,768]{5,4,3,2,1,0:T(8,128)(2,1)} %constant_dynamic-slice_fusion.18), channel_id=1, source_target_pairs={{0,4},{4,0},{1,5},{5,1},{2,6},{6,2},{3,7},{7,3},{8,12},{12,8},{9,1... | collective-permute-start | bytes 1769480 | tf_op jit(solution)/shard_map/ppermute | solution.py:313
  171.7 29.7 %collective-permute-start.14 = (bf16[1,2,2,1,96,768]{5,4,3,2,1,0:T(8,128)(2,1)}, bf16[1,2,2,1,96,768]{5,4,3,2,1,0:T(8,128)(2,1)}, u32[]{:S(2)}, u32[]{:S(2)}) collective-permute-start(bf16[1,2,2,1,96,768]{5,4,3,2,1,0:T(8,128)(2,1)} %constant_dynamic-slice_fusion.18), channel_id=1, source_target_pairs={{0,2},{2,0},{1,3},{3,1},{4,6},{6,4},{5,7},{7,5},{8,10},{10,8},{9,1... | collective-permute-start | bytes 1769480 | tf_op jit(solution)/shard_map/ppermute | solution.py:313
  175.8 43.3 %collective-permute-start.15 = (bf16[1,2,2,1,96,768]{5,4,3,2,1,0:T(8,128)(2,1)}, bf16[1,2,2,1,96,768]{5,4,3,2,1,0:T(8,128)(2,1)}, u32[]{:S(2)}, u32[]{:S(2)}) collective-permute-start(bf16[1,2,2,1,96,768]{5,4,3,2,1,0:T(8,128)(2,1)} %constant_dynamic-slice_fusion.18), channel_id=1, source_target_pairs={{0,6},{2,4},{4,2},{6,0},{1,7},{3,5},{5,3},{7,1},{8,14},{10,12},{12... | collective-permute-start | bytes 1769480 | tf_op jit(solution)/shard_map/ppermute | solution.py:326
  189.4 48.6 %all-to-all-start = ((bf16[16,4,8,768]{3,2,1,0:T(8,128)(2,1)}), bf16[16,4,8,768]{3,2,1,0:T(8,128)(2,1)S(1)}, u32[]{:S(2)}, u32[]{:S(2)}) async-start(bf16[16,4,8,768]{3,2,1,0:T(8,128)(2,1)} %convolution_convert_fusion.15), calls=%async_computation | async-start | bytes 1572864 | tf_op jit(solution)/shard_map/all_to_all | solution.py:778
  198.2 337.9 %reduce-scatter.2.cloned.1.call-start = ((), (), s32[]{:S(2)}) async-start(), calls=%async_computation.5 | async-start | bytes 5013504 | tf_op jit(solution)/shard_map/reduce_scatter | solution.py:834
  307.2 49.1 %collective-permute-start.19 = (bf16[2,256,768]{2,1,0:T(8,128)(2,1)}, bf16[2,256,768]{2,1,0:T(8,128)(2,1)}, u32[]{:S(2)}, u32[]{:S(2)}) collective-permute-start(bf16[2,256,768]{2,1,0:T(8,128)(2,1)} %dynamic-slice_bitcast_fusion.2), channel_id=1, source_target_pairs={{0,2},{2,0},{1,3},{3,1},{4,6},{6,4},{5,7},{7,5},{8,10},{10,8},{9,1... | collective-permute-start | bytes 2359304 | tf_op jit(solution)/shard_map/ppermute | solution.py:313
  356.4 145.2 %collective-permute-start.21 = (bf16[2,256,768]{2,1,0:T(8,128)(2,1)}, bf16[2,256,768]{2,1,0:T(8,128)(2,1)}, u32[]{:S(2)}, u32[]{:S(2)}) collective-permute-start(bf16[2,256,768]{2,1,0:T(8,128)(2,1)} %collective-permute-done.19), channel_id=1, source_target_pairs={{0,1},{1,0},{2,3},{3,2},{4,5},{5,4},{6,7},{7,6},{8,9},{9,8},{10,11... | collective-permute-start | bytes 2359304 | tf_op jit(solution)/shard_map/ppermute | solution.py:313
  366.1 54.8 %all-to-all-start.1 = ((bf16[16,4,8,768]{3,2,1,0:T(8,128)(2,1)}), bf16[16,4,8,768]{3,2,1,0:T(8,128)(2,1)}, u32[]{:S(2)}, u32[]{:S(2)}) async-start(bf16[16,4,8,768]{3,2,1,0:T(8,128)(2,1)} %bitcast.84), calls=%async_computation.1 | async-start | bytes 1572864 | tf_op jit(solution)/shard_map/all_to_all | solution.py:873
  381.7 39.1 %collective-permute-start.23 = (bf16[2,2,2,1,96,768]{5,4,3,2,1,0:T(8,128)(2,1)}, bf16[2,2,2,1,96,768]{5,4,3,2,1,0:T(8,128)(2,1)}, u32[]{:S(2)}, u32[]{:S(2)}) collective-permute-start(bf16[2,2,2,1,96,768]{5,4,3,2,1,0:T(8,128)(2,1)} %constant_dynamic-slice_fusion.12), channel_id=1, source_target_pairs={{0,4},{4,0},{1,5},{5,1},{2,6},{6,2},{3,7},{7,3},{8,12},{12,8},{9,1... | collective-permute-start | bytes 3538952 | tf_op jit(solution)/shard_map/ppermute | solution.py:313
  413.3 42.1 %collective-permute-start.26 = (bf16[1,2,2,2,96,768]{5,4,3,2,1,0:T(8,128)(2,1)}, bf16[1,2,2,2,96,768]{5,4,3,2,1,0:T(8,128)(2,1)}, u32[]{:S(2)}, u32[]{:S(2)}) collective-permute-start(bf16[1,2,2,2,96,768]{5,4,3,2,1,0:T(8,128)(2,1)} %constant_dynamic-slice_fusion.11), channel_id=1, source_target_pairs={{0,2},{2,0},{1,3},{3,1},{4,6},{6,4},{5,7},{7,5},{8,10},{10,8},{9,1... | collective-permute-start | bytes 3538952 | tf_op jit(solution)/shard_map/ppermute | solution.py:313
  463.2 17.1 %collective-permute-start.31 = (bf16[1,2,2,1,96,768]{5,4,3,2,1,0:T(8,128)(2,1)}, bf16[1,2,2,1,96,768]{5,4,3,2,1,0:T(8,128)(2,1)}, u32[]{:S(2)}, u32[]{:S(2)}) collective-permute-start(bf16[1,2,2,1,96,768]{5,4,3,2,1,0:T(8,128)(2,1)} %get-tuple-element.484), channel_id=1, source_target_pairs={{0,4},{4,0},{1,5},{5,1},{2,6},{6,2},{3,7},{7,3},{8,12},{12,8},{9,1... | collective-permute-start | bytes 1769480 | tf_op jit(solution)/shard_map/ppermute | solution.py:313
  493.4 43.7 %collective-permute-start.32 = (bf16[2,2,2,2,1,208,512]{6,5,4,3,2,1,0:T(8,128)(2,1)}, bf16[2,2,2,2,1,208,512]{6,5,4,3,2,1,0:T(8,128)(2,1)}, u32[]{:S(2)}, u32[]{:S(2)}) collective-permute-start(bf16[2,2,2,2,1,208,512]{6,5,4,3,2,1,0:T(8,128)(2,1)} %pad_maximum_fusion.2), channel_id=1, source_target_pairs={{0,1},{1,0},{2,3},{3,2},{4,5},{5,4},{6,7},{7,6},{8,9},{9,8},{10,11... | collective-permute-start | bytes 10223624 | tf_op jit(solution)/shard_map/ppermute | solution.py:313
  515.0 31.3 %collective-permute-start.33 = (bf16[2,2,1,2,1,64,1280]{6,5,4,3,2,1,0:T(8,128)(2,1)}, bf16[2,2,1,2,1,64,1280]{6,5,4,3,2,1,0:T(8,128)(2,1)}, u32[]{:S(2)}, u32[]{:S(2)}) collective-permute-start(bf16[2,2,1,2,1,64,1280]{6,5,4,3,2,1,0:T(8,128)(2,1)} %get-tuple-element.478), channel_id=1, source_target_pairs={{0,4},{4,0},{1,5},{5,1},{2,6},{6,2},{3,7},{7,3},{8,12},{12,8},{9,1... | collective-permute-start | bytes 3932168 | tf_op jit(solution)/shard_map/ppermute | solution.py:313
  523.2 62.0 %collective-permute-start.44 = (bf16[1,1,1,1,192,768]{5,4,3,2,1,0:T(8,128)(2,1)}, bf16[1,1,1,1,192,768]{5,4,3,2,1,0:T(8,128)(2,1)}, u32[]{:S(2)}, u32[]{:S(2)}) collective-permute-start(bf16[1,1,1,1,192,768]{5,4,3,2,1,0:T(8,128)(2,1)} %pad_maximum_fusion.12), channel_id=1, source_target_pairs={{0,24},{8,16},{16,8},{24,0},{1,25},{9,17},{17,9},{25,1},{2,26},{10... | collective-permute-start | bytes 884744 | tf_op jit(solution)/shard_map/ppermute | solution.py:313
  530.0 59.6 %collective-permute-start.43 = (bf16[1,1,1,1,192,768]{5,4,3,2,1,0:T(8,128)(2,1)}, bf16[1,1,1,1,192,768]{5,4,3,2,1,0:T(8,128)(2,1)}, u32[]{:S(2)}, u32[]{:S(2)}) collective-permute-start(bf16[1,1,1,1,192,768]{5,4,3,2,1,0:T(8,128)(2,1)} %pad_maximum_fusion.11), channel_id=1, source_target_pairs={{0,8},{8,0},{16,24},{24,16},{1,9},{9,1},{17,25},{25,17},{2,10},{10... | collective-permute-start | bytes 884744 | tf_op jit(solution)/shard_map/ppermute | solution.py:313
  548.0 16.7 %collective-permute-start.45 = (bf16[2,2,1,1,1,64,1280]{6,5,4,3,2,1,0:T(8,128)(2,1)S(1)}, bf16[2,2,1,1,1,64,1280]{6,5,4,3,2,1,0:T(8,128)(2,1)S(1)}, u32[]{:S(2)}, u32[]{:S(2)}) collective-permute-start(bf16[2,2,1,1,1,64,1280]{6,5,4,3,2,1,0:T(8,128)(2,1)S(1)} %get-tuple-element.491), channel_id=1, source_target_pairs={{0,2},{2,0},{1,3},{3,1},{4,6},{6,4},{5,7},{7,5},{8,10},{10,8},{9,1... | collective-permute-start | bytes 1966088 | tf_op jit(solution)/shard_map/ppermute | solution.py:313
  550.2 21.1 %collective-permute-start.34 = (bf16[2,256,768]{2,1,0:T(8,128)(2,1)S(1)}, bf16[2,256,768]{2,1,0:T(8,128)(2,1)S(1)}, u32[]{:S(2)}, u32[]{:S(2)}) collective-permute-start(bf16[2,256,768]{2,1,0:T(8,128)(2,1)S(1)} %fusion.60), channel_id=1, source_target_pairs={{0,1},{1,0},{2,3},{3,2},{4,5},{5,4},{6,7},{7,6},{8,9},{9,8},{10,11... | collective-permute-start | bytes 2359304 | tf_op jit(solution)/shard_map/ppermute | solution.py:313
  578.6 23.1 %collective-permute-start.36 = (bf16[2,2,1,1,1,208,512]{6,5,4,3,2,1,0:T(8,128)(2,1)}, bf16[2,2,1,1,1,208,512]{6,5,4,3,2,1,0:T(8,128)(2,1)S(1)}, u32[]{:S(2)}, u32[]{:S(2)}) collective-permute-start(bf16[2,2,1,1,1,208,512]{6,5,4,3,2,1,0:T(8,128)(2,1)} %get-tuple-element.475), channel_id=1, source_target_pairs={{0,4},{4,0},{1,5},{5,1},{2,6},{6,2},{3,7},{7,3},{8,12},{12,8},{9,1... | collective-permute-start | bytes 2555912 | tf_op jit(solution)/shard_map/ppermute | solution.py:313
  581.4 35.7 %collective-permute-start.37 = (bf16[2,2,1,1,1,208,512]{6,5,4,3,2,1,0:T(8,128)(2,1)}, bf16[2,2,1,1,1,208,512]{6,5,4,3,2,1,0:T(8,128)(2,1)}, u32[]{:S(2)}, u32[]{:S(2)}) collective-permute-start(bf16[2,2,1,1,1,208,512]{6,5,4,3,2,1,0:T(8,128)(2,1)} %get-tuple-element.476), channel_id=1, source_target_pairs={{0,2},{2,0},{1,3},{3,1},{4,6},{6,4},{5,7},{7,5},{8,10},{10,8},{9,1... | collective-permute-start | bytes 2555912 | tf_op jit(solution)/shard_map/ppermute | solution.py:313
  583.3 33.8 %collective-permute-start.38 = (bf16[2,2,1,1,1,208,512]{6,5,4,3,2,1,0:T(8,128)(2,1)}, bf16[2,2,1,1,1,208,512]{6,5,4,3,2,1,0:T(8,128)(2,1)}, u32[]{:S(2)}, u32[]{:S(2)}) collective-permute-start(bf16[2,2,1,1,1,208,512]{6,5,4,3,2,1,0:T(8,128)(2,1)} %get-tuple-element.474), channel_id=1, source_target_pairs={{0,6},{2,4},{4,2},{6,0},{1,7},{3,5},{5,3},{7,1},{8,14},{10,12},{12... | collective-permute-start | bytes 2555912 | tf_op jit(solution)/shard_map/ppermute | solution.py:326
  585.2 16.5 %collective-permute-start.42 = (bf16[1,1,1,1,192,768]{5,4,3,2,1,0:T(8,128)(2,1)S(1)}, bf16[1,1,1,1,192,768]{5,4,3,2,1,0:T(8,128)(2,1)S(1)}, u32[]{:S(2)}, u32[]{:S(2)}) collective-permute-start(bf16[1,1,1,1,192,768]{5,4,3,2,1,0:T(8,128)(2,1)S(1)} %copy-done.99), channel_id=1, source_target_pairs={{0,16},{8,24},{16,0},{24,8},{1,17},{9,25},{17,1},{25,9},{2,18},{10... | collective-permute-start | bytes 884744 | tf_op jit(solution)/shard_map/ppermute | solution.py:313
  589.6 59.1 %collective-permute-start.35 = (bf16[256,768]{1,0:T(8,128)(2,1)}, bf16[256,768]{1,0:T(8,128)(2,1)}, u32[]{:S(2)}, u32[]{:S(2)}) collective-permute-start(bf16[256,768]{1,0:T(8,128)(2,1)} %fusion.82), channel_id=1, source_target_pairs={{0,2},{2,0},{1,3},{3,1},{4,6},{6,4},{5,7},{7,5},{8,10},{10,8},{9,1... | collective-permute-start | bytes 1179656 | tf_op jit(solution)/shard_map/ppermute | solution.py:313
  (213 other events, 2520.6 us)
Sparse Core Ops, SparseCore 0:
  16.6 124.7 all-gather.2
  144.7 100.8 all-gather.4
  356.4 152.7 reduce-scatter.1
